TPU v7x, 32 devices: a whole 2x2x4 slice. The times are simulated.
32 devices in a mesh: ctx: 8 (over z, y), head: 4 (over x, core).
Axes of the slice: x: 2, y: 2, z: 4, core: 2. Of those that a mesh axis runs over, the one named last changes fastest.
Arguments:
- query: bfloat16 [1024, 2048], P('ctx', 'head'), may hold values from -6 to 6
- keys: bfloat16 [1024, 2048], P('ctx', 'head'), may hold values from -10 to 10
- values: bfloat16 [1024, 2048], P('ctx', 'head'), may hold values from -12 to 12
- log_decay: float32 [1024, 16], P('ctx', 'head'), may hold values from -1 to 0
- norm_gain: float32 [2048], P('head'), may hold values from 0.1 to 1.9
- out_weight: bfloat16 [2048, 6144], P('head'), may hold values from -0.1875 to 0.1875
Outputs:
- mixed: bfloat16 [1024, 6144], P('ctx', 'head')
All inputs are finite; a program needn't handle non-finite values.
Results may differ from a plain program's by a relative error of at most 0.014.
Values may be sent and summed in bfloat16 or wider, within the bound.
No kernel may reach another device: no remote copies, remote signals or barrier semaphores. Data moves between devices by JAX's collectives and lax.ppermute only.
A program may use at most 128 MiB of HBM per device.

v0:
```python
import jax
import jax.numpy as jnp
from jax import lax
from jax.sharding import PartitionSpec as P


def entering(value, axis, join, neutral):
    count, mine = (lax.axis_size(axis), lax.axis_index(axis))
    pieces = jax.tree.map(lambda part: lax.all_gather(part, axis), value)
    so_far = jax.tree.map(
        lambda part, zero: jnp.full_like(part, 0) + jnp.asarray(zero, part.dtype), value, neutral
    )

    def hop(position, so_far):
        longer = join(so_far, jax.tree.map(lambda part: part[position], pieces))
        return jax.tree.map(lambda new, old: jnp.where(position < mine, new, old), longer, so_far)

    return lax.fori_loop(0, count - 1, hop, so_far)


def combine_states(earlier, later):
    return (earlier[0] * later[0], later[0][:, None, None] * earlier[1] + later[1])


def local(query, keys, values, log_decay, norm_gain, out_weight):
    tok_rows, full_width = query.shape
    head_count = log_decay.shape[1]
    head_dim = full_width // head_count

    def by_head(array):
        return array.reshape(tok_rows, head_count, head_dim).transpose(1, 0, 2)

    queries = by_head(query)
    key_rows = by_head(keys)
    value_rows = by_head(values)
    cumulative = jnp.cumsum(log_decay.T, axis=1)
    tail_decay = jnp.exp(cumulative[:, -1:] - cumulative)
    kv_local = jnp.einsum(
        "hte,htf->hef",
        key_rows.astype(jnp.float32) * tail_decay[:, :, None],
        value_rows.astype(jnp.float32),
        precision=lax.Precision.HIGHEST,
    )
    decay_total = jnp.exp(cumulative[:, -1])
    carried = entering(
        (decay_total, kv_local),
        "ctx",
        combine_states,
        (jnp.ones_like(decay_total), jnp.zeros_like(kv_local)),
    )
    state_in = carried[1]
    row_index = lax.broadcasted_iota(jnp.int32, (tok_rows, tok_rows), 0)
    col_index = lax.broadcasted_iota(jnp.int32, (tok_rows, tok_rows), 1)
    causal = (row_index >= col_index)[None]
    scores = jnp.einsum("hte,hse->hts", queries, key_rows, preferred_element_type=jnp.float32)
    differ = jnp.where(causal, cumulative[:, :, None] - cumulative[:, None, :], -1e30)
    block_weights = (jnp.exp(differ) * scores).astype(jnp.bfloat16)
    within = jnp.einsum(
        "hts,hse->hte", block_weights, value_rows, preferred_element_type=jnp.float32
    )
    carried_part = jnp.exp(cumulative)[:, :, None] * jnp.einsum(
        "hte,hef->htf", queries.astype(jnp.float32), state_in, precision=lax.Precision.HIGHEST
    )
    attn = (within + carried_part).transpose(1, 0, 2).reshape(tok_rows, full_width)
    squares = lax.psum(jnp.sum(attn * attn, axis=1), "head")
    row_scale = lax.rsqrt(squares / (full_width * lax.axis_size("head")) + 1e-05)
    normed = (attn * row_scale[:, None] * norm_gain[None, :]).astype(jnp.bfloat16)
    partial_out = jnp.dot(normed, out_weight, preferred_element_type=jnp.float32)
    mixed = lax.psum_scatter(
        partial_out.astype(jnp.bfloat16), "head", scatter_dimension=1, tiled=True
    )
    return mixed


def solution(mesh):
    placed = (
        P("ctx", "head"),
        P("ctx", "head"),
        P("ctx", "head"),
        P("ctx", "head"),
        P("head"),
        P("head", None),
    )
    return jax.shard_map(
        local, mesh=mesh, in_specs=placed, out_specs=P("ctx", "head"), check_vma=False
    )
```

profile of v0, /device:TPU:0, one launch (start us, length us, event | category | flops | bytes accessed | tf_op | source)
XLA Modules:
  0.0 116.0 jit_solution(6012932278899716085)
XLA Ops:
  6.5 0.0 copy-start
  6.5 0.0 all-gather.4.cloned.1.call-start
  6.5 1.0 reduce_window_sum.11
  7.6 0.2 slice_reduce_fusion
  7.7 0.1 exponential_bitcast_fusion
  7.8 1.0 copy.26
  8.9 1.9 %fusion.6 = f32[4,128,128]{2,1,0:T(8,128)} fusion(bf16[4,128,128]{1,2,0:T(8,128)(2,1)S(1)} %bitcast.76, f32[4,128]{1,0:T(4,128)S(1)} %get-tuple-element.131, bf16[128,512]{1,0:T(8,128)(2,1)} %param.10), kind=kOutput, calls=%fused_computation.14 | convolution fusion | flops 100794368 | bytes 526336 | tf_op jit(solution)/shard_map/hte,htf->hef/dot_general | solution.py:38
  10.7 0.0 copy-start.1
  10.7 0.0 all-gather.4.cloned.1.call-update
  10.8 0.0 reduce-scatter.2.cloned.1.call-start
  10.8 1.3 %dynamic-slice = u32[1]{0:T(128)} dynamic-slice(u32[32]{0:T(128)} %constant.45, u32[]{:T(128)S(6)} %add.46), dynamic_slice_sizes={1} | dynamic-slice | bytes 12
  12.7 0.2 dynamic-update-slice
  13.0 23.2 %all-reduce = f32[32]{0:T(128)S(1)} all-reduce(f32[32]{0:T(128)S(1)} %dynamic-update-slice), channel_id=2, replica_groups=mesh['ctx'=8,'head'=4] {'ctx'}, use_global_device_ids=true, to_apply=%add | all-reduce | flops 32 | bytes 256
  36.1 0.1 reshape.62
  36.2 0.0 copy-done
  36.2 1.3 %convolution_bitcast_fusion.1 = f32[128,4,128]{0,2,1:T(8,128)S(1)} fusion(bf16[4,128,128]{1,2,0:T(8,128)(2,1)S(1)} %bitcast.77, f32[4,128]{1,0:T(4,128)S(1)} %reduce_window_sum.11, pred[128,128]{1,0:T(8,128)(4,1)S(1)} %iota_compare_fusion, bf16[128,512]{1,0:T(8,128)(2,1)} %param.10, bf16[128,512]{1,0:T(8,128)(2,1)S(1)} %copy-done), kind=kOutput, calls=%fused_computation.8 | convolution fusion | flops 33816576 | bytes 673792 | tf_op jit(solution)/shard_map/hts,hse->hte/dot_general | solution.py:58
  37.5 25.7 %all-gather.4.cloned.1.call-done = f32[32,128,128]{2,1,0:T(8,128)} async-done(((f32[4,128,128]{2,1,0:T(8,128)}), f32[32,128,128]{2,1,0:T(8,128)}) %all-gather.4.cloned.1.call-update) | async-done | bytes 2097168 | tf_op jit(solution)/shard_map/all_gather | solution.py:9
  63.2 7.6 %while.14 = (s32[]{:T(128)}, f32[4,128,128]{2,1,0:T(8,128)S(1)}, s32[]{:T(128)}, f32[8,4]{1,0:T(8,128)S(1)}, f32[8,4,128,128]{3,2,1,0:T(8,128)}, /*index=5*/s32[]{:T(128)}, s32[]{:T(128)}) while((s32[]{:T(128)}, f32[4,128,128]{2,1,0:T(8,128)S(1)}, s32[]{:T(128)}, f32[8,4]{1,0:T(8,128)S(1)}, f32[8,4,128,128]{3,2,1,0:T(8,128)}, ...), condition=%wide.region_2.3_spmd.clone, body=%wide.region_1.2_spmd.clone.sunk | while | flops 262148 | bytes 786585 | solution.py:18
  63.2 1.0 fusion.32
  64.3 1.1 fusion.32
  65.4 1.1 fusion.32
  66.5 1.1 fusion.32
  67.6 1.1 fusion.32
  68.7 1.1 fusion.32
  69.7 1.1 fusion.32
  70.8 0.4 multiply_reduce_fusion
  71.2 5.7 %psum.7 = f32[128]{0:T(128)S(1)} all-reduce(f32[128]{0:T(128)S(1)} %get-tuple-element.132), channel_id=1, replica_groups=mesh['ctx'=8,'head'=4] {'head'}, use_global_device_ids=true, to_apply=%region_4.5 | all-reduce | flops 128 | bytes 1024 | tf_op jit(solution)/shard_map/psum | solution.py:65
  76.9 0.0 copy-done.1
  76.9 0.1 fusion.5
  77.1 5.0 %convolution_convert_fusion = bf16[128,6144]{1,0:T(8,128)(2,1)} fusion(bf16[128,512]{0,1:T(8,128)(2,1)S(1)} %fusion.5, bf16[512,6144]{1,0:T(8,128)(2,1)} %param.13), kind=kOutput, calls=%fused_computation.3 | convolution fusion | flops 806092800 | bytes 7995392 | tf_op jit(solution)/shard_map/dot_general | solution.py:68
  82.0 0.0 reduce-scatter.2.cloned.1.call-update
  82.0 27.1 %reduce-scatter.2.cloned.1.call-done = bf16[128,1536]{1,0:T(8,128)(2,1)} async-done(((bf16[128,6144]{1,0:T(8,128)(2,1)}), bf16[128,1536]{1,0:T(8,128)(2,1)}) %reduce-scatter.2.cloned.1.call-update) | async-done | bytes 393232 | tf_op jit(solution)/shard_map/reduce_scatter | solution.py:69
  (11 shorter events, 0.1 us)
Async XLA Ops:
  6.5 29.7 %copy-start = (bf16[128,512]{1,0:T(8,128)(2,1)S(1)}, bf16[128,512]{1,0:T(8,128)(2,1)}, u32[]{:S(2)}) copy-start(bf16[128,512]{1,0:T(8,128)(2,1)} %param.8) | copy-start | bytes 393220
  6.5 56.7 %all-gather.4.cloned.1.call-start = ((), (), s32[]{:S(2)}) async-start(), calls=%async_computation.2 | async-start | bytes 2359296 | tf_op jit(solution)/shard_map/all_gather | solution.py:9
  10.7 66.2 %copy-start.1 = (f32[512]{0:T(512)S(1)}, f32[512]{0:T(512)}, u32[]{:S(2)}) copy-start(f32[512]{0:T(512)} %param.12) | copy-start | bytes 6148
  10.8 98.4 %reduce-scatter.2.cloned.1.call-start = ((), (), s32[]{:S(2)}) async-start(), calls=%async_computation.1 | async-start | bytes 1966080 | tf_op jit(solution)/shard_map/reduce_scatter | solution.py:69
Sparse Core Ops, SparseCore 0:
  10.9 52.2 all-gather.3
  82.2 26.9 reduce-scatter.1
where the time goes:
time: 116 us
  waiting for transfers between devices  52.8 us (46%)
  blocking collectives  28.8 us (25%)
  between operations  14.1 us (12%)
  other arithmetic  8.61 us (7%)
  matrix products  8.53 us (7%)
  local copies, waits for them, and re-layouts  2.85 us (2%)
    reduce_scatter x1, waiting for transfers between devices, local(): lax.psum_scatter(partial_out.astype(jnp.bfloat16), 'head', scatter_dimens...  27.1 us
    all_gather x1, waiting for transfers between devices, entering(): pieces = jax.tree.map(lambda part: lax.all_gather(part, axis), value)  25.7 us
    unnamed x1, blocking collectives  23.2 us
    select_n x7, other arithmetic, hop(): jnp.where(position < mine, new, old)  7.36 us
    psum x1, blocking collectives, local(): squares = lax.psum(jnp.sum(attn * attn, axis=1), 'head')  5.66 us
    dot_general x1, matrix products, local(): jnp.dot(normed, out_weight, preferred_element_type=jnp.float32)  4.97 us
  transfers between devices with their start and end apart: 2, of which 2 were waited for; matrix products, arithmetic and copies ran while one was open for 2% of the time, Pallas kernels for 0%

commit v1 on v0

v1 whole, which is shorter than its diff:
```python
import functools

import jax
import jax.numpy as jnp
from jax import lax
from jax.experimental import pallas as pl
from jax.experimental.pallas import tpu as pltpu
from jax.sharding import PartitionSpec as P

F32, BF16 = jnp.float32, jnp.bfloat16
HIGHEST = lax.Precision.HIGHEST
VMEM = pl.BlockSpec(memory_space=pltpu.VMEM)
FAR = pl.BlockSpec(memory_space=pltpu.HBM)
LANES = 128
SUBLANES = 16


def call(body, outs, operands, far=0, out_places=None, scratch=(), cost=1.0):
    held = [pltpu.with_memory_space_constraint(o, pltpu.HBM) for o in operands[:far]]
    return pl.pallas_call(
        body,
        out_shape=outs,
        in_specs=[FAR] * far + [VMEM] * (len(operands) - far),
        out_specs=out_places or [VMEM] * len(outs),
        scratch_shapes=scratch,
        cost_estimate=pl.CostEstimate(flops=int(cost * 1e9), bytes_accessed=int(cost * 1e6), transcendentals=0),
        compiler_params=pltpu.CompilerParams(vmem_limit_bytes=32 << 20),
    )(*held, *operands[far:])


def shape(dims, dtype):
    return jax.ShapeDtypeStruct(dims, dtype)


def padded(rows):
    return -(-rows // SUBLANES) * SUBLANES


def split3(value):
    high = value.astype(BF16)
    rest = value - high.astype(F32)
    mid = rest.astype(BF16)
    return high, mid, (rest - mid.astype(F32)).astype(BF16)


def stacked(value, heads):
    parts = list(split3(value))
    fill = padded(3 * heads) - 3 * heads
    if fill:
        parts.append(jnp.zeros((fill, LANES), BF16))
    return jnp.concatenate([part.astype(F32) for part in parts], axis=0).astype(BF16)


def unstacked(rows, heads):
    rows = rows.astype(F32)
    return rows[:heads] + rows[heads : 2 * heads] + rows[2 * heads : 3 * heads]


def triangle(tokens):
    row = lax.broadcasted_iota(jnp.int32, (tokens, tokens), 0)
    col = lax.broadcasted_iota(jnp.int32, (tokens, tokens), 1)
    return row, col


def column_sums(decay):
    row, col = triangle(decay.shape[1])
    lower = jnp.where(row >= col, 1.0, 0.0).astype(F32)
    return lax.dot_general(lower, decay, (((1,), (1,)), ((), ())), precision=HIGHEST)


def row_sums(decay):
    row, col = triangle(decay.shape[1])
    upper = jnp.where(row <= col, 1.0, 0.0).astype(F32)
    return jnp.dot(decay, upper, precision=HIGHEST)


def odd(axis, step=0):
    return (lax.axis_index(axis) >> step) % 2 == 1


def fetch(sources, targets, semaphores):
    copies = [
        pltpu.make_async_copy(source, target, semaphores.at[index])
        for index, (source, target) in enumerate(zip(sources, targets))
    ]
    for copy in copies:
        copy.start()
    return copies


def states_kernel(keys_far, values_far, decay_far, message, keys, values, decay, semaphores):
    for copy in fetch((keys_far, values_far, decay_far), (keys, values, decay), semaphores):
        copy.wait()
    heads, tokens = decay.shape
    width = keys.shape[1] // heads
    column = column_sums(decay[...])
    tail = jnp.exp(column[tokens - 1 : tokens, :] - column)
    for head in range(heads):
        own = slice(head * width, (head + 1) * width)
        faded = (keys[:, own].astype(F32) * tail[:, head : head + 1]).astype(BF16)
        state = lax.dot_general(
            faded, values[:, own], (((0,), (0,)), ((), ())), preferred_element_type=F32
        )
        message[own, :] = state.astype(BF16)
    total = jnp.sum(decay[...], axis=1, keepdims=True)
    message[heads * width :, :] = stacked(jnp.broadcast_to(jnp.exp(total), (heads, LANES)), heads)


def weights_kernel(far_count, weight_far, _, *refs):
    *weights, token, semaphores = refs
    columns = weights[0].shape[1]
    me = lax.axis_index("head")
    copies = []
    for index in range(2 * far_count):
        owner = me ^ ((far_count - 1 - index // 2) << 1) ^ (1 - index % 2)
        source = weight_far.at[:, pl.ds(pl.multiple_of(owner * columns, LANES), columns)]
        copies.append(pltpu.make_async_copy(source, weights[index], semaphores.at[index]))
        copies[-1].start()
    token[...] = jnp.zeros_like(token)
    for copy in copies:
        copy.wait()


def within_kernel(query_far, keys_far, values_far, decay_far, _, within, grown, query, keys, values, decay, semaphores):
    for copy in fetch((query_far, keys_far, values_far, decay_far), (query, keys, values, decay), semaphores):
        copy.wait()
    heads, tokens = decay.shape
    width = keys.shape[1] // heads
    column = column_sums(decay[...])
    line = row_sums(decay[...])
    grown[...] = jnp.exp(column)
    row, col = triangle(tokens)
    for head in range(heads):
        own = slice(head * width, (head + 1) * width)
        scores = lax.dot_general(
            query[:, own], keys[:, own], (((1,), (1,)), ((), ())), preferred_element_type=F32
        )
        differ = jnp.where(row >= col, column[:, head : head + 1] - line[head : head + 1, :], -1e30)
        weights = (jnp.exp(differ) * scores).astype(BF16)
        within[:, own] = jnp.dot(weights, values[:, own], preferred_element_type=F32)


def join_kernel(step, heads, *refs):
    first = step == 0
    if first:
        mine, theirs, _, joined, entering, entering_decay = refs
    else:
        mine, theirs, before, before_decay, joined, entering, entering_decay = refs
    later = odd("ctx", step)
    rows = mine.shape[0] - padded(3 * heads)
    width = rows // heads
    my_decay = unstacked(mine[rows:, :], heads)
    their_decay = unstacked(theirs[rows:, :], heads)
    one = jnp.ones_like(my_decay)
    for_theirs = jnp.where(later, my_decay, one)
    for_mine = jnp.where(later, one, their_decay)
    if first:
        for_entering = jnp.where(later, one, 0.0 * one)
        entering_decay[...] = jnp.where(later, their_decay, one)
    else:
        for_entering = jnp.where(later, before_decay[...], 0.0 * one)
        entering_decay[...] = before_decay[...] * jnp.where(later, their_decay, one)
    for head in range(heads):
        own = slice(head * width, (head + 1) * width)
        row = slice(head, head + 1)
        received = theirs[own, :].astype(F32)
        joined[own, :] = (for_theirs[row] * received + for_mine[row] * mine[own, :].astype(F32)).astype(BF16)
        added = for_entering[row] * received
        entering[own, :] = added if first else before[own, :] + added
    joined[rows:, :] = stacked(my_decay * their_decay, heads)


def attend_kernel(step, heads, query, within, grown, before, before_decay, theirs, gain, message):
    later = odd("ctx", step)
    tokens, full = query.shape
    width = full // heads
    scale = jnp.where(later, before_decay[...], 0.0 * before_decay[...])
    squares = jnp.zeros((tokens, 1), F32)
    for head in range(heads):
        own = slice(head * width, (head + 1) * width)
        state = before[own, :] + scale[head : head + 1] * theirs[own, :].astype(F32)
        carried = jnp.dot(query[:, own], state.astype(BF16), preferred_element_type=F32)
        attn = within[:, own] + grown[:, head : head + 1] * carried
        squares = squares + jnp.sum(attn * attn, axis=1, keepdims=True)
        message[:, own] = (attn * gain[:, own]).astype(BF16)
    high, mid, low = split3(squares)
    lane = lax.broadcasted_iota(jnp.int32, (tokens, LANES), 1)
    pieces = jnp.where(lane == 0, high.astype(F32), 0.0)
    pieces = jnp.where(lane == 1, mid.astype(F32), pieces)
    message[:, full:] = jnp.where(lane == 2, low.astype(F32), pieces).astype(BF16)


def squares_row(mine, theirs, full):
    column = jnp.sum(mine[:, full:].astype(F32) + theirs[:, full:].astype(F32), axis=1, keepdims=True)
    row, col = triangle(mine.shape[0])
    return jnp.sum(jnp.where(row == col, column, 0.0), axis=0, keepdims=True)


def product(mine, theirs, my_weight, their_weight, full):
    return jnp.dot(mine[:, :full], my_weight[...], preferred_element_type=F32) + jnp.dot(
        theirs[:, :full], their_weight[...], preferred_element_type=F32
    )


def away_kernel(full, mine, theirs, my_weight, their_weight, *refs):
    *received, message = refs
    tokens = mine.shape[0]
    blocks = my_weight.shape[1] // LANES
    result = product(mine, theirs, my_weight, their_weight, full)
    for block in range(blocks):
        there = slice(block * tokens, (block + 1) * tokens)
        part = result[:, block * LANES : (block + 1) * LANES]
        for other in received:
            part = part + other[there, :].astype(F32)
        message[there, :] = part.astype(BF16)
    total = squares_row(mine, theirs, full)
    for other in received:
        total = total + unstacked(other[blocks * tokens :, :], 1)
    message[blocks * tokens :, :] = stacked(total, 1)


def home_kernel(full, mine, theirs, my_weight, their_weight, result):
    result[...] = product(mine, theirs, my_weight, their_weight, full)


def finish_kernel(full, mine, theirs, partial, *refs):
    *received, out, staged, semaphores = refs
    tokens, columns = partial.shape
    blocks = columns // LANES
    total = squares_row(mine, theirs, full)
    for other in received:
        total = total + unstacked(other[blocks * tokens :, :], 1)
    row, col = triangle(tokens)
    total = jnp.sum(jnp.where(row == col, total, 0.0), axis=1, keepdims=True)
    scale = lax.rsqrt(total / (full * lax.axis_size("head")) + 1e-05)
    count = semaphores.shape[0]
    copies = []
    for chunk in range(count):
        for block in range(chunk * blocks // count, (chunk + 1) * blocks // count):
            own = slice(block * LANES, (block + 1) * LANES)
            summed = partial[:, own]
            for other in received:
                summed = summed + other[block * tokens : (block + 1) * tokens, :].astype(F32)
            staged[:, own] = (summed * scale).astype(BF16)
        whole = slice(chunk * blocks // count * LANES, (chunk + 1) * blocks // count * LANES)
        copies.append(pltpu.make_async_copy(staged.at[:, whole], out.at[:, whole], semaphores.at[chunk]))
        copies[-1].start()
    for copy in copies:
        copy.wait()


def local(query, keys, values, log_decay, norm_gain, out_weight):
    tokens, full = query.shape
    heads = log_decay.shape[1]
    steps = lax.axis_size("ctx").bit_length() - 1
    groups = lax.axis_size("head")
    columns = out_weight.shape[1] // groups
    decay = log_decay.T
    message_shape = shape((full + padded(3 * heads), LANES), BF16)
    dma = pltpu.SemaphoreType.DMA

    def swap(value, axis, bit):
        count = lax.axis_size(axis)
        return lax.ppermute(value, axis, [(i, i ^ bit) for i in range(count)])

    blocks = [pltpu.VMEM(array.shape, array.dtype) for array in (query, keys, values, decay)]
    (message,) = call(
        states_kernel,
        [message_shape],
        (keys, values, decay),
        far=3,
        scratch=[*blocks[1:], dma((3,))],
    )
    theirs = swap(message, "ctx", 1)

    far_count = groups // 2
    *weights, token = call(
        functools.partial(weights_kernel, far_count),
        [shape((full, columns), BF16)] * (2 * far_count) + [shape((8, LANES), F32)],
        (out_weight, message),
        far=1,
        scratch=[dma((2 * far_count,))],
        cost=2.0,
    )
    my_weights, their_weights = {}, {}
    for index in range(0, 2 * far_count, 2):
        far = far_count - 1 - index // 2
        their_weights[far] = swap(weights[index], "head", 1)
        my_weights[far] = weights[index + 1]

    entering = (token,)
    for step in range(steps - 1):
        message, *entering = call(
            functools.partial(join_kernel, step, heads),
            [message_shape, shape((full, LANES), F32), shape((heads, LANES), F32)],
            (message, theirs, *entering),
            cost=30.0 if step == steps - 2 else 0.1,
        )
        theirs = swap(message, "ctx", 2 << step)
        if step == 0:
            within, grown = call(
                within_kernel,
                [shape((tokens, full), F32), shape((tokens, heads), F32)],
                (query, keys, values, decay, message),
                far=4,
                scratch=[*blocks, dma((4,))],
                cost=1.0,
            )
    (mine,) = call(
        functools.partial(attend_kernel, steps - 1, heads),
        [shape((tokens, full + LANES), BF16)],
        (query, within, grown, *entering, theirs, norm_gain[None, :]),
    )
    mate = swap(mine, "head", 1)

    received = [[] for _ in range(far_count)]
    reach = far_count // 2
    while reach:
        for far in range(reach, 2 * reach):
            (away,) = call(
                functools.partial(away_kernel, full),
                [shape((columns // LANES * tokens + SUBLANES, LANES), BF16)],
                (mine, mate, my_weights[far], their_weights[far], *received[far]),
            )
            received[far - reach].append(swap(away, "head", reach << 1))
        reach //= 2
    (partial,) = call(
        functools.partial(home_kernel, full),
        [shape((tokens, columns), F32)],
        (mine, mate, my_weights[0], their_weights[0]),
    )
    (mixed,) = call(
        functools.partial(finish_kernel, full),
        [shape((tokens, columns), BF16)],
        (mine, mate, partial, *received[0]),
        out_places=[FAR],
        scratch=[pltpu.VMEM((tokens, columns), BF16), dma((3,))],
    )
    return mixed


def solution(mesh):
    placed = (
        P("ctx", "head"),
        P("ctx", "head"),
        P("ctx", "head"),
        P("ctx", "head"),
        P("head"),
        P("head", None),
    )
    return jax.shard_map(
        local, mesh=mesh, in_specs=placed, out_specs=P("ctx", "head"), check_vma=False
    )
```

time: 116 us -> 35.9 us (0.31)
  waiting for transfers between devices: 52.8 us -> 16.5 us
  blocking collectives: 28.8 us -> 0 us
  between operations: 14.1 us -> 0.07 us
  starting transfers between devices: 0.04 us -> 10.1 us
  Pallas kernels: 0 us -> 9.1 us
  other arithmetic: 8.61 us -> 0 us
  matrix products: 8.53 us -> 0 us
  local copies, waits for them, and re-layouts: 2.85 us -> 0.01 us
    reduce_scatter x1 -> x0, waiting for transfers between devices: 27.1 us -> none  [local(): lax.psum_scatter(partial_out.astype(jnp.bfloat16), 'head', scatter_dimens...]
    all_gather x1 -> x0, waiting for transfers between devices: 25.7 us -> none  [entering(): pieces = jax.tree.map(lambda part: lax.all_gather(part, axis), value)]
    unnamed x1 -> x0, blocking collectives: 23.2 us -> none
    ppermute x0 -> x7, waiting for transfers between devices: none -> 16.5 us  [swap(): return lax.ppermute(value, axis, [(i, i ^ bit) for i in range(count)])]
    ppermute x0 -> x7, starting transfers between devices: none -> 10.1 us  [swap(): return lax.ppermute(value, axis, [(i, i ^ bit) for i in range(count)])]
    pallas_call x0 -> x9, Pallas kernels: none -> 9.1 us  [call(): pl.pallas_call(body, out_shape=outs, in_specs=[FAR] * far + [VMEM] * (len...]
    dot_general x4 -> x0, matrix products: 8.53 us -> none  [the longest x1 4.97 us: local(): jnp.dot(normed, out_weight, preferred_element_type=jnp.float32)]
    select_n x7 -> x0, other arithmetic: 7.36 us -> none  [hop(): jnp.where(position < mine, new, old)]
  transfers between devices with their start and end apart: 2 -> 7, of which waited for: 2 -> 5; matrix products, arithmetic and copies ran while one was open for 2% -> 0% of each run, Pallas kernels for 0% -> 18%
where the time goes in v1:
time: 35.9 us; the launch traced here: 35.7 us
  waiting for transfers between devices  16.5 us (46%)
  starting transfers between devices  10.1 us (28%)
  Pallas kernels  9.1 us (25%)
    ppermute x7, waiting for transfers between devices, swap(): return lax.ppermute(value, axis, [(i, i ^ bit) for i in range(count)])  16.5 us
    ppermute x7, starting transfers between devices, swap(): return lax.ppermute(value, axis, [(i, i ^ bit) for i in range(count)])  10.1 us
    pallas_call x9, Pallas kernels, call(): pl.pallas_call(body, out_shape=outs, in_specs=[FAR] * far + [VMEM] * (len...  9.1 us
  transfers between devices with their start and end apart: 7, of which 5 were waited for; matrix products, arithmetic and copies ran while one was open for 0% of the time, Pallas kernels for 18%

profile of v1, /device:TPU:0, one launch (start us, length us, event | category | flops | bytes accessed | tf_op | source)
XLA Modules:
  0.0 35.7 jit_solution(5216118353954019339)
XLA Ops:
  0.0 1.5 %shard_map.64._.refs_0_ = bf16[528,128]{1,0:T(8,128)(2,1)S(1)} custom-call(bf16[128,512]{1,0:T(8,128)(2,1)} %keys_far.3, bf16[128,512]{1,0:T(8,128)(2,1)} %values_far.3, f32[4,128]{1,0:T(4,128)} %bitcast.3), custom_call_target="tpu_custom_call" | custom-call | flops 1000000000 | bytes 1000000 | tf_op jit(solution)/shard_map/pallas_call | solution.py:20
  1.6 3.0 %collective-permute-start = (bf16[528,128]{1,0:T(8,128)(2,1)S(1)}, bf16[528,128]{1,0:T(8,128)(2,1)S(1)}, u32[]{:S(2)}, u32[]{:S(2)}) collective-permute-start(bf16[528,128]{1,0:T(8,128)(2,1)S(1)} %shard_map.64._.refs_0_), channel_id=1, source_target_pairs={{0,4},{4,0},{8,12},{12,8},{16,20},{20,16},{24,28},{28,24},{1,5},{5... | collective-permute-start | bytes 405512 | tf_op jit(solution)/shard_map/ppermute | solution.py:264
  4.6 2.9 %shard_map.65 = (bf16[512,1536]{1,0:T(8,128)(2,1)S(1)}, bf16[512,1536]{1,0:T(8,128)(2,1)S(1)}, bf16[512,1536]{1,0:T(8,128)(2,1)S(1)}, bf16[512,1536]{1,0:T(8,128)(2,1)S(1)}, f32[8,128]{1,0:T(8,128)S(1)}) custom-call(bf16[512,6144]{1,0:T(8,128)(2,1)} %weight_far.1, bf16[528,128]{1,0:T(8,128)(2,1)S(1)} %shard_map.64._.refs_0_), custom_call_target="tpu_custom_call" | custom-call | flops 2000000000 | bytes 2000000 | tf_op jit(solution)/shard_map/pallas_call | solution.py:20
  7.5 0.7 %collective-permute-done.refs_1_ = bf16[528,128]{1,0:T(8,128)(2,1)S(1)} collective-permute-done((bf16[528,128]{1,0:T(8,128)(2,1)S(1)}, bf16[528,128]{1,0:T(8,128)(2,1)S(1)}, u32[]{:S(2)}, u32[]{:S(2)}) %collective-permute-start) | collective-permute-done | bytes 135200 | tf_op jit(solution)/shard_map/ppermute | solution.py:264
  8.2 0.1 shard_map.66
  8.3 1.9 %collective-permute-start.1 = (bf16[528,128]{1,0:T(8,128)(2,1)S(1)}, bf16[528,128]{1,0:T(8,128)(2,1)S(1)}, u32[]{:S(2)}, u32[]{:S(2)}) collective-permute-start(bf16[528,128]{1,0:T(8,128)(2,1)S(1)} %get-tuple-element.19._.refs_0_), channel_id=1, source_target_pairs={{0,8},{4,12},{8,0},{12,4},{16,24},{20,28},{24,16},{28,20},{1,9},{5... | collective-permute-start | bytes 405512 | tf_op jit(solution)/shard_map/ppermute | solution.py:264
  10.1 0.0 collective-permute-start.4
  10.1 0.5 %collective-permute-start.5 = (bf16[512,1536]{1,0:T(8,128)(2,1)S(1)}, bf16[512,1536]{1,0:T(8,128)(2,1)S(1)}, u32[]{:S(2)}, u32[]{:S(2)}) collective-permute-start(bf16[512,1536]{1,0:T(8,128)(2,1)S(1)} %get-tuple-element.30), channel_id=1, source_target_pairs={{0,1},{1,0},{2,3},{3,2},{4,5},{5,4},{6,7},{7,6},{8,9},{9,8},{10,11... | collective-permute-start | bytes 4718600 | tf_op jit(solution)/shard_map/ppermute | solution.py:264
  10.6 2.7 %collective-permute-done.1.refs_1_ = bf16[528,128]{1,0:T(8,128)(2,1)S(1)} collective-permute-done((bf16[528,128]{1,0:T(8,128)(2,1)S(1)}, bf16[528,128]{1,0:T(8,128)(2,1)S(1)}, u32[]{:S(2)}, u32[]{:S(2)}) %collective-permute-start.1) | collective-permute-done | bytes 135200 | tf_op jit(solution)/shard_map/ppermute | solution.py:264
  13.3 0.1 shard_map.68
  13.4 0.0 copy-start
  13.5 0.0 copy-start.1
  13.5 2.9 %collective-permute-start.2 = (bf16[528,128]{1,0:T(8,128)(2,1)S(1)}, bf16[528,128]{1,0:T(8,128)(2,1)S(1)}, u32[]{:S(2)}, u32[]{:S(2)}) collective-permute-start(bf16[528,128]{1,0:T(8,128)(2,1)S(1)} %get-tuple-element.26), channel_id=1, source_target_pairs={{0,16},{4,20},{8,24},{12,28},{16,0},{20,4},{24,8},{28,12},{1,17},{... | collective-permute-start | bytes 405512 | tf_op jit(solution)/shard_map/ppermute | solution.py:264
  16.3 2.0 %shard_map.67 = (f32[128,512]{1,0:T(8,128)S(1)}, f32[128,4]{1,0:T(8,128)S(1)}) custom-call(bf16[128,512]{1,0:T(8,128)(2,1)} %query.1, bf16[128,512]{1,0:T(8,128)(2,1)} %keys_far.3, bf16[128,512]{1,0:T(8,128)(2,1)} %values_far.3, f32[4,128]{1,0:T(4,128)} %bitcast.4, bf16[528,128]{1,0:T(8,128)(2,1)S(1)} %get-tuple-element.19._.refs_0_), custom_call_target="tpu_custom_call" | custom-call | flops 1000000000 | bytes 1000000 | tf_op jit(solution)/shard_map/pallas_call | solution.py:20
  18.3 2.6 %collective-permute-done.2.theirs = bf16[528,128]{1,0:T(8,128)(2,1)S(1)} collective-permute-done((bf16[528,128]{1,0:T(8,128)(2,1)S(1)}, bf16[528,128]{1,0:T(8,128)(2,1)S(1)}, u32[]{:S(2)}, u32[]{:S(2)}) %collective-permute-start.2) | collective-permute-done | bytes 135200 | tf_op jit(solution)/shard_map/ppermute | solution.py:264
  20.9 0.0 copy-done
  21.0 0.0 copy-done.1
  21.0 0.4 %shard_map.69.mine = bf16[128,640]{1,0:T(8,128)(2,1)S(1)} custom-call(bf16[128,512]{1,0:T(8,128)(2,1)S(1)} %copy-done, f32[128,512]{1,0:T(8,128)S(1)} %get-tuple-element.20.within, f32[128,4]{1,0:T(8,128)S(1)} %get-tuple-element.21.grown, f32[512,128]{1,0:T(8,128)S(1)} %get-tuple-element.24.before, f32[4,128]{1,0:T(4,128)S(1)} %get-tuple-element.25.before_decay, ...), custom_call_target="tpu_custom_call" | custom-call | flops 1000000000 | bytes 1000000 | tf_op jit(solution)/shard_map/pallas_call | solution.py:20
  21.3 0.1 collective-permute-start.3
  21.4 1.4 %collective-permute-done.3.theirs = bf16[128,640]{1,0:T(8,128)(2,1)S(1)} collective-permute-done((bf16[128,640]{1,0:T(8,128)(2,1)S(1)}, bf16[128,640]{1,0:T(8,128)(2,1)S(1)}, u32[]{:S(2)}, u32[]{:S(2)}) %collective-permute-start.3) | collective-permute-done | bytes 163872 | tf_op jit(solution)/shard_map/ppermute | solution.py:264
  22.8 0.0 collective-permute-done.5.their_weight
  22.8 0.6 %shard_map.71 = bf16[1552,128]{1,0:T(8,128)(2,1)S(1)} custom-call(bf16[128,640]{1,0:T(8,128)(2,1)S(1)} %shard_map.69.mine, bf16[128,640]{1,0:T(8,128)(2,1)S(1)} %collective-permute-done.3.theirs, bf16[512,1536]{1,0:T(8,128)(2,1)S(1)} %get-tuple-element.29.my_weight, bf16[512,1536]{1,0:T(8,128)(2,1)S(1)} %collective-permute-done.5.their_weight), custom_call_target="tpu_custom_call" | custom-call | flops 1000000000 | bytes 1000000 | tf_op jit(solution)/shard_map/pallas_call | solution.py:20
  23.4 1.7 %collective-permute-start.6 = (bf16[1552,128]{1,0:T(8,128)(2,1)S(1)}, bf16[1552,128]{1,0:T(8,128)(2,1)S(1)}, u32[]{:S(2)}, u32[]{:S(2)}) collective-permute-start(bf16[1552,128]{1,0:T(8,128)(2,1)S(1)} %shard_map.71), channel_id=1, source_target_pairs={{0,2},{1,3},{2,0},{3,1},{4,6},{5,7},{6,4},{7,5},{8,10},{9,11},{10,... | collective-permute-start | bytes 1191944 | tf_op jit(solution)/shard_map/ppermute | solution.py:264
  25.1 0.0 collective-permute-done.4.their_weight
  25.1 0.6 %shard_map.70.partial = f32[128,1536]{1,0:T(8,128)S(1)} custom-call(bf16[128,640]{1,0:T(8,128)(2,1)S(1)} %shard_map.69.mine, bf16[128,640]{1,0:T(8,128)(2,1)S(1)} %collective-permute-done.3.theirs, bf16[512,1536]{1,0:T(8,128)(2,1)S(1)} %get-tuple-element.27.my_weight, bf16[512,1536]{1,0:T(8,128)(2,1)S(1)} %collective-permute-done.4.their_weight), custom_call_target="tpu_custom_call" | custom-call | flops 1000000000 | bytes 1000000 | tf_op jit(solution)/shard_map/pallas_call | solution.py:20
  25.7 9.0 %collective-permute-done.6.refs_0_ = bf16[1552,128]{1,0:T(8,128)(2,1)S(1)} collective-permute-done((bf16[1552,128]{1,0:T(8,128)(2,1)S(1)}, bf16[1552,128]{1,0:T(8,128)(2,1)S(1)}, u32[]{:S(2)}, u32[]{:S(2)}) %collective-permute-start.6) | collective-permute-done | bytes 397344 | tf_op jit(solution)/shard_map/ppermute | solution.py:264
  34.7 1.0 %shard_map.72 = bf16[128,1536]{1,0:T(8,128)(2,1)} custom-call(bf16[128,640]{1,0:T(8,128)(2,1)S(1)} %shard_map.69.mine, bf16[128,640]{1,0:T(8,128)(2,1)S(1)} %collective-permute-done.3.theirs, f32[128,1536]{1,0:T(8,128)S(1)} %shard_map.70.partial, bf16[1552,128]{1,0:T(8,128)(2,1)S(1)} %collective-permute-done.6.refs_0_), custom_call_target="tpu_custom_call" | custom-call | flops 1000000000 | bytes 1000000 | tf_op jit(solution)/shard_map/pallas_call | solution.py:20
Async XLA Ops:
  1.6 6.6 %collective-permute-start = (bf16[528,128]{1,0:T(8,128)(2,1)S(1)}, bf16[528,128]{1,0:T(8,128)(2,1)S(1)}, u32[]{:S(2)}, u32[]{:S(2)}) collective-permute-start(bf16[528,128]{1,0:T(8,128)(2,1)S(1)} %shard_map.64._.refs_0_), channel_id=1, source_target_pairs={{0,4},{4,0},{8,12},{12,8},{16,20},{20,16},{24,28},{28,24},{1,5},{5... | collective-permute-start | bytes 405512 | tf_op jit(solution)/shard_map/ppermute | solution.py:264
  8.3 5.1 %collective-permute-start.1 = (bf16[528,128]{1,0:T(8,128)(2,1)S(1)}, bf16[528,128]{1,0:T(8,128)(2,1)S(1)}, u32[]{:S(2)}, u32[]{:S(2)}) collective-permute-start(bf16[528,128]{1,0:T(8,128)(2,1)S(1)} %get-tuple-element.19._.refs_0_), channel_id=1, source_target_pairs={{0,8},{4,12},{8,0},{12,4},{16,24},{20,28},{24,16},{28,20},{1,9},{5... | collective-permute-start | bytes 405512 | tf_op jit(solution)/shard_map/ppermute | solution.py:264
  10.1 15.0 %collective-permute-start.4 = (bf16[512,1536]{1,0:T(8,128)(2,1)S(1)}, bf16[512,1536]{1,0:T(8,128)(2,1)S(1)}, u32[]{:S(2)}, u32[]{:S(2)}) collective-permute-start(bf16[512,1536]{1,0:T(8,128)(2,1)S(1)} %get-tuple-element.28), channel_id=1, source_target_pairs={{0,1},{1,0},{2,3},{3,2},{4,5},{5,4},{6,7},{7,6},{8,9},{9,8},{10,11... | collective-permute-start | bytes 4718600 | tf_op jit(solution)/shard_map/ppermute | solution.py:264
  10.1 12.7 %collective-permute-start.5 = (bf16[512,1536]{1,0:T(8,128)(2,1)S(1)}, bf16[512,1536]{1,0:T(8,128)(2,1)S(1)}, u32[]{:S(2)}, u32[]{:S(2)}) collective-permute-start(bf16[512,1536]{1,0:T(8,128)(2,1)S(1)} %get-tuple-element.30), channel_id=1, source_target_pairs={{0,1},{1,0},{2,3},{3,2},{4,5},{5,4},{6,7},{7,6},{8,9},{9,8},{10,11... | collective-permute-start | bytes 4718600 | tf_op jit(solution)/shard_map/ppermute | solution.py:264
  13.4 7.5 %copy-start = (bf16[128,512]{1,0:T(8,128)(2,1)S(1)}, bf16[128,512]{1,0:T(8,128)(2,1)}, u32[]{:S(2)}) copy-start(bf16[128,512]{1,0:T(8,128)(2,1)} %query.1) | copy-start | bytes 393220
  13.5 7.5 %copy-start.1 = (f32[512]{0:T(512)S(1)}, f32[512]{0:T(512)}, u32[]{:S(2)}) copy-start(f32[512]{0:T(512)} %param.10) | copy-start | bytes 6148
  13.5 7.5 %collective-permute-start.2 = (bf16[528,128]{1,0:T(8,128)(2,1)S(1)}, bf16[528,128]{1,0:T(8,128)(2,1)S(1)}, u32[]{:S(2)}, u32[]{:S(2)}) collective-permute-start(bf16[528,128]{1,0:T(8,128)(2,1)S(1)} %get-tuple-element.26), channel_id=1, source_target_pairs={{0,16},{4,20},{8,24},{12,28},{16,0},{20,4},{24,8},{28,12},{1,17},{... | collective-permute-start | bytes 405512 | tf_op jit(solution)/shard_map/ppermute | solution.py:264
  21.3 1.5 %collective-permute-start.3 = (bf16[128,640]{1,0:T(8,128)(2,1)S(1)}, bf16[128,640]{1,0:T(8,128)(2,1)S(1)}, u32[]{:S(2)}, u32[]{:S(2)}) collective-permute-start(bf16[128,640]{1,0:T(8,128)(2,1)S(1)} %shard_map.69.mine), channel_id=1, source_target_pairs={{0,1},{1,0},{2,3},{3,2},{4,5},{5,4},{6,7},{7,6},{8,9},{9,8},{10,11... | collective-permute-start | bytes 491528 | tf_op jit(solution)/shard_map/ppermute | solution.py:264
  23.4 11.3 %collective-permute-start.6 = (bf16[1552,128]{1,0:T(8,128)(2,1)S(1)}, bf16[1552,128]{1,0:T(8,128)(2,1)S(1)}, u32[]{:S(2)}, u32[]{:S(2)}) collective-permute-start(bf16[1552,128]{1,0:T(8,128)(2,1)S(1)} %shard_map.71), channel_id=1, source_target_pairs={{0,2},{1,3},{2,0},{3,1},{4,6},{5,7},{6,4},{7,5},{8,10},{9,11},{10,... | collective-permute-start | bytes 1191944 | tf_op jit(solution)/shard_map/ppermute | solution.py:264

commit v2 on v1

--- a/solution.py
+++ b/solution.py
@@ -13,6 +13,7 @@
 FAR = pl.BlockSpec(memory_space=pltpu.HBM)
 LANES = 128
 SUBLANES = 16
+PARTS = 3
 
 
 def call(body, outs, operands, far=0, out_places=None, scratch=(), cost=1.0):
@@ -89,11 +90,13 @@
 
 
 def states_kernel(keys_far, values_far, decay_far, message, keys, values, decay, semaphores):
-    for copy in fetch((keys_far, values_far, decay_far), (keys, values, decay), semaphores):
-        copy.wait()
+    decay_copy, *copies = fetch((decay_far, keys_far, values_far), (decay, keys, values), semaphores)
+    decay_copy.wait()
     heads, tokens = decay.shape
     width = keys.shape[1] // heads
     column = column_sums(decay[...])
+    for copy in copies:
+        copy.wait()
     tail = jnp.exp(column[tokens - 1 : tokens, :] - column)
     for head in range(heads):
         own = slice(head * width, (head + 1) * width)
@@ -167,7 +170,8 @@
         joined[own, :] = (for_theirs[row] * received + for_mine[row] * mine[own, :].astype(F32)).astype(BF16)
         added = for_entering[row] * received
         entering[own, :] = added if first else before[own, :] + added
-    joined[rows:, :] = stacked(my_decay * their_decay, heads)
+    if joined.shape[0] > rows:
+        joined[rows:, :] = stacked(my_decay * their_decay, heads)
 
 
 def attend_kernel(step, heads, query, within, grown, before, before_decay, theirs, gain, message):
@@ -196,55 +200,78 @@
     return jnp.sum(jnp.where(row == col, column, 0.0), axis=0, keepdims=True)
 
 
-def product(mine, theirs, my_weight, their_weight, full):
-    return jnp.dot(mine[:, :full], my_weight[...], preferred_element_type=F32) + jnp.dot(
-        theirs[:, :full], their_weight[...], preferred_element_type=F32
-    )
-
-
-def away_kernel(full, mine, theirs, my_weight, their_weight, *refs):
+def ahead_kernel(full, mine, weight, result):
+    result[...] = jnp.dot(mine[:, :full], weight[...], preferred_element_type=F32)
+
+
+def away_kernel(full, first_block, partial, mine, theirs, their_weight, *refs):
     *received, message = refs
     tokens = mine.shape[0]
-    blocks = my_weight.shape[1] // LANES
-    result = product(mine, theirs, my_weight, their_weight, full)
+    blocks = message.shape[0] // tokens
+    columns = slice(first_block * LANES, (first_block + blocks) * LANES)
+    result = partial[:, columns] + jnp.dot(theirs[:, :full], their_weight[:, columns], preferred_element_type=F32)
     for block in range(blocks):
         there = slice(block * tokens, (block + 1) * tokens)
         part = result[:, block * LANES : (block + 1) * LANES]
         for other in received:
             part = part + other[there, :].astype(F32)
         message[there, :] = part.astype(BF16)
+    if first_block == 0:
+        total = squares_row(mine, theirs, full)
+        for other in received:
+            total = total + unstacked(other[blocks * tokens :, :], 1)
+        message[blocks * tokens :, :] = stacked(total, 1)
+
+
+def home_kernel(full, mine, theirs, my_weight, their_weight, result):
+    result[...] = jnp.dot(mine[:, :full], my_weight[...], preferred_element_type=F32) + jnp.dot(
+        theirs[:, :full], their_weight[...], preferred_element_type=F32
+    )
+
+
+def scaled(partial, first_block, received, scale, out):
+    tokens, columns = out.shape
+    for block in range(columns // LANES):
+        summed = partial[:, (first_block + block) * LANES : (first_block + block + 1) * LANES]
+        for other in received:
+            summed = summed + other[block * tokens : (block + 1) * tokens, :].astype(F32)
+        out[:, block * LANES : (block + 1) * LANES] = (summed * scale).astype(BF16)
+
+
+def first_kernel(full, mine, theirs, partial, *refs):
+    *received, scale, out = refs
+    tokens, columns = out.shape
     total = squares_row(mine, theirs, full)
     for other in received:
-        total = total + unstacked(other[blocks * tokens :, :], 1)
-    message[blocks * tokens :, :] = stacked(total, 1)
-
-
-def home_kernel(full, mine, theirs, my_weight, their_weight, result):
-    result[...] = product(mine, theirs, my_weight, their_weight, full)
-
-
-def finish_kernel(full, mine, theirs, partial, *refs):
-    *received, out, staged, semaphores = refs
-    tokens, columns = partial.shape
-    blocks = columns // LANES
-    total = squares_row(mine, theirs, full)
-    for other in received:
-        total = total + unstacked(other[blocks * tokens :, :], 1)
+        total = total + unstacked(other[columns // LANES * tokens :, :], 1)
     row, col = triangle(tokens)
     total = jnp.sum(jnp.where(row == col, total, 0.0), axis=1, keepdims=True)
-    scale = lax.rsqrt(total / (full * lax.axis_size("head")) + 1e-05)
-    count = semaphores.shape[0]
+    factor = lax.rsqrt(total / (full * lax.axis_size("head")) + 1e-05)
+    scale[...] = factor
+    scaled(partial, 0, received, factor, out)
+
+
+def middle_kernel(first_block, partial, scale, *refs):
+    *received, out = refs
+    scaled(partial, first_block, received, scale[...], out)
+
+
+def last_kernel(first_block, done_count, partial, scale, *refs):
+    done, received = refs[:done_count], refs[done_count:-3]
+    out, staged, semaphores = refs[-3:]
     copies = []
-    for chunk in range(count):
-        for block in range(chunk * blocks // count, (chunk + 1) * blocks // count):
-            own = slice(block * LANES, (block + 1) * LANES)
-            summed = partial[:, own]
-            for other in received:
-                summed = summed + other[block * tokens : (block + 1) * tokens, :].astype(F32)
-            staged[:, own] = (summed * scale).astype(BF16)
-        whole = slice(chunk * blocks // count * LANES, (chunk + 1) * blocks // count * LANES)
-        copies.append(pltpu.make_async_copy(staged.at[:, whole], out.at[:, whole], semaphores.at[chunk]))
+
+    def write(source, column):
+        there = out.at[:, column : column + source.shape[1]]
+        copies.append(pltpu.make_async_copy(source, there, semaphores.at[len(copies)]))
         copies[-1].start()
+
+    column = 0
+    for part in done:
+        write(part, column)
+        column += part.shape[1]
+    scaled(partial, first_block, received, scale[...], staged)
+    write(staged, column)
     for copy in copies:
         copy.wait()
 
@@ -292,7 +319,11 @@
     for step in range(steps - 1):
         message, *entering = call(
             functools.partial(join_kernel, step, heads),
-            [message_shape, shape((full, LANES), F32), shape((heads, LANES), F32)],
+            [
+                message_shape if step < steps - 2 else shape((full, LANES), BF16),
+                shape((full, LANES), F32),
+                shape((heads, LANES), F32),
+            ],
             (message, theirs, *entering),
             cost=30.0 if step == steps - 2 else 0.1,
         )
@@ -312,29 +343,57 @@
         (query, within, grown, *entering, theirs, norm_gain[None, :]),
     )
     mate = swap(mine, "head", 1)
-
-    received = [[] for _ in range(far_count)]
+    ahead = {}
+    for far in range(1, far_count):
+        (ahead[far],) = call(
+            functools.partial(ahead_kernel, full),
+            [shape((tokens, columns), F32)],
+            (mine, my_weights[far]),
+            cost=0.4,
+        )
+
+    blocks_out = columns // LANES
+    cuts = [0, blocks_out // 4, blocks_out - blocks_out // 6, blocks_out]
+    received = [[[] for _ in range(PARTS)] for _ in range(far_count)]
     reach = far_count // 2
     while reach:
         for far in range(reach, 2 * reach):
-            (away,) = call(
-                functools.partial(away_kernel, full),
-                [shape((columns // LANES * tokens + SUBLANES, LANES), BF16)],
-                (mine, mate, my_weights[far], their_weights[far], *received[far]),
-            )
-            received[far - reach].append(swap(away, "head", reach << 1))
+            for part, (first, end) in enumerate(zip(cuts[:-1], cuts[1:])):
+                (away,) = call(
+                    functools.partial(away_kernel, full, first),
+                    [shape(((end - first) * tokens + (SUBLANES if first == 0 else 0), LANES), BF16)],
+                    (ahead[far], mine, mate, their_weights[far], *received[far][part]),
+                    cost=0.2,
+                )
+                received[far - reach][part].append(swap(away, "head", reach << 1))
         reach //= 2
     (partial,) = call(
         functools.partial(home_kernel, full),
         [shape((tokens, columns), F32)],
         (mine, mate, my_weights[0], their_weights[0]),
-    )
+        cost=0.6,
+    )
+    widths = [(end - first) * LANES for first, end in zip(cuts[:-1], cuts[1:])]
+    scale, part_done = call(
+        functools.partial(first_kernel, full),
+        [shape((tokens, 1), F32), shape((tokens, widths[0]), BF16)],
+        (mine, mate, partial, *received[0][0]),
+        cost=0.3,
+    )
+    done = [part_done]
+    for part in range(1, PARTS - 1):
+        done += call(
+            functools.partial(middle_kernel, cuts[part]),
+            [shape((tokens, widths[part]), BF16)],
+            (partial, scale, *received[0][part]),
+            cost=0.2,
+        )
     (mixed,) = call(
-        functools.partial(finish_kernel, full),
+        functools.partial(last_kernel, cuts[PARTS - 1], len(done)),
         [shape((tokens, columns), BF16)],
-        (mine, mate, partial, *received[0]),
+        (partial, scale, *done, *received[0][PARTS - 1]),
         out_places=[FAR],
-        scratch=[pltpu.VMEM((tokens, columns), BF16), dma((3,))],
+        scratch=[pltpu.VMEM((tokens, widths[-1]), BF16), dma((PARTS,))],
     )
     return mixed
 

time: 35.9 us -> 35 us (0.975)
  waiting for transfers between devices: 16.5 us -> 12.9 us
  starting transfers between devices: 10.1 us -> 12.3 us
  Pallas kernels: 9.1 us -> 9.5 us
    ppermute x7 -> x9, waiting for transfers between devices: 16.5 us -> 12.9 us  [swap(): return lax.ppermute(value, axis, [(i, i ^ bit) for i in range(count)])]
    ppermute x7 -> x9, starting transfers between devices: 10.1 us -> 12.3 us  [swap(): return lax.ppermute(value, axis, [(i, i ^ bit) for i in range(count)])]
    pallas_call x9 -> x14, Pallas kernels: 9.1 us -> 9.5 us  [call(): pl.pallas_call(body, out_shape=outs, in_specs=[FAR] * far + [VMEM] * (len...]
  transfers between devices with their start and end apart: 7 -> 9, of which waited for: 5 -> 6; matrix products, arithmetic and copies ran while one was open for 0% -> 0% of each run, Pallas kernels for 18% -> 21%
where the time goes in v2:
time: 35 us; the launch traced here: 34.8 us
  waiting for transfers between devices  12.9 us (37%)
  starting transfers between devices  12.3 us (35%)
  Pallas kernels  9.5 us (27%)
    ppermute x9, waiting for transfers between devices, swap(): return lax.ppermute(value, axis, [(i, i ^ bit) for i in range(count)])  12.9 us
    ppermute x9, starting transfers between devices, swap(): return lax.ppermute(value, axis, [(i, i ^ bit) for i in range(count)])  12.3 us
    pallas_call x14, Pallas kernels, call(): pl.pallas_call(body, out_shape=outs, in_specs=[FAR] * far + [VMEM] * (len...  9.5 us
  transfers between devices with their start and end apart: 9, of which 6 were waited for; matrix products, arithmetic and copies ran while one was open for 0% of the time, Pallas kernels for 21%

profile of v2, /device:TPU:0, one launch (start us, length us, event | category | flops | bytes accessed | tf_op | source)
XLA Modules:
  0.0 34.8 jit_solution(1480030323401774443)
XLA Ops:
  0.0 1.3 %shard_map.64._.refs_0_ = bf16[528,128]{1,0:T(8,128)(2,1)S(1)} custom-call(bf16[128,512]{1,0:T(8,128)(2,1)} %keys_far.3, bf16[128,512]{1,0:T(8,128)(2,1)} %values_far.3, f32[4,128]{1,0:T(4,128)} %bitcast.3), custom_call_target="tpu_custom_call" | custom-call | flops 1000000000 | bytes 1000000 | tf_op jit(solution)/shard_map/pallas_call | solution.py:21
  1.4 3.0 %collective-permute-start = (bf16[528,128]{1,0:T(8,128)(2,1)S(1)}, bf16[528,128]{1,0:T(8,128)(2,1)S(1)}, u32[]{:S(2)}, u32[]{:S(2)}) collective-permute-start(bf16[528,128]{1,0:T(8,128)(2,1)S(1)} %shard_map.64._.refs_0_), channel_id=1, source_target_pairs={{0,4},{4,0},{8,12},{12,8},{16,20},{20,16},{24,28},{28,24},{1,5},{5... | collective-permute-start | bytes 405512 | tf_op jit(solution)/shard_map/ppermute | solution.py:291
  4.4 2.9 %shard_map.65 = (bf16[512,1536]{1,0:T(8,128)(2,1)S(1)}, bf16[512,1536]{1,0:T(8,128)(2,1)S(1)}, bf16[512,1536]{1,0:T(8,128)(2,1)S(1)}, bf16[512,1536]{1,0:T(8,128)(2,1)S(1)}, f32[8,128]{1,0:T(8,128)S(1)}) custom-call(bf16[512,6144]{1,0:T(8,128)(2,1)} %weight_far.1, bf16[528,128]{1,0:T(8,128)(2,1)S(1)} %shard_map.64._.refs_0_), custom_call_target="tpu_custom_call" | custom-call | flops 2000000000 | bytes 2000000 | tf_op jit(solution)/shard_map/pallas_call | solution.py:21
  7.3 0.7 %collective-permute-done.refs_1_ = bf16[528,128]{1,0:T(8,128)(2,1)S(1)} collective-permute-done((bf16[528,128]{1,0:T(8,128)(2,1)S(1)}, bf16[528,128]{1,0:T(8,128)(2,1)S(1)}, u32[]{:S(2)}, u32[]{:S(2)}) %collective-permute-start) | collective-permute-done | bytes 135200 | tf_op jit(solution)/shard_map/ppermute | solution.py:291
  8.0 0.1 shard_map.66
  8.1 1.9 %collective-permute-start.1 = (bf16[528,128]{1,0:T(8,128)(2,1)S(1)}, bf16[528,128]{1,0:T(8,128)(2,1)S(1)}, u32[]{:S(2)}, u32[]{:S(2)}) collective-permute-start(bf16[528,128]{1,0:T(8,128)(2,1)S(1)} %get-tuple-element.21._.refs_0_), channel_id=1, source_target_pairs={{0,8},{4,12},{8,0},{12,4},{16,24},{20,28},{24,16},{28,20},{1,9},{5... | collective-permute-start | bytes 405512 | tf_op jit(solution)/shard_map/ppermute | solution.py:291
  9.9 0.0 collective-permute-start.4
  9.9 0.5 %collective-permute-start.5 = (bf16[512,1536]{1,0:T(8,128)(2,1)S(1)}, bf16[512,1536]{1,0:T(8,128)(2,1)S(1)}, u32[]{:S(2)}, u32[]{:S(2)}) collective-permute-start(bf16[512,1536]{1,0:T(8,128)(2,1)S(1)} %get-tuple-element.32), channel_id=1, source_target_pairs={{0,1},{1,0},{2,3},{3,2},{4,5},{5,4},{6,7},{7,6},{8,9},{9,8},{10,11... | collective-permute-start | bytes 4718600 | tf_op jit(solution)/shard_map/ppermute | solution.py:291
  10.4 2.7 %collective-permute-done.1.refs_1_ = bf16[528,128]{1,0:T(8,128)(2,1)S(1)} collective-permute-done((bf16[528,128]{1,0:T(8,128)(2,1)S(1)}, bf16[528,128]{1,0:T(8,128)(2,1)S(1)}, u32[]{:S(2)}, u32[]{:S(2)}) %collective-permute-start.1) | collective-permute-done | bytes 135200 | tf_op jit(solution)/shard_map/ppermute | solution.py:291
  13.1 0.1 shard_map.68
  13.2 0.0 copy-start
  13.2 0.0 copy-start.1
  13.3 2.9 %collective-permute-start.2 = (bf16[512,128]{1,0:T(8,128)(2,1)S(1)}, bf16[512,128]{1,0:T(8,128)(2,1)S(1)}, u32[]{:S(2)}, u32[]{:S(2)}) collective-permute-start(bf16[512,128]{1,0:T(8,128)(2,1)S(1)} %get-tuple-element.28), channel_id=1, source_target_pairs={{0,16},{4,20},{8,24},{12,28},{16,0},{20,4},{24,8},{28,12},{1,17},{... | collective-permute-start | bytes 393224 | tf_op jit(solution)/shard_map/ppermute | solution.py:291
  16.1 2.0 %shard_map.67 = (f32[128,512]{1,0:T(8,128)S(1)}, f32[128,4]{1,0:T(8,128)S(1)}) custom-call(bf16[128,512]{1,0:T(8,128)(2,1)} %query.1, bf16[128,512]{1,0:T(8,128)(2,1)} %keys_far.3, bf16[128,512]{1,0:T(8,128)(2,1)} %values_far.3, f32[4,128]{1,0:T(4,128)} %bitcast.4, bf16[528,128]{1,0:T(8,128)(2,1)S(1)} %get-tuple-element.21._.refs_0_), custom_call_target="tpu_custom_call" | custom-call | flops 1000000000 | bytes 1000000 | tf_op jit(solution)/shard_map/pallas_call | solution.py:21
  18.1 2.5 %collective-permute-done.2.theirs = bf16[512,128]{1,0:T(8,128)(2,1)S(1)} collective-permute-done((bf16[512,128]{1,0:T(8,128)(2,1)S(1)}, bf16[512,128]{1,0:T(8,128)(2,1)S(1)}, u32[]{:S(2)}, u32[]{:S(2)}) %collective-permute-start.2) | collective-permute-done | bytes 131104 | tf_op jit(solution)/shard_map/ppermute | solution.py:291
  20.6 0.0 copy-done
  20.6 0.0 copy-done.1
  20.6 0.4 %shard_map.69.mine = bf16[128,640]{1,0:T(8,128)(2,1)S(1)} custom-call(bf16[128,512]{1,0:T(8,128)(2,1)S(1)} %copy-done, f32[128,512]{1,0:T(8,128)S(1)} %get-tuple-element.22.within, f32[128,4]{1,0:T(8,128)S(1)} %get-tuple-element.23.grown, f32[512,128]{1,0:T(8,128)S(1)} %get-tuple-element.26.before, f32[4,128]{1,0:T(4,128)S(1)} %get-tuple-element.27.before_decay, ...), custom_call_target="tpu_custom_call" | custom-call | flops 1000000000 | bytes 1000000 | tf_op jit(solution)/shard_map/pallas_call | solution.py:21
  21.0 0.1 collective-permute-start.3
  21.0 0.4 %shard_map.71.partial = f32[128,1536]{1,0:T(8,128)S(1)} custom-call(bf16[128,640]{1,0:T(8,128)(2,1)S(1)} %shard_map.69.mine, bf16[512,1536]{1,0:T(8,128)(2,1)S(1)} %get-tuple-element.31.weight), custom_call_target="tpu_custom_call" | custom-call | flops 400000000 | bytes 400000 | tf_op jit(solution)/shard_map/pallas_call | solution.py:21
  21.4 1.0 %collective-permute-done.3.theirs = bf16[128,640]{1,0:T(8,128)(2,1)S(1)} collective-permute-done((bf16[128,640]{1,0:T(8,128)(2,1)S(1)}, bf16[128,640]{1,0:T(8,128)(2,1)S(1)}, u32[]{:S(2)}, u32[]{:S(2)}) %collective-permute-start.3) | collective-permute-done | bytes 163872 | tf_op jit(solution)/shard_map/ppermute | solution.py:291
  22.4 0.0 collective-permute-done.5.their_weight
  22.4 0.3 shard_map.74
  22.8 1.8 %collective-permute-start.7 = (bf16[896,128]{1,0:T(8,128)(2,1)S(1)}, bf16[896,128]{1,0:T(8,128)(2,1)S(1)}, u32[]{:S(2)}, u32[]{:S(2)}) collective-permute-start(bf16[896,128]{1,0:T(8,128)(2,1)S(1)} %shard_map.74), channel_id=1, source_target_pairs={{0,2},{1,3},{2,0},{3,1},{4,6},{5,7},{6,4},{7,5},{8,10},{9,11},{10,... | collective-permute-start | bytes 688136 | tf_op jit(solution)/shard_map/ppermute | solution.py:291
  24.5 0.2 shard_map.72
  24.8 0.4 %collective-permute-start.6 = (bf16[400,128]{1,0:T(8,128)(2,1)S(1)}, bf16[400,128]{1,0:T(8,128)(2,1)S(1)}, u32[]{:S(2)}, u32[]{:S(2)}) collective-permute-start(bf16[400,128]{1,0:T(8,128)(2,1)S(1)} %shard_map.72), channel_id=1, source_target_pairs={{0,2},{1,3},{2,0},{3,1},{4,6},{5,7},{6,4},{7,5},{8,10},{9,11},{10,... | collective-permute-start | bytes 307208 | tf_op jit(solution)/shard_map/ppermute | solution.py:291
  25.1 0.2 shard_map.76
  25.3 1.8 %collective-permute-start.8 = (bf16[256,128]{1,0:T(8,128)(2,1)S(1)}, bf16[256,128]{1,0:T(8,128)(2,1)S(1)}, u32[]{:S(2)}, u32[]{:S(2)}) collective-permute-start(bf16[256,128]{1,0:T(8,128)(2,1)S(1)} %shard_map.76), channel_id=1, source_target_pairs={{0,2},{1,3},{2,0},{3,1},{4,6},{5,7},{6,4},{7,5},{8,10},{9,11},{10,... | collective-permute-start | bytes 196616 | tf_op jit(solution)/shard_map/ppermute | solution.py:291
  27.1 0.0 collective-permute-done.4.their_weight
  27.1 0.6 %shard_map.70.partial = f32[128,1536]{1,0:T(8,128)S(1)} custom-call(bf16[128,640]{1,0:T(8,128)(2,1)S(1)} %shard_map.69.mine, bf16[128,640]{1,0:T(8,128)(2,1)S(1)} %collective-permute-done.3.theirs, bf16[512,1536]{1,0:T(8,128)(2,1)S(1)} %get-tuple-element.29.my_weight, bf16[512,1536]{1,0:T(8,128)(2,1)S(1)} %collective-permute-done.4.their_weight), custom_call_target="tpu_custom_call" | custom-call | flops 600000000 | bytes 600000 | tf_op jit(solution)/shard_map/pallas_call | solution.py:21
  27.7 5.7 %collective-permute-done.6.refs_0_ = bf16[400,128]{1,0:T(8,128)(2,1)S(1)} collective-permute-done((bf16[400,128]{1,0:T(8,128)(2,1)S(1)}, bf16[400,128]{1,0:T(8,128)(2,1)S(1)}, u32[]{:S(2)}, u32[]{:S(2)}) %collective-permute-start.6) | collective-permute-done | bytes 102432 | tf_op jit(solution)/shard_map/ppermute | solution.py:291
  33.4 0.2 shard_map.73
  33.6 0.0 collective-permute-done.7.refs_0_
  33.6 0.1 shard_map.75.refs_1_
  33.7 0.4 %collective-permute-done.8.refs_2_ = bf16[256,128]{1,0:T(8,128)(2,1)S(1)} collective-permute-done((bf16[256,128]{1,0:T(8,128)(2,1)S(1)}, bf16[256,128]{1,0:T(8,128)(2,1)S(1)}, u32[]{:S(2)}, u32[]{:S(2)}) %collective-permute-start.8) | collective-permute-done | bytes 65568 | tf_op jit(solution)/shard_map/ppermute | solution.py:291
  34.1 0.8 %shard_map.77 = bf16[128,1536]{1,0:T(8,128)(2,1)} custom-call(f32[128,1536]{1,0:T(8,128)S(1)} %shard_map.70.partial, f32[128,1]{1,0:T(8,128)S(1)} %get-tuple-element.33.scale, bf16[128,384]{1,0:T(8,128)(2,1)S(1)} %get-tuple-element.34.refs_0_, bf16[128,896]{1,0:T(8,128)(2,1)S(1)} %shard_map.75.refs_1_, bf16[256,128]{1,0:T(8,128)(2,1)S(1)} %collective-permute-done.8.refs_2_), custom_call_target="tpu_custom_call" | custom-call | flops 1000000000 | bytes 1000000 | tf_op jit(solution)/shard_map/pallas_call | solution.py:21
Async XLA Ops:
  1.4 6.6 %collective-permute-start = (bf16[528,128]{1,0:T(8,128)(2,1)S(1)}, bf16[528,128]{1,0:T(8,128)(2,1)S(1)}, u32[]{:S(2)}, u32[]{:S(2)}) collective-permute-start(bf16[528,128]{1,0:T(8,128)(2,1)S(1)} %shard_map.64._.refs_0_), channel_id=1, source_target_pairs={{0,4},{4,0},{8,12},{12,8},{16,20},{20,16},{24,28},{28,24},{1,5},{5... | collective-permute-start | bytes 405512 | tf_op jit(solution)/shard_map/ppermute | solution.py:291
  8.1 5.1 %collective-permute-start.1 = (bf16[528,128]{1,0:T(8,128)(2,1)S(1)}, bf16[528,128]{1,0:T(8,128)(2,1)S(1)}, u32[]{:S(2)}, u32[]{:S(2)}) collective-permute-start(bf16[528,128]{1,0:T(8,128)(2,1)S(1)} %get-tuple-element.21._.refs_0_), channel_id=1, source_target_pairs={{0,8},{4,12},{8,0},{12,4},{16,24},{20,28},{24,16},{28,20},{1,9},{5... | collective-permute-start | bytes 405512 | tf_op jit(solution)/shard_map/ppermute | solution.py:291
  9.9 17.2 %collective-permute-start.4 = (bf16[512,1536]{1,0:T(8,128)(2,1)S(1)}, bf16[512,1536]{1,0:T(8,128)(2,1)S(1)}, u32[]{:S(2)}, u32[]{:S(2)}) collective-permute-start(bf16[512,1536]{1,0:T(8,128)(2,1)S(1)} %get-tuple-element.30), channel_id=1, source_target_pairs={{0,1},{1,0},{2,3},{3,2},{4,5},{5,4},{6,7},{7,6},{8,9},{9,8},{10,11... | collective-permute-start | bytes 4718600 | tf_op jit(solution)/shard_map/ppermute | solution.py:291
  9.9 12.5 %collective-permute-start.5 = (bf16[512,1536]{1,0:T(8,128)(2,1)S(1)}, bf16[512,1536]{1,0:T(8,128)(2,1)S(1)}, u32[]{:S(2)}, u32[]{:S(2)}) collective-permute-start(bf16[512,1536]{1,0:T(8,128)(2,1)S(1)} %get-tuple-element.32), channel_id=1, source_target_pairs={{0,1},{1,0},{2,3},{3,2},{4,5},{5,4},{6,7},{7,6},{8,9},{9,8},{10,11... | collective-permute-start | bytes 4718600 | tf_op jit(solution)/shard_map/ppermute | solution.py:291
  13.2 7.4 %copy-start = (bf16[128,512]{1,0:T(8,128)(2,1)S(1)}, bf16[128,512]{1,0:T(8,128)(2,1)}, u32[]{:S(2)}) copy-start(bf16[128,512]{1,0:T(8,128)(2,1)} %query.1) | copy-start | bytes 393220
  13.2 7.4 %copy-start.1 = (f32[512]{0:T(512)S(1)}, f32[512]{0:T(512)}, u32[]{:S(2)}) copy-start(f32[512]{0:T(512)} %param.10) | copy-start | bytes 6148
  13.3 7.3 %collective-permute-start.2 = (bf16[512,128]{1,0:T(8,128)(2,1)S(1)}, bf16[512,128]{1,0:T(8,128)(2,1)S(1)}, u32[]{:S(2)}, u32[]{:S(2)}) collective-permute-start(bf16[512,128]{1,0:T(8,128)(2,1)S(1)} %get-tuple-element.28), channel_id=1, source_target_pairs={{0,16},{4,20},{8,24},{12,28},{16,0},{20,4},{24,8},{28,12},{1,17},{... | collective-permute-start | bytes 393224 | tf_op jit(solution)/shard_map/ppermute | solution.py:291
  21.0 1.5 %collective-permute-start.3 = (bf16[128,640]{1,0:T(8,128)(2,1)S(1)}, bf16[128,640]{1,0:T(8,128)(2,1)S(1)}, u32[]{:S(2)}, u32[]{:S(2)}) collective-permute-start(bf16[128,640]{1,0:T(8,128)(2,1)S(1)} %shard_map.69.mine), channel_id=1, source_target_pairs={{0,1},{1,0},{2,3},{3,2},{4,5},{5,4},{6,7},{7,6},{8,9},{9,8},{10,11... | collective-permute-start | bytes 491528 | tf_op jit(solution)/shard_map/ppermute | solution.py:291
  22.8 10.8 %collective-permute-start.7 = (bf16[896,128]{1,0:T(8,128)(2,1)S(1)}, bf16[896,128]{1,0:T(8,128)(2,1)S(1)}, u32[]{:S(2)}, u32[]{:S(2)}) collective-permute-start(bf16[896,128]{1,0:T(8,128)(2,1)S(1)} %shard_map.74), channel_id=1, source_target_pairs={{0,2},{1,3},{2,0},{3,1},{4,6},{5,7},{6,4},{7,5},{8,10},{9,11},{10,... | collective-permute-start | bytes 688136 | tf_op jit(solution)/shard_map/ppermute | solution.py:291
  24.8 8.6 %collective-permute-start.6 = (bf16[400,128]{1,0:T(8,128)(2,1)S(1)}, bf16[400,128]{1,0:T(8,128)(2,1)S(1)}, u32[]{:S(2)}, u32[]{:S(2)}) collective-permute-start(bf16[400,128]{1,0:T(8,128)(2,1)S(1)} %shard_map.72), channel_id=1, source_target_pairs={{0,2},{1,3},{2,0},{3,1},{4,6},{5,7},{6,4},{7,5},{8,10},{9,11},{10,... | collective-permute-start | bytes 307208 | tf_op jit(solution)/shard_map/ppermute | solution.py:291
  25.3 8.7 %collective-permute-start.8 = (bf16[256,128]{1,0:T(8,128)(2,1)S(1)}, bf16[256,128]{1,0:T(8,128)(2,1)S(1)}, u32[]{:S(2)}, u32[]{:S(2)}) collective-permute-start(bf16[256,128]{1,0:T(8,128)(2,1)S(1)} %shard_map.76), channel_id=1, source_target_pairs={{0,2},{1,3},{2,0},{3,1},{4,6},{5,7},{6,4},{7,5},{8,10},{9,11},{10,... | collective-permute-start | bytes 196616 | tf_op jit(solution)/shard_map/ppermute | solution.py:291

commit v3 on v2

--- a/solution.py
+++ b/solution.py
@@ -89,24 +89,26 @@
     return copies
 
 
-def states_kernel(keys_far, values_far, decay_far, message, keys, values, decay, semaphores):
+def states_kernel(keys_far, values_far, decay_far, message, keys, values, decay, tails, semaphores):
     decay_copy, *copies = fetch((decay_far, keys_far, values_far), (decay, keys, values), semaphores)
     decay_copy.wait()
     heads, tokens = decay.shape
     width = keys.shape[1] // heads
     column = column_sums(decay[...])
+    tail = jnp.exp(column[tokens - 1 : tokens, :] - column)
+    for head in range(heads):
+        tails[:, head * width : (head + 1) * width] = jnp.broadcast_to(tail[:, head : head + 1], (tokens, width))
+    total = jnp.sum(decay[...], axis=1, keepdims=True)
+    message[heads * width :, :] = stacked(jnp.broadcast_to(jnp.exp(total), (heads, LANES)), heads)
     for copy in copies:
         copy.wait()
-    tail = jnp.exp(column[tokens - 1 : tokens, :] - column)
     for head in range(heads):
         own = slice(head * width, (head + 1) * width)
-        faded = (keys[:, own].astype(F32) * tail[:, head : head + 1]).astype(BF16)
+        faded = (keys[:, own].astype(F32) * tails[:, own]).astype(BF16)
         state = lax.dot_general(
             faded, values[:, own], (((0,), (0,)), ((), ())), preferred_element_type=F32
         )
         message[own, :] = state.astype(BF16)
-    total = jnp.sum(decay[...], axis=1, keepdims=True)
-    message[heads * width :, :] = stacked(jnp.broadcast_to(jnp.exp(total), (heads, LANES)), heads)
 
 
 def weights_kernel(far_count, weight_far, _, *refs):
@@ -124,14 +126,16 @@
         copy.wait()
 
 
-def within_kernel(query_far, keys_far, values_far, decay_far, _, within, grown, query, keys, values, decay, semaphores):
+def within_kernel(step, query_far, keys_far, values_far, decay_far, before, before_decay, *refs):
+    within, factor, query, keys, values, decay, semaphores = refs
     for copy in fetch((query_far, keys_far, values_far, decay_far), (query, keys, values, decay), semaphores):
         copy.wait()
     heads, tokens = decay.shape
     width = keys.shape[1] // heads
     column = column_sums(decay[...])
     line = row_sums(decay[...])
-    grown[...] = jnp.exp(column)
+    grown = jnp.exp(column)
+    scale = jnp.where(odd("ctx", step), before_decay[...], 0.0 * before_decay[...])
     row, col = triangle(tokens)
     for head in range(heads):
         own = slice(head * width, (head + 1) * width)
@@ -140,7 +144,10 @@
         )
         differ = jnp.where(row >= col, column[:, head : head + 1] - line[head : head + 1, :], -1e30)
         weights = (jnp.exp(differ) * scores).astype(BF16)
-        within[:, own] = jnp.dot(weights, values[:, own], preferred_element_type=F32)
+        carried = jnp.dot(query[:, own], before[own, :].astype(BF16), preferred_element_type=F32)
+        spread = jnp.broadcast_to(grown[:, head : head + 1], (tokens, width))
+        within[:, own] = jnp.dot(weights, values[:, own], preferred_element_type=F32) + spread * carried
+        factor[:, own] = spread * scale[head : head + 1]
 
 
 def join_kernel(step, heads, *refs):
@@ -174,19 +181,17 @@
         joined[rows:, :] = stacked(my_decay * their_decay, heads)
 
 
-def attend_kernel(step, heads, query, within, grown, before, before_decay, theirs, gain, message):
-    later = odd("ctx", step)
+def attend_kernel(heads, query, within, factor, theirs, gain, message):
     tokens, full = query.shape
     width = full // heads
-    scale = jnp.where(later, before_decay[...], 0.0 * before_decay[...])
-    squares = jnp.zeros((tokens, 1), F32)
+    squares = jnp.zeros((tokens, width), F32)
     for head in range(heads):
         own = slice(head * width, (head + 1) * width)
-        state = before[own, :] + scale[head : head + 1] * theirs[own, :].astype(F32)
-        carried = jnp.dot(query[:, own], state.astype(BF16), preferred_element_type=F32)
-        attn = within[:, own] + grown[:, head : head + 1] * carried
-        squares = squares + jnp.sum(attn * attn, axis=1, keepdims=True)
+        carried = jnp.dot(query[:, own], theirs[own, :], preferred_element_type=F32)
+        attn = within[:, own] + factor[:, own] * carried
+        squares = squares + attn * attn
         message[:, own] = (attn * gain[:, own]).astype(BF16)
+    squares = jnp.sum(squares, axis=1, keepdims=True)
     high, mid, low = split3(squares)
     lane = lax.broadcasted_iota(jnp.int32, (tokens, LANES), 1)
     pieces = jnp.where(lane == 0, high.astype(F32), 0.0)
@@ -204,7 +209,7 @@
     result[...] = jnp.dot(mine[:, :full], weight[...], preferred_element_type=F32)
 
 
-def away_kernel(full, first_block, partial, mine, theirs, their_weight, *refs):
+def away_kernel(full, first_block, leading, partial, mine, theirs, their_weight, *refs):
     *received, message = refs
     tokens = mine.shape[0]
     blocks = message.shape[0] // tokens
@@ -216,7 +221,7 @@
         for other in received:
             part = part + other[there, :].astype(F32)
         message[there, :] = part.astype(BF16)
-    if first_block == 0:
+    if leading:
         total = squares_row(mine, theirs, full)
         for other in received:
             total = total + unstacked(other[blocks * tokens :, :], 1)
@@ -238,22 +243,18 @@
         out[:, block * LANES : (block + 1) * LANES] = (summed * scale).astype(BF16)
 
 
-def first_kernel(full, mine, theirs, partial, *refs):
-    *received, scale, out = refs
-    tokens, columns = out.shape
+def middle_kernel(full, cuts, count, mine, theirs, partial, *refs):
+    received, (scale, *outs) = refs[: len(cuts) * count], refs[len(cuts) * count :]
+    groups = [received[part * count : (part + 1) * count] for part in range(len(cuts))]
     total = squares_row(mine, theirs, full)
-    for other in received:
-        total = total + unstacked(other[columns // LANES * tokens :, :], 1)
-    row, col = triangle(tokens)
+    for other in groups[-1]:
+        total = total + unstacked(other[other.shape[0] - SUBLANES :, :], 1)
+    row, col = triangle(mine.shape[0])
     total = jnp.sum(jnp.where(row == col, total, 0.0), axis=1, keepdims=True)
     factor = lax.rsqrt(total / (full * lax.axis_size("head")) + 1e-05)
     scale[...] = factor
-    scaled(partial, 0, received, factor, out)
-
-
-def middle_kernel(first_block, partial, scale, *refs):
-    *received, out = refs
-    scaled(partial, first_block, received, scale[...], out)
+    for first_block, group, out in zip(cuts, groups, outs):
+        scaled(partial, first_block, group, factor, out)
 
 
 def last_kernel(first_block, done_count, partial, scale, *refs):
@@ -296,7 +297,7 @@
         [message_shape],
         (keys, values, decay),
         far=3,
-        scratch=[*blocks[1:], dma((3,))],
+        scratch=[*blocks[1:], pltpu.VMEM((tokens, full), F32), dma((3,))],
     )
     theirs = swap(message, "ctx", 1)
 
@@ -328,19 +329,18 @@
             cost=30.0 if step == steps - 2 else 0.1,
         )
         theirs = swap(message, "ctx", 2 << step)
-        if step == 0:
-            within, grown = call(
-                within_kernel,
-                [shape((tokens, full), F32), shape((tokens, heads), F32)],
-                (query, keys, values, decay, message),
-                far=4,
-                scratch=[*blocks, dma((4,))],
-                cost=1.0,
-            )
+    within, factor = call(
+        functools.partial(within_kernel, steps - 1),
+        [shape((tokens, full), F32)] * 2,
+        (query, keys, values, decay, *entering),
+        far=4,
+        scratch=[*blocks, dma((4,))],
+        cost=1.0,
+    )
     (mine,) = call(
-        functools.partial(attend_kernel, steps - 1, heads),
+        functools.partial(attend_kernel, heads),
         [shape((tokens, full + LANES), BF16)],
-        (query, within, grown, *entering, theirs, norm_gain[None, :]),
+        (query, within, factor, theirs, norm_gain[None, :]),
     )
     mate = swap(mine, "head", 1)
     ahead = {}
@@ -360,8 +360,8 @@
         for far in range(reach, 2 * reach):
             for part, (first, end) in enumerate(zip(cuts[:-1], cuts[1:])):
                 (away,) = call(
-                    functools.partial(away_kernel, full, first),
-                    [shape(((end - first) * tokens + (SUBLANES if first == 0 else 0), LANES), BF16)],
+                    functools.partial(away_kernel, full, first, part == PARTS - 2),
+                    [shape(((end - first) * tokens + SUBLANES * (part == PARTS - 2), LANES), BF16)],
                     (ahead[far], mine, mate, their_weights[far], *received[far][part]),
                     cost=0.2,
                 )
@@ -374,20 +374,12 @@
         cost=0.6,
     )
     widths = [(end - first) * LANES for first, end in zip(cuts[:-1], cuts[1:])]
-    scale, part_done = call(
-        functools.partial(first_kernel, full),
-        [shape((tokens, 1), F32), shape((tokens, widths[0]), BF16)],
-        (mine, mate, partial, *received[0][0]),
+    scale, *done = call(
+        functools.partial(middle_kernel, full, cuts[: PARTS - 1], len(received[0][0])),
+        [shape((tokens, 1), F32)] + [shape((tokens, width), BF16) for width in widths[:-1]],
+        (mine, mate, partial, *(other for group in received[0][:-1] for other in group)),
         cost=0.3,
     )
-    done = [part_done]
-    for part in range(1, PARTS - 1):
-        done += call(
-            functools.partial(middle_kernel, cuts[part]),
-            [shape((tokens, widths[part]), BF16)],
-            (partial, scale, *received[0][part]),
-            cost=0.2,
-        )
     (mixed,) = call(
         functools.partial(last_kernel, cuts[PARTS - 1], len(done)),
         [shape((tokens, columns), BF16)],

time: 35 us -> 34.9 us (level)
  Pallas kernels: 9.5 us -> 8.99 us
  waiting for transfers between devices: 12.9 us -> 13.3 us
    pallas_call x14 -> x13, Pallas kernels: 9.5 us -> 8.99 us  [call(): pl.pallas_call(body, out_shape=outs, in_specs=[FAR] * far + [VMEM] * (len...]
    ppermute x9, waiting for transfers between devices: 12.9 us -> 13.3 us  [swap(): return lax.ppermute(value, axis, [(i, i ^ bit) for i in range(count)])]
  transfers between devices with their start and end apart: 9 -> 9, of which waited for: 6 -> 6; matrix products, arithmetic and copies ran while one was open for 0% -> 0% of each run, Pallas kernels for 21% -> 20%
where the time goes in v3:
time: 34.9 us; the launch traced here: 34.7 us
  waiting for transfers between devices  13.3 us (38%)
  starting transfers between devices  12.3 us (35%)
  Pallas kernels  8.99 us (26%)
    ppermute x9, waiting for transfers between devices, swap(): return lax.ppermute(value, axis, [(i, i ^ bit) for i in range(count)])  13.3 us
    ppermute x9, starting transfers between devices, swap(): return lax.ppermute(value, axis, [(i, i ^ bit) for i in range(count)])  12.3 us
    pallas_call x13, Pallas kernels, call(): pl.pallas_call(body, out_shape=outs, in_specs=[FAR] * far + [VMEM] * (len...  8.99 us
  transfers between devices with their start and end apart: 9, of which 6 were waited for; matrix products, arithmetic and copies ran while one was open for 0% of the time, Pallas kernels for 20%

profile of v3, /device:TPU:0, one launch (start us, length us, event | category | flops | bytes accessed | tf_op | source)
XLA Modules:
  0.0 34.7 jit_solution(13077562463465400630)
XLA Ops:
  0.0 1.3 %shard_map.64._.refs_0_ = bf16[528,128]{1,0:T(8,128)(2,1)S(1)} custom-call(bf16[128,512]{1,0:T(8,128)(2,1)} %keys_far.3, bf16[128,512]{1,0:T(8,128)(2,1)} %values_far.3, f32[4,128]{1,0:T(4,128)} %bitcast.3), custom_call_target="tpu_custom_call" | custom-call | flops 1000000000 | bytes 1000000 | tf_op jit(solution)/shard_map/pallas_call | solution.py:21
  1.3 3.0 %collective-permute-start = (bf16[528,128]{1,0:T(8,128)(2,1)S(1)}, bf16[528,128]{1,0:T(8,128)(2,1)S(1)}, u32[]{:S(2)}, u32[]{:S(2)}) collective-permute-start(bf16[528,128]{1,0:T(8,128)(2,1)S(1)} %shard_map.64._.refs_0_), channel_id=1, source_target_pairs={{0,4},{4,0},{8,12},{12,8},{16,20},{20,16},{24,28},{28,24},{1,5},{5... | collective-permute-start | bytes 405512 | tf_op jit(solution)/shard_map/ppermute | solution.py:292
  4.4 2.9 %shard_map.65 = (bf16[512,1536]{1,0:T(8,128)(2,1)S(1)}, bf16[512,1536]{1,0:T(8,128)(2,1)S(1)}, bf16[512,1536]{1,0:T(8,128)(2,1)S(1)}, bf16[512,1536]{1,0:T(8,128)(2,1)S(1)}, f32[8,128]{1,0:T(8,128)S(1)}) custom-call(bf16[512,6144]{1,0:T(8,128)(2,1)} %weight_far.1, bf16[528,128]{1,0:T(8,128)(2,1)S(1)} %shard_map.64._.refs_0_), custom_call_target="tpu_custom_call" | custom-call | flops 2000000000 | bytes 2000000 | tf_op jit(solution)/shard_map/pallas_call | solution.py:21
  7.2 0.7 %collective-permute-done.refs_1_ = bf16[528,128]{1,0:T(8,128)(2,1)S(1)} collective-permute-done((bf16[528,128]{1,0:T(8,128)(2,1)S(1)}, bf16[528,128]{1,0:T(8,128)(2,1)S(1)}, u32[]{:S(2)}, u32[]{:S(2)}) %collective-permute-start) | collective-permute-done | bytes 135200 | tf_op jit(solution)/shard_map/ppermute | solution.py:292
  7.9 0.1 shard_map.66
  8.0 1.9 %collective-permute-start.1 = (bf16[528,128]{1,0:T(8,128)(2,1)S(1)}, bf16[528,128]{1,0:T(8,128)(2,1)S(1)}, u32[]{:S(2)}, u32[]{:S(2)}) collective-permute-start(bf16[528,128]{1,0:T(8,128)(2,1)S(1)} %get-tuple-element.22.refs_0_), channel_id=1, source_target_pairs={{0,8},{4,12},{8,0},{12,4},{16,24},{20,28},{24,16},{28,20},{1,9},{5... | collective-permute-start | bytes 405512 | tf_op jit(solution)/shard_map/ppermute | solution.py:292
  9.9 0.0 collective-permute-start.4
  9.9 0.5 %collective-permute-start.5 = (bf16[512,1536]{1,0:T(8,128)(2,1)S(1)}, bf16[512,1536]{1,0:T(8,128)(2,1)S(1)}, u32[]{:S(2)}, u32[]{:S(2)}) collective-permute-start(bf16[512,1536]{1,0:T(8,128)(2,1)S(1)} %get-tuple-element.33), channel_id=1, source_target_pairs={{0,1},{1,0},{2,3},{3,2},{4,5},{5,4},{6,7},{7,6},{8,9},{9,8},{10,11... | collective-permute-start | bytes 4718600 | tf_op jit(solution)/shard_map/ppermute | solution.py:292
  10.4 2.7 %collective-permute-done.1.refs_1_ = bf16[528,128]{1,0:T(8,128)(2,1)S(1)} collective-permute-done((bf16[528,128]{1,0:T(8,128)(2,1)S(1)}, bf16[528,128]{1,0:T(8,128)(2,1)S(1)}, u32[]{:S(2)}, u32[]{:S(2)}) %collective-permute-start.1) | collective-permute-done | bytes 135200 | tf_op jit(solution)/shard_map/ppermute | solution.py:292
  13.1 0.1 shard_map.67
  13.2 2.9 %collective-permute-start.2 = (bf16[512,128]{1,0:T(8,128)(2,1)S(1)}, bf16[512,128]{1,0:T(8,128)(2,1)S(1)}, u32[]{:S(2)}, u32[]{:S(2)}) collective-permute-start(bf16[512,128]{1,0:T(8,128)(2,1)S(1)} %get-tuple-element.29), channel_id=1, source_target_pairs={{0,16},{4,20},{8,24},{12,28},{16,0},{20,4},{24,8},{28,12},{1,17},{... | collective-permute-start | bytes 393224 | tf_op jit(solution)/shard_map/ppermute | solution.py:292
  16.1 0.0 copy-start
  16.1 0.0 copy-start.1
  16.1 1.6 %shard_map.68 = (f32[128,512]{1,0:T(8,128)S(1)}, f32[128,512]{1,0:T(8,128)S(1)}) custom-call(bf16[128,512]{1,0:T(8,128)(2,1)} %query.1, bf16[128,512]{1,0:T(8,128)(2,1)} %keys_far.3, bf16[128,512]{1,0:T(8,128)(2,1)} %values_far.3, f32[4,128]{1,0:T(4,128)} %bitcast.4, f32[512,128]{1,0:T(8,128)S(1)} %get-tuple-element.25.before, ...), custom_call_target="tpu_custom_call" | custom-call | flops 1000000000 | bytes 1000000 | tf_op jit(solution)/shard_map/pallas_call | solution.py:21
  17.7 2.8 %collective-permute-done.2.theirs = bf16[512,128]{1,0:T(8,128)(2,1)S(1)} collective-permute-done((bf16[512,128]{1,0:T(8,128)(2,1)S(1)}, bf16[512,128]{1,0:T(8,128)(2,1)S(1)}, u32[]{:S(2)}, u32[]{:S(2)}) %collective-permute-start.2) | collective-permute-done | bytes 131104 | tf_op jit(solution)/shard_map/ppermute | solution.py:292
  20.5 0.0 copy-done
  20.5 0.0 copy-done.1
  20.6 0.3 shard_map.69.mine
  20.8 0.1 collective-permute-start.3
  20.9 0.4 %shard_map.71.partial = f32[128,1536]{1,0:T(8,128)S(1)} custom-call(bf16[128,640]{1,0:T(8,128)(2,1)S(1)} %shard_map.69.mine, bf16[512,1536]{1,0:T(8,128)(2,1)S(1)} %get-tuple-element.32.weight), custom_call_target="tpu_custom_call" | custom-call | flops 400000000 | bytes 400000 | tf_op jit(solution)/shard_map/pallas_call | solution.py:21
  21.3 1.0 %collective-permute-done.3.theirs = bf16[128,640]{1,0:T(8,128)(2,1)S(1)} collective-permute-done((bf16[128,640]{1,0:T(8,128)(2,1)S(1)}, bf16[128,640]{1,0:T(8,128)(2,1)S(1)}, u32[]{:S(2)}, u32[]{:S(2)}) %collective-permute-start.3) | collective-permute-done | bytes 163872 | tf_op jit(solution)/shard_map/ppermute | solution.py:292
  22.3 0.0 collective-permute-done.5.their_weight
  22.3 0.3 shard_map.73
  22.6 1.8 %collective-permute-start.7 = (bf16[912,128]{1,0:T(8,128)(2,1)S(1)}, bf16[912,128]{1,0:T(8,128)(2,1)S(1)}, u32[]{:S(2)}, u32[]{:S(2)}) collective-permute-start(bf16[912,128]{1,0:T(8,128)(2,1)S(1)} %shard_map.73), channel_id=1, source_target_pairs={{0,2},{1,3},{2,0},{3,1},{4,6},{5,7},{6,4},{7,5},{8,10},{9,11},{10,... | collective-permute-start | bytes 700424 | tf_op jit(solution)/shard_map/ppermute | solution.py:292
  24.4 0.2 shard_map.72
  24.6 0.4 %collective-permute-start.6 = (bf16[384,128]{1,0:T(8,128)(2,1)S(1)}, bf16[384,128]{1,0:T(8,128)(2,1)S(1)}, u32[]{:S(2)}, u32[]{:S(2)}) collective-permute-start(bf16[384,128]{1,0:T(8,128)(2,1)S(1)} %shard_map.72), channel_id=1, source_target_pairs={{0,2},{1,3},{2,0},{3,1},{4,6},{5,7},{6,4},{7,5},{8,10},{9,11},{10,... | collective-permute-start | bytes 294920 | tf_op jit(solution)/shard_map/ppermute | solution.py:292
  25.0 0.2 shard_map.75
  25.2 1.8 %collective-permute-start.8 = (bf16[256,128]{1,0:T(8,128)(2,1)S(1)}, bf16[256,128]{1,0:T(8,128)(2,1)S(1)}, u32[]{:S(2)}, u32[]{:S(2)}) collective-permute-start(bf16[256,128]{1,0:T(8,128)(2,1)S(1)} %shard_map.75), channel_id=1, source_target_pairs={{0,2},{1,3},{2,0},{3,1},{4,6},{5,7},{6,4},{7,5},{8,10},{9,11},{10,... | collective-permute-start | bytes 196616 | tf_op jit(solution)/shard_map/ppermute | solution.py:292
  27.0 0.0 collective-permute-done.4.their_weight
  27.0 0.6 %shard_map.70.partial = f32[128,1536]{1,0:T(8,128)S(1)} custom-call(bf16[128,640]{1,0:T(8,128)(2,1)S(1)} %shard_map.69.mine, bf16[128,640]{1,0:T(8,128)(2,1)S(1)} %collective-permute-done.3.theirs, bf16[512,1536]{1,0:T(8,128)(2,1)S(1)} %get-tuple-element.30.my_weight, bf16[512,1536]{1,0:T(8,128)(2,1)S(1)} %collective-permute-done.4.their_weight), custom_call_target="tpu_custom_call" | custom-call | flops 600000000 | bytes 600000 | tf_op jit(solution)/shard_map/pallas_call | solution.py:21
  27.6 5.7 %collective-permute-done.6.refs_0_ = bf16[384,128]{1,0:T(8,128)(2,1)S(1)} collective-permute-done((bf16[384,128]{1,0:T(8,128)(2,1)S(1)}, bf16[384,128]{1,0:T(8,128)(2,1)S(1)}, u32[]{:S(2)}, u32[]{:S(2)}) %collective-permute-start.6) | collective-permute-done | bytes 98336 | tf_op jit(solution)/shard_map/ppermute | solution.py:292
  33.2 0.0 collective-permute-done.7.refs_1_
  33.2 0.2 shard_map.74
  33.5 0.4 %collective-permute-done.8.refs_2_ = bf16[256,128]{1,0:T(8,128)(2,1)S(1)} collective-permute-done((bf16[256,128]{1,0:T(8,128)(2,1)S(1)}, bf16[256,128]{1,0:T(8,128)(2,1)S(1)}, u32[]{:S(2)}, u32[]{:S(2)}) %collective-permute-start.8) | collective-permute-done | bytes 65568 | tf_op jit(solution)/shard_map/ppermute | solution.py:292
  33.9 0.8 %shard_map.76 = bf16[128,1536]{1,0:T(8,128)(2,1)} custom-call(f32[128,1536]{1,0:T(8,128)S(1)} %shard_map.70.partial, f32[128,1]{1,0:T(8,128)S(1)} %get-tuple-element.34.scale, bf16[128,384]{1,0:T(8,128)(2,1)S(1)} %get-tuple-element.35.refs_0_, bf16[128,896]{1,0:T(8,128)(2,1)S(1)} %get-tuple-element.36.refs_1_, ...), custom_call_target="tpu_custom_call" | custom-call | flops 1000000000 | bytes 1000000 | tf_op jit(solution)/shard_map/pallas_call | solution.py:21
Async XLA Ops:
  1.3 6.6 %collective-permute-start = (bf16[528,128]{1,0:T(8,128)(2,1)S(1)}, bf16[528,128]{1,0:T(8,128)(2,1)S(1)}, u32[]{:S(2)}, u32[]{:S(2)}) collective-permute-start(bf16[528,128]{1,0:T(8,128)(2,1)S(1)} %shard_map.64._.refs_0_), channel_id=1, source_target_pairs={{0,4},{4,0},{8,12},{12,8},{16,20},{20,16},{24,28},{28,24},{1,5},{5... | collective-permute-start | bytes 405512 | tf_op jit(solution)/shard_map/ppermute | solution.py:292
  8.0 5.1 %collective-permute-start.1 = (bf16[528,128]{1,0:T(8,128)(2,1)S(1)}, bf16[528,128]{1,0:T(8,128)(2,1)S(1)}, u32[]{:S(2)}, u32[]{:S(2)}) collective-permute-start(bf16[528,128]{1,0:T(8,128)(2,1)S(1)} %get-tuple-element.22.refs_0_), channel_id=1, source_target_pairs={{0,8},{4,12},{8,0},{12,4},{16,24},{20,28},{24,16},{28,20},{1,9},{5... | collective-permute-start | bytes 405512 | tf_op jit(solution)/shard_map/ppermute | solution.py:292
  9.9 17.1 %collective-permute-start.4 = (bf16[512,1536]{1,0:T(8,128)(2,1)S(1)}, bf16[512,1536]{1,0:T(8,128)(2,1)S(1)}, u32[]{:S(2)}, u32[]{:S(2)}) collective-permute-start(bf16[512,1536]{1,0:T(8,128)(2,1)S(1)} %get-tuple-element.31), channel_id=1, source_target_pairs={{0,1},{1,0},{2,3},{3,2},{4,5},{5,4},{6,7},{7,6},{8,9},{9,8},{10,11... | collective-permute-start | bytes 4718600 | tf_op jit(solution)/shard_map/ppermute | solution.py:292
  9.9 12.4 %collective-permute-start.5 = (bf16[512,1536]{1,0:T(8,128)(2,1)S(1)}, bf16[512,1536]{1,0:T(8,128)(2,1)S(1)}, u32[]{:S(2)}, u32[]{:S(2)}) collective-permute-start(bf16[512,1536]{1,0:T(8,128)(2,1)S(1)} %get-tuple-element.33), channel_id=1, source_target_pairs={{0,1},{1,0},{2,3},{3,2},{4,5},{5,4},{6,7},{7,6},{8,9},{9,8},{10,11... | collective-permute-start | bytes 4718600 | tf_op jit(solution)/shard_map/ppermute | solution.py:292
  13.2 7.3 %collective-permute-start.2 = (bf16[512,128]{1,0:T(8,128)(2,1)S(1)}, bf16[512,128]{1,0:T(8,128)(2,1)S(1)}, u32[]{:S(2)}, u32[]{:S(2)}) collective-permute-start(bf16[512,128]{1,0:T(8,128)(2,1)S(1)} %get-tuple-element.29), channel_id=1, source_target_pairs={{0,16},{4,20},{8,24},{12,28},{16,0},{20,4},{24,8},{28,12},{1,17},{... | collective-permute-start | bytes 393224 | tf_op jit(solution)/shard_map/ppermute | solution.py:292
  16.1 4.5 %copy-start = (bf16[128,512]{1,0:T(8,128)(2,1)S(1)}, bf16[128,512]{1,0:T(8,128)(2,1)}, u32[]{:S(2)}) copy-start(bf16[128,512]{1,0:T(8,128)(2,1)} %query.1) | copy-start | bytes 393220
  16.1 4.5 %copy-start.1 = (f32[512]{0:T(512)S(1)}, f32[512]{0:T(512)}, u32[]{:S(2)}) copy-start(f32[512]{0:T(512)} %param.10) | copy-start | bytes 6148
  20.8 1.5 %collective-permute-start.3 = (bf16[128,640]{1,0:T(8,128)(2,1)S(1)}, bf16[128,640]{1,0:T(8,128)(2,1)S(1)}, u32[]{:S(2)}, u32[]{:S(2)}) collective-permute-start(bf16[128,640]{1,0:T(8,128)(2,1)S(1)} %shard_map.69.mine), channel_id=1, source_target_pairs={{0,1},{1,0},{2,3},{3,2},{4,5},{5,4},{6,7},{7,6},{8,9},{9,8},{10,11... | collective-permute-start | bytes 491528 | tf_op jit(solution)/shard_map/ppermute | solution.py:292
  22.6 10.6 %collective-permute-start.7 = (bf16[912,128]{1,0:T(8,128)(2,1)S(1)}, bf16[912,128]{1,0:T(8,128)(2,1)S(1)}, u32[]{:S(2)}, u32[]{:S(2)}) collective-permute-start(bf16[912,128]{1,0:T(8,128)(2,1)S(1)} %shard_map.73), channel_id=1, source_target_pairs={{0,2},{1,3},{2,0},{3,1},{4,6},{5,7},{6,4},{7,5},{8,10},{9,11},{10,... | collective-permute-start | bytes 700424 | tf_op jit(solution)/shard_map/ppermute | solution.py:292
  24.6 8.6 %collective-permute-start.6 = (bf16[384,128]{1,0:T(8,128)(2,1)S(1)}, bf16[384,128]{1,0:T(8,128)(2,1)S(1)}, u32[]{:S(2)}, u32[]{:S(2)}) collective-permute-start(bf16[384,128]{1,0:T(8,128)(2,1)S(1)} %shard_map.72), channel_id=1, source_target_pairs={{0,2},{1,3},{2,0},{3,1},{4,6},{5,7},{6,4},{7,5},{8,10},{9,11},{10,... | collective-permute-start | bytes 294920 | tf_op jit(solution)/shard_map/ppermute | solution.py:292
  25.2 8.7 %collective-permute-start.8 = (bf16[256,128]{1,0:T(8,128)(2,1)S(1)}, bf16[256,128]{1,0:T(8,128)(2,1)S(1)}, u32[]{:S(2)}, u32[]{:S(2)}) collective-permute-start(bf16[256,128]{1,0:T(8,128)(2,1)S(1)} %shard_map.75), channel_id=1, source_target_pairs={{0,2},{1,3},{2,0},{3,1},{4,6},{5,7},{6,4},{7,5},{8,10},{9,11},{10,... | collective-permute-start | bytes 196616 | tf_op jit(solution)/shard_map/ppermute | solution.py:292

commit v4 on v3

--- a/solution.py
+++ b/solution.py
@@ -111,19 +111,29 @@
         message[own, :] = state.astype(BF16)
 
 
-def weights_kernel(far_count, weight_far, _, *refs):
+def weights_kernel(far_count, split, weight_far, _, *refs):
     *weights, token, semaphores = refs
     columns = weights[0].shape[1]
     me = lax.axis_index("head")
     copies = []
-    for index in range(2 * far_count):
-        owner = me ^ ((far_count - 1 - index // 2) << 1) ^ (1 - index % 2)
-        source = weight_far.at[:, pl.ds(pl.multiple_of(owner * columns, LANES), columns)]
-        copies.append(pltpu.make_async_copy(source, weights[index], semaphores.at[index]))
+
+    def copy(owner, first, end, target):
+        start = pl.multiple_of(owner * columns + first, LANES)
+        source = weight_far.at[:, pl.ds(start, end - first)]
+        copies.append(pltpu.make_async_copy(source, target.at[:, first:end], semaphores.at[len(copies)]))
         copies[-1].start()
+
+    for index, target in enumerate(weights):
+        far = far_count - 1 - index // 2
+        owner = me ^ (far << 1) ^ (1 - index % 2)
+        if far % 2:
+            copy(owner, 0, split, target)
+            copy(owner ^ 1, split, columns, target)
+        else:
+            copy(owner, 0, columns, target)
     token[...] = jnp.zeros_like(token)
-    for copy in copies:
-        copy.wait()
+    for one in copies:
+        one.wait()
 
 
 def within_kernel(step, query_far, keys_far, values_far, decay_far, before, before_decay, *refs):
@@ -302,12 +312,14 @@
     theirs = swap(message, "ctx", 1)
 
     far_count = groups // 2
+    blocks_out = columns // LANES
+    cuts = [0, blocks_out // 4, blocks_out - blocks_out // 4, blocks_out]
     *weights, token = call(
-        functools.partial(weights_kernel, far_count),
+        functools.partial(weights_kernel, far_count, cuts[-2] * LANES),
         [shape((full, columns), BF16)] * (2 * far_count) + [shape((8, LANES), F32)],
         (out_weight, message),
         far=1,
-        scratch=[dma((2 * far_count,))],
+        scratch=[dma((3 * far_count,))],
         cost=2.0,
     )
     my_weights, their_weights = {}, {}
@@ -352,8 +364,6 @@
             cost=0.4,
         )
 
-    blocks_out = columns // LANES
-    cuts = [0, blocks_out // 4, blocks_out - blocks_out // 6, blocks_out]
     received = [[[] for _ in range(PARTS)] for _ in range(far_count)]
     reach = far_count // 2
     while reach:
@@ -365,7 +375,8 @@
                     (ahead[far], mine, mate, their_weights[far], *received[far][part]),
                     cost=0.2,
                 )
-                received[far - reach][part].append(swap(away, "head", reach << 1))
+                hop = 3 if reach == 1 and part == PARTS - 1 else reach << 1
+                received[far - reach][part].append(swap(away, "head", hop))
         reach //= 2
     (partial,) = call(
         functools.partial(home_kernel, full),

time: 34.9 us -> 34.2 us (0.980)
  starting transfers between devices: 12.3 us -> 11.5 us
    ppermute x9, starting transfers between devices: 12.3 us -> 11.5 us  [swap(): return lax.ppermute(value, axis, [(i, i ^ bit) for i in range(count)])]
where the time goes in v4:
time: 34.2 us; the launch traced here: 33.9 us
  waiting for transfers between devices  13.3 us (39%)
  starting transfers between devices  11.5 us (34%)
  Pallas kernels  9 us (26%)
    ppermute x9, waiting for transfers between devices, swap(): return lax.ppermute(value, axis, [(i, i ^ bit) for i in range(count)])  13.3 us
    ppermute x9, starting transfers between devices, swap(): return lax.ppermute(value, axis, [(i, i ^ bit) for i in range(count)])  11.5 us
    pallas_call x13, Pallas kernels, call(): pl.pallas_call(body, out_shape=outs, in_specs=[FAR] * far + [VMEM] * (len...  9 us
  transfers between devices with their start and end apart: 9, of which 6 were waited for; matrix products, arithmetic and copies ran while one was open for 0% of the time, Pallas kernels for 20%

profile of v4, /device:TPU:0, one launch (start us, length us, event | category | flops | bytes accessed | tf_op | source)
XLA Modules:
  0.0 33.9 jit_solution(3021265255647082266)
XLA Ops:
  0.0 1.3 %shard_map.64._.refs_0_ = bf16[528,128]{1,0:T(8,128)(2,1)S(1)} custom-call(bf16[128,512]{1,0:T(8,128)(2,1)} %keys_far.3, bf16[128,512]{1,0:T(8,128)(2,1)} %values_far.3, f32[4,128]{1,0:T(4,128)} %bitcast.3), custom_call_target="tpu_custom_call" | custom-call | flops 1000000000 | bytes 1000000 | tf_op jit(solution)/shard_map/pallas_call | solution.py:21
  1.3 3.0 %collective-permute-start = (bf16[528,128]{1,0:T(8,128)(2,1)S(1)}, bf16[528,128]{1,0:T(8,128)(2,1)S(1)}, u32[]{:S(2)}, u32[]{:S(2)}) collective-permute-start(bf16[528,128]{1,0:T(8,128)(2,1)S(1)} %shard_map.64._.refs_0_), channel_id=1, source_target_pairs={{0,4},{4,0},{8,12},{12,8},{16,20},{20,16},{24,28},{28,24},{1,5},{5... | collective-permute-start | bytes 405512 | tf_op jit(solution)/shard_map/ppermute | solution.py:302
  4.4 2.9 %shard_map.65 = (bf16[512,1536]{1,0:T(8,128)(2,1)S(1)}, bf16[512,1536]{1,0:T(8,128)(2,1)S(1)}, bf16[512,1536]{1,0:T(8,128)(2,1)S(1)}, bf16[512,1536]{1,0:T(8,128)(2,1)S(1)}, f32[8,128]{1,0:T(8,128)S(1)}) custom-call(bf16[512,6144]{1,0:T(8,128)(2,1)} %weight_far.1, bf16[528,128]{1,0:T(8,128)(2,1)S(1)} %shard_map.64._.refs_0_), custom_call_target="tpu_custom_call" | custom-call | flops 2000000000 | bytes 2000000 | tf_op jit(solution)/shard_map/pallas_call | solution.py:21
  7.3 0.7 %collective-permute-done.refs_1_ = bf16[528,128]{1,0:T(8,128)(2,1)S(1)} collective-permute-done((bf16[528,128]{1,0:T(8,128)(2,1)S(1)}, bf16[528,128]{1,0:T(8,128)(2,1)S(1)}, u32[]{:S(2)}, u32[]{:S(2)}) %collective-permute-start) | collective-permute-done | bytes 135200 | tf_op jit(solution)/shard_map/ppermute | solution.py:302
  7.9 0.1 shard_map.66
  8.0 1.9 %collective-permute-start.1 = (bf16[528,128]{1,0:T(8,128)(2,1)S(1)}, bf16[528,128]{1,0:T(8,128)(2,1)S(1)}, u32[]{:S(2)}, u32[]{:S(2)}) collective-permute-start(bf16[528,128]{1,0:T(8,128)(2,1)S(1)} %get-tuple-element.22.refs_0_), channel_id=1, source_target_pairs={{0,8},{4,12},{8,0},{12,4},{16,24},{20,28},{24,16},{28,20},{1,9},{5... | collective-permute-start | bytes 405512 | tf_op jit(solution)/shard_map/ppermute | solution.py:302
  9.9 0.0 collective-permute-start.4
  9.9 0.5 %collective-permute-start.5 = (bf16[512,1536]{1,0:T(8,128)(2,1)S(1)}, bf16[512,1536]{1,0:T(8,128)(2,1)S(1)}, u32[]{:S(2)}, u32[]{:S(2)}) collective-permute-start(bf16[512,1536]{1,0:T(8,128)(2,1)S(1)} %get-tuple-element.33), channel_id=1, source_target_pairs={{0,1},{1,0},{2,3},{3,2},{4,5},{5,4},{6,7},{7,6},{8,9},{9,8},{10,11... | collective-permute-start | bytes 4718600 | tf_op jit(solution)/shard_map/ppermute | solution.py:302
  10.4 2.7 %collective-permute-done.1.refs_1_ = bf16[528,128]{1,0:T(8,128)(2,1)S(1)} collective-permute-done((bf16[528,128]{1,0:T(8,128)(2,1)S(1)}, bf16[528,128]{1,0:T(8,128)(2,1)S(1)}, u32[]{:S(2)}, u32[]{:S(2)}) %collective-permute-start.1) | collective-permute-done | bytes 135200 | tf_op jit(solution)/shard_map/ppermute | solution.py:302
  13.1 0.1 shard_map.67
  13.2 2.9 %collective-permute-start.2 = (bf16[512,128]{1,0:T(8,128)(2,1)S(1)}, bf16[512,128]{1,0:T(8,128)(2,1)S(1)}, u32[]{:S(2)}, u32[]{:S(2)}) collective-permute-start(bf16[512,128]{1,0:T(8,128)(2,1)S(1)} %get-tuple-element.29), channel_id=1, source_target_pairs={{0,16},{4,20},{8,24},{12,28},{16,0},{20,4},{24,8},{28,12},{1,17},{... | collective-permute-start | bytes 393224 | tf_op jit(solution)/shard_map/ppermute | solution.py:302
  16.1 0.0 copy-start
  16.1 0.0 copy-start.1
  16.1 1.6 %shard_map.68 = (f32[128,512]{1,0:T(8,128)S(1)}, f32[128,512]{1,0:T(8,128)S(1)}) custom-call(bf16[128,512]{1,0:T(8,128)(2,1)} %query.1, bf16[128,512]{1,0:T(8,128)(2,1)} %keys_far.3, bf16[128,512]{1,0:T(8,128)(2,1)} %values_far.3, f32[4,128]{1,0:T(4,128)} %bitcast.4, f32[512,128]{1,0:T(8,128)S(1)} %get-tuple-element.25.before, ...), custom_call_target="tpu_custom_call" | custom-call | flops 1000000000 | bytes 1000000 | tf_op jit(solution)/shard_map/pallas_call | solution.py:21
  17.7 2.8 %collective-permute-done.2.theirs = bf16[512,128]{1,0:T(8,128)(2,1)S(1)} collective-permute-done((bf16[512,128]{1,0:T(8,128)(2,1)S(1)}, bf16[512,128]{1,0:T(8,128)(2,1)S(1)}, u32[]{:S(2)}, u32[]{:S(2)}) %collective-permute-start.2) | collective-permute-done | bytes 131104 | tf_op jit(solution)/shard_map/ppermute | solution.py:302
  20.5 0.0 copy-done
  20.5 0.0 copy-done.1
  20.6 0.3 shard_map.69.mine
  20.8 0.1 collective-permute-start.3
  20.9 0.4 %shard_map.71.partial = f32[128,1536]{1,0:T(8,128)S(1)} custom-call(bf16[128,640]{1,0:T(8,128)(2,1)S(1)} %shard_map.69.mine, bf16[512,1536]{1,0:T(8,128)(2,1)S(1)} %get-tuple-element.32.weight), custom_call_target="tpu_custom_call" | custom-call | flops 400000000 | bytes 400000 | tf_op jit(solution)/shard_map/pallas_call | solution.py:21
  21.3 1.0 %collective-permute-done.3.theirs = bf16[128,640]{1,0:T(8,128)(2,1)S(1)} collective-permute-done((bf16[128,640]{1,0:T(8,128)(2,1)S(1)}, bf16[128,640]{1,0:T(8,128)(2,1)S(1)}, u32[]{:S(2)}, u32[]{:S(2)}) %collective-permute-start.3) | collective-permute-done | bytes 163872 | tf_op jit(solution)/shard_map/ppermute | solution.py:302
  22.3 0.0 collective-permute-done.5.their_weight
  22.3 0.3 shard_map.73
  22.6 1.8 %collective-permute-start.7 = (bf16[784,128]{1,0:T(8,128)(2,1)S(1)}, bf16[784,128]{1,0:T(8,128)(2,1)S(1)}, u32[]{:S(2)}, u32[]{:S(2)}) collective-permute-start(bf16[784,128]{1,0:T(8,128)(2,1)S(1)} %shard_map.73), channel_id=1, source_target_pairs={{0,2},{1,3},{2,0},{3,1},{4,6},{5,7},{6,4},{7,5},{8,10},{9,11},{10,... | collective-permute-start | bytes 602120 | tf_op jit(solution)/shard_map/ppermute | solution.py:302
  24.4 0.2 shard_map.72
  24.6 0.4 %collective-permute-start.6 = (bf16[384,128]{1,0:T(8,128)(2,1)S(1)}, bf16[384,128]{1,0:T(8,128)(2,1)S(1)}, u32[]{:S(2)}, u32[]{:S(2)}) collective-permute-start(bf16[384,128]{1,0:T(8,128)(2,1)S(1)} %shard_map.72), channel_id=1, source_target_pairs={{0,2},{1,3},{2,0},{3,1},{4,6},{5,7},{6,4},{7,5},{8,10},{9,11},{10,... | collective-permute-start | bytes 294920 | tf_op jit(solution)/shard_map/ppermute | solution.py:302
  25.0 0.2 shard_map.75
  25.2 1.0 %collective-permute-start.8 = (bf16[384,128]{1,0:T(8,128)(2,1)S(1)}, bf16[384,128]{1,0:T(8,128)(2,1)S(1)}, u32[]{:S(2)}, u32[]{:S(2)}) collective-permute-start(bf16[384,128]{1,0:T(8,128)(2,1)S(1)} %shard_map.75), channel_id=1, source_target_pairs={{0,3},{1,2},{2,1},{3,0},{4,7},{5,6},{6,5},{7,4},{8,11},{9,10},{10,... | collective-permute-start | bytes 294920 | tf_op jit(solution)/shard_map/ppermute | solution.py:302
  26.2 0.0 collective-permute-done.4.their_weight
  26.2 0.6 %shard_map.70.partial = f32[128,1536]{1,0:T(8,128)S(1)} custom-call(bf16[128,640]{1,0:T(8,128)(2,1)S(1)} %shard_map.69.mine, bf16[128,640]{1,0:T(8,128)(2,1)S(1)} %collective-permute-done.3.theirs, bf16[512,1536]{1,0:T(8,128)(2,1)S(1)} %get-tuple-element.30.my_weight, bf16[512,1536]{1,0:T(8,128)(2,1)S(1)} %collective-permute-done.4.their_weight), custom_call_target="tpu_custom_call" | custom-call | flops 600000000 | bytes 600000 | tf_op jit(solution)/shard_map/pallas_call | solution.py:21
  26.8 5.8 %collective-permute-done.6.refs_0_ = bf16[384,128]{1,0:T(8,128)(2,1)S(1)} collective-permute-done((bf16[384,128]{1,0:T(8,128)(2,1)S(1)}, bf16[384,128]{1,0:T(8,128)(2,1)S(1)}, u32[]{:S(2)}, u32[]{:S(2)}) %collective-permute-start.6) | collective-permute-done | bytes 98336 | tf_op jit(solution)/shard_map/ppermute | solution.py:302
  32.6 0.0 collective-permute-done.7.refs_1_
  32.6 0.2 shard_map.74
  32.9 0.3 collective-permute-done.8.refs_2_
  33.1 0.8 %shard_map.76 = bf16[128,1536]{1,0:T(8,128)(2,1)} custom-call(f32[128,1536]{1,0:T(8,128)S(1)} %shard_map.70.partial, f32[128,1]{1,0:T(8,128)S(1)} %get-tuple-element.34.scale, bf16[128,384]{1,0:T(8,128)(2,1)S(1)} %get-tuple-element.35.refs_0_, bf16[128,768]{1,0:T(8,128)(2,1)S(1)} %get-tuple-element.36.refs_1_, ...), custom_call_target="tpu_custom_call" | custom-call | flops 1000000000 | bytes 1000000 | tf_op jit(solution)/shard_map/pallas_call | solution.py:21
Async XLA Ops:
  1.3 6.6 %collective-permute-start = (bf16[528,128]{1,0:T(8,128)(2,1)S(1)}, bf16[528,128]{1,0:T(8,128)(2,1)S(1)}, u32[]{:S(2)}, u32[]{:S(2)}) collective-permute-start(bf16[528,128]{1,0:T(8,128)(2,1)S(1)} %shard_map.64._.refs_0_), channel_id=1, source_target_pairs={{0,4},{4,0},{8,12},{12,8},{16,20},{20,16},{24,28},{28,24},{1,5},{5... | collective-permute-start | bytes 405512 | tf_op jit(solution)/shard_map/ppermute | solution.py:302
  8.0 5.1 %collective-permute-start.1 = (bf16[528,128]{1,0:T(8,128)(2,1)S(1)}, bf16[528,128]{1,0:T(8,128)(2,1)S(1)}, u32[]{:S(2)}, u32[]{:S(2)}) collective-permute-start(bf16[528,128]{1,0:T(8,128)(2,1)S(1)} %get-tuple-element.22.refs_0_), channel_id=1, source_target_pairs={{0,8},{4,12},{8,0},{12,4},{16,24},{20,28},{24,16},{28,20},{1,9},{5... | collective-permute-start | bytes 405512 | tf_op jit(solution)/shard_map/ppermute | solution.py:302
  9.9 16.3 %collective-permute-start.4 = (bf16[512,1536]{1,0:T(8,128)(2,1)S(1)}, bf16[512,1536]{1,0:T(8,128)(2,1)S(1)}, u32[]{:S(2)}, u32[]{:S(2)}) collective-permute-start(bf16[512,1536]{1,0:T(8,128)(2,1)S(1)} %get-tuple-element.31), channel_id=1, source_target_pairs={{0,1},{1,0},{2,3},{3,2},{4,5},{5,4},{6,7},{7,6},{8,9},{9,8},{10,11... | collective-permute-start | bytes 4718600 | tf_op jit(solution)/shard_map/ppermute | solution.py:302
  9.9 12.4 %collective-permute-start.5 = (bf16[512,1536]{1,0:T(8,128)(2,1)S(1)}, bf16[512,1536]{1,0:T(8,128)(2,1)S(1)}, u32[]{:S(2)}, u32[]{:S(2)}) collective-permute-start(bf16[512,1536]{1,0:T(8,128)(2,1)S(1)} %get-tuple-element.33), channel_id=1, source_target_pairs={{0,1},{1,0},{2,3},{3,2},{4,5},{5,4},{6,7},{7,6},{8,9},{9,8},{10,11... | collective-permute-start | bytes 4718600 | tf_op jit(solution)/shard_map/ppermute | solution.py:302
  13.2 7.3 %collective-permute-start.2 = (bf16[512,128]{1,0:T(8,128)(2,1)S(1)}, bf16[512,128]{1,0:T(8,128)(2,1)S(1)}, u32[]{:S(2)}, u32[]{:S(2)}) collective-permute-start(bf16[512,128]{1,0:T(8,128)(2,1)S(1)} %get-tuple-element.29), channel_id=1, source_target_pairs={{0,16},{4,20},{8,24},{12,28},{16,0},{20,4},{24,8},{28,12},{1,17},{... | collective-permute-start | bytes 393224 | tf_op jit(solution)/shard_map/ppermute | solution.py:302
  16.1 4.5 %copy-start = (bf16[128,512]{1,0:T(8,128)(2,1)S(1)}, bf16[128,512]{1,0:T(8,128)(2,1)}, u32[]{:S(2)}) copy-start(bf16[128,512]{1,0:T(8,128)(2,1)} %query.1) | copy-start | bytes 393220
  16.1 4.5 %copy-start.1 = (f32[512]{0:T(512)S(1)}, f32[512]{0:T(512)}, u32[]{:S(2)}) copy-start(f32[512]{0:T(512)} %param.10) | copy-start | bytes 6148
  20.8 1.5 %collective-permute-start.3 = (bf16[128,640]{1,0:T(8,128)(2,1)S(1)}, bf16[128,640]{1,0:T(8,128)(2,1)S(1)}, u32[]{:S(2)}, u32[]{:S(2)}) collective-permute-start(bf16[128,640]{1,0:T(8,128)(2,1)S(1)} %shard_map.69.mine), channel_id=1, source_target_pairs={{0,1},{1,0},{2,3},{3,2},{4,5},{5,4},{6,7},{7,6},{8,9},{9,8},{10,11... | collective-permute-start | bytes 491528 | tf_op jit(solution)/shard_map/ppermute | solution.py:302
  22.6 10.0 %collective-permute-start.7 = (bf16[784,128]{1,0:T(8,128)(2,1)S(1)}, bf16[784,128]{1,0:T(8,128)(2,1)S(1)}, u32[]{:S(2)}, u32[]{:S(2)}) collective-permute-start(bf16[784,128]{1,0:T(8,128)(2,1)S(1)} %shard_map.73), channel_id=1, source_target_pairs={{0,2},{1,3},{2,0},{3,1},{4,6},{5,7},{6,4},{7,5},{8,10},{9,11},{10,... | collective-permute-start | bytes 602120 | tf_op jit(solution)/shard_map/ppermute | solution.py:302
  24.6 8.0 %collective-permute-start.6 = (bf16[384,128]{1,0:T(8,128)(2,1)S(1)}, bf16[384,128]{1,0:T(8,128)(2,1)S(1)}, u32[]{:S(2)}, u32[]{:S(2)}) collective-permute-start(bf16[384,128]{1,0:T(8,128)(2,1)S(1)} %shard_map.72), channel_id=1, source_target_pairs={{0,2},{1,3},{2,0},{3,1},{4,6},{5,7},{6,4},{7,5},{8,10},{9,11},{10,... | collective-permute-start | bytes 294920 | tf_op jit(solution)/shard_map/ppermute | solution.py:302
  25.2 7.9 %collective-permute-start.8 = (bf16[384,128]{1,0:T(8,128)(2,1)S(1)}, bf16[384,128]{1,0:T(8,128)(2,1)S(1)}, u32[]{:S(2)}, u32[]{:S(2)}) collective-permute-start(bf16[384,128]{1,0:T(8,128)(2,1)S(1)} %shard_map.75), channel_id=1, source_target_pairs={{0,3},{1,2},{2,1},{3,0},{4,7},{5,6},{6,5},{7,4},{8,11},{9,10},{10,... | collective-permute-start | bytes 294920 | tf_op jit(solution)/shard_map/ppermute | solution.py:302

commit v5 on v4

--- a/solution.py
+++ b/solution.py
@@ -64,9 +64,13 @@
 
 
 def column_sums(decay):
-    row, col = triangle(decay.shape[1])
-    lower = jnp.where(row >= col, 1.0, 0.0).astype(F32)
-    return lax.dot_general(lower, decay, (((1,), (1,)), ((), ())), precision=HIGHEST)
+    heads, tokens = decay.shape
+    row, col = triangle(tokens)
+    lower = jnp.where(row >= col, 1.0, 0.0).astype(BF16)
+    sums = [
+        lax.dot_general(lower, part, (((1,), (1,)), ((), ())), preferred_element_type=F32) for part in split3(decay)
+    ]
+    return sums[0] + (sums[1] + sums[2])
 
 
 def row_sums(decay):
@@ -104,9 +108,9 @@
         copy.wait()
     for head in range(heads):
         own = slice(head * width, (head + 1) * width)
-        faded = (keys[:, own].astype(F32) * tails[:, own]).astype(BF16)
+        faded = (values[:, own].astype(F32) * tails[:, own]).astype(BF16)
         state = lax.dot_general(
-            faded, values[:, own], (((0,), (0,)), ((), ())), preferred_element_type=F32
+            keys[:, own], faded, (((0,), (0,)), ((), ())), preferred_element_type=F32
         )
         message[own, :] = state.astype(BF16)
 
@@ -313,7 +317,7 @@
 
     far_count = groups // 2
     blocks_out = columns // LANES
-    cuts = [0, blocks_out // 4, blocks_out - blocks_out // 4, blocks_out]
+    cuts = [0, blocks_out // 3, blocks_out - blocks_out // 4, blocks_out]
     *weights, token = call(
         functools.partial(weights_kernel, far_count, cuts[-2] * LANES),
         [shape((full, columns), BF16)] * (2 * far_count) + [shape((8, LANES), F32)],

time: 34.2 us -> 34.1 us (level)
  no operation moved by 1% of the time
where the time goes in v5:
time: 34.1 us; the launch traced here: 33.8 us
  waiting for transfers between devices  13.4 us (39%)
  starting transfers between devices  11.5 us (34%)
  Pallas kernels  8.92 us (26%)
    ppermute x9, waiting for transfers between devices, swap(): return lax.ppermute(value, axis, [(i, i ^ bit) for i in range(count)])  13.4 us
    ppermute x9, starting transfers between devices, swap(): return lax.ppermute(value, axis, [(i, i ^ bit) for i in range(count)])  11.5 us
    pallas_call x13, Pallas kernels, call(): pl.pallas_call(body, out_shape=outs, in_specs=[FAR] * far + [VMEM] * (len...  8.92 us
  transfers between devices with their start and end apart: 9, of which 6 were waited for; matrix products, arithmetic and copies ran while one was open for 0% of the time, Pallas kernels for 20%

profile of v5, /device:TPU:0, one launch (start us, length us, event | category | flops | bytes accessed | tf_op | source)
XLA Modules:
  0.0 33.8 jit_solution(14610391785766007422)
XLA Ops:
  0.0 1.3 %shard_map.64._.refs_0_ = bf16[528,128]{1,0:T(8,128)(2,1)S(1)} custom-call(bf16[128,512]{1,0:T(8,128)(2,1)} %keys_far.3, bf16[128,512]{1,0:T(8,128)(2,1)} %values_far.3, f32[4,128]{1,0:T(4,128)} %bitcast.3), custom_call_target="tpu_custom_call" | custom-call | flops 1000000000 | bytes 1000000 | tf_op jit(solution)/shard_map/pallas_call | solution.py:21
  1.3 3.0 %collective-permute-start = (bf16[528,128]{1,0:T(8,128)(2,1)S(1)}, bf16[528,128]{1,0:T(8,128)(2,1)S(1)}, u32[]{:S(2)}, u32[]{:S(2)}) collective-permute-start(bf16[528,128]{1,0:T(8,128)(2,1)S(1)} %shard_map.64._.refs_0_), channel_id=1, source_target_pairs={{0,4},{4,0},{8,12},{12,8},{16,20},{20,16},{24,28},{28,24},{1,5},{5... | collective-permute-start | bytes 405512 | tf_op jit(solution)/shard_map/ppermute | solution.py:306
  4.3 2.9 %shard_map.65 = (bf16[512,1536]{1,0:T(8,128)(2,1)S(1)}, bf16[512,1536]{1,0:T(8,128)(2,1)S(1)}, bf16[512,1536]{1,0:T(8,128)(2,1)S(1)}, bf16[512,1536]{1,0:T(8,128)(2,1)S(1)}, f32[8,128]{1,0:T(8,128)S(1)}) custom-call(bf16[512,6144]{1,0:T(8,128)(2,1)} %weight_far.1, bf16[528,128]{1,0:T(8,128)(2,1)S(1)} %shard_map.64._.refs_0_), custom_call_target="tpu_custom_call" | custom-call | flops 2000000000 | bytes 2000000 | tf_op jit(solution)/shard_map/pallas_call | solution.py:21
  7.2 0.7 %collective-permute-done.refs_1_ = bf16[528,128]{1,0:T(8,128)(2,1)S(1)} collective-permute-done((bf16[528,128]{1,0:T(8,128)(2,1)S(1)}, bf16[528,128]{1,0:T(8,128)(2,1)S(1)}, u32[]{:S(2)}, u32[]{:S(2)}) %collective-permute-start) | collective-permute-done | bytes 135200 | tf_op jit(solution)/shard_map/ppermute | solution.py:306
  7.9 0.1 shard_map.66
  8.0 1.9 %collective-permute-start.1 = (bf16[528,128]{1,0:T(8,128)(2,1)S(1)}, bf16[528,128]{1,0:T(8,128)(2,1)S(1)}, u32[]{:S(2)}, u32[]{:S(2)}) collective-permute-start(bf16[528,128]{1,0:T(8,128)(2,1)S(1)} %get-tuple-element.22.refs_0_), channel_id=1, source_target_pairs={{0,8},{4,12},{8,0},{12,4},{16,24},{20,28},{24,16},{28,20},{1,9},{5... | collective-permute-start | bytes 405512 | tf_op jit(solution)/shard_map/ppermute | solution.py:306
  9.8 0.0 collective-permute-start.4
  9.8 0.5 %collective-permute-start.5 = (bf16[512,1536]{1,0:T(8,128)(2,1)S(1)}, bf16[512,1536]{1,0:T(8,128)(2,1)S(1)}, u32[]{:S(2)}, u32[]{:S(2)}) collective-permute-start(bf16[512,1536]{1,0:T(8,128)(2,1)S(1)} %get-tuple-element.33), channel_id=1, source_target_pairs={{0,1},{1,0},{2,3},{3,2},{4,5},{5,4},{6,7},{7,6},{8,9},{9,8},{10,11... | collective-permute-start | bytes 4718600 | tf_op jit(solution)/shard_map/ppermute | solution.py:306
  10.4 2.7 %collective-permute-done.1.refs_1_ = bf16[528,128]{1,0:T(8,128)(2,1)S(1)} collective-permute-done((bf16[528,128]{1,0:T(8,128)(2,1)S(1)}, bf16[528,128]{1,0:T(8,128)(2,1)S(1)}, u32[]{:S(2)}, u32[]{:S(2)}) %collective-permute-start.1) | collective-permute-done | bytes 135200 | tf_op jit(solution)/shard_map/ppermute | solution.py:306
  13.1 0.1 shard_map.67
  13.2 2.9 %collective-permute-start.2 = (bf16[512,128]{1,0:T(8,128)(2,1)S(1)}, bf16[512,128]{1,0:T(8,128)(2,1)S(1)}, u32[]{:S(2)}, u32[]{:S(2)}) collective-permute-start(bf16[512,128]{1,0:T(8,128)(2,1)S(1)} %get-tuple-element.29), channel_id=1, source_target_pairs={{0,16},{4,20},{8,24},{12,28},{16,0},{20,4},{24,8},{28,12},{1,17},{... | collective-permute-start | bytes 393224 | tf_op jit(solution)/shard_map/ppermute | solution.py:306
  16.0 0.0 copy-start
  16.0 0.0 copy-start.1
  16.0 1.6 %shard_map.68 = (f32[128,512]{1,0:T(8,128)S(1)}, f32[128,512]{1,0:T(8,128)S(1)}) custom-call(bf16[128,512]{1,0:T(8,128)(2,1)} %query.1, bf16[128,512]{1,0:T(8,128)(2,1)} %keys_far.3, bf16[128,512]{1,0:T(8,128)(2,1)} %values_far.3, f32[4,128]{1,0:T(4,128)} %bitcast.4, f32[512,128]{1,0:T(8,128)S(1)} %get-tuple-element.25.before, ...), custom_call_target="tpu_custom_call" | custom-call | flops 1000000000 | bytes 1000000 | tf_op jit(solution)/shard_map/pallas_call | solution.py:21
  17.6 2.9 %collective-permute-done.2.theirs = bf16[512,128]{1,0:T(8,128)(2,1)S(1)} collective-permute-done((bf16[512,128]{1,0:T(8,128)(2,1)S(1)}, bf16[512,128]{1,0:T(8,128)(2,1)S(1)}, u32[]{:S(2)}, u32[]{:S(2)}) %collective-permute-start.2) | collective-permute-done | bytes 131104 | tf_op jit(solution)/shard_map/ppermute | solution.py:306
  20.5 0.0 copy-done
  20.5 0.0 copy-done.1
  20.5 0.3 shard_map.69.mine
  20.8 0.1 collective-permute-start.3
  20.9 0.4 %shard_map.71.partial = f32[128,1536]{1,0:T(8,128)S(1)} custom-call(bf16[128,640]{1,0:T(8,128)(2,1)S(1)} %shard_map.69.mine, bf16[512,1536]{1,0:T(8,128)(2,1)S(1)} %get-tuple-element.32.weight), custom_call_target="tpu_custom_call" | custom-call | flops 400000000 | bytes 400000 | tf_op jit(solution)/shard_map/pallas_call | solution.py:21
  21.2 1.0 %collective-permute-done.3.theirs = bf16[128,640]{1,0:T(8,128)(2,1)S(1)} collective-permute-done((bf16[128,640]{1,0:T(8,128)(2,1)S(1)}, bf16[128,640]{1,0:T(8,128)(2,1)S(1)}, u32[]{:S(2)}, u32[]{:S(2)}) %collective-permute-start.3) | collective-permute-done | bytes 163872 | tf_op jit(solution)/shard_map/ppermute | solution.py:306
  22.3 0.0 collective-permute-done.5.their_weight
  22.3 0.3 shard_map.73
  22.5 1.8 %collective-permute-start.7 = (bf16[656,128]{1,0:T(8,128)(2,1)S(1)}, bf16[656,128]{1,0:T(8,128)(2,1)S(1)}, u32[]{:S(2)}, u32[]{:S(2)}) collective-permute-start(bf16[656,128]{1,0:T(8,128)(2,1)S(1)} %shard_map.73), channel_id=1, source_target_pairs={{0,2},{1,3},{2,0},{3,1},{4,6},{5,7},{6,4},{7,5},{8,10},{9,11},{10,... | collective-permute-start | bytes 503816 | tf_op jit(solution)/shard_map/ppermute | solution.py:306
  24.3 0.2 shard_map.72
  24.6 0.4 %collective-permute-start.6 = (bf16[512,128]{1,0:T(8,128)(2,1)S(1)}, bf16[512,128]{1,0:T(8,128)(2,1)S(1)}, u32[]{:S(2)}, u32[]{:S(2)}) collective-permute-start(bf16[512,128]{1,0:T(8,128)(2,1)S(1)} %shard_map.72), channel_id=1, source_target_pairs={{0,2},{1,3},{2,0},{3,1},{4,6},{5,7},{6,4},{7,5},{8,10},{9,11},{10,... | collective-permute-start | bytes 393224 | tf_op jit(solution)/shard_map/ppermute | solution.py:306
  24.9 0.2 shard_map.75
  25.2 1.0 %collective-permute-start.8 = (bf16[384,128]{1,0:T(8,128)(2,1)S(1)}, bf16[384,128]{1,0:T(8,128)(2,1)S(1)}, u32[]{:S(2)}, u32[]{:S(2)}) collective-permute-start(bf16[384,128]{1,0:T(8,128)(2,1)S(1)} %shard_map.75), channel_id=1, source_target_pairs={{0,3},{1,2},{2,1},{3,0},{4,7},{5,6},{6,5},{7,4},{8,11},{9,10},{10,... | collective-permute-start | bytes 294920 | tf_op jit(solution)/shard_map/ppermute | solution.py:306
  26.1 0.0 collective-permute-done.4.their_weight
  26.1 0.6 %shard_map.70.partial = f32[128,1536]{1,0:T(8,128)S(1)} custom-call(bf16[128,640]{1,0:T(8,128)(2,1)S(1)} %shard_map.69.mine, bf16[128,640]{1,0:T(8,128)(2,1)S(1)} %collective-permute-done.3.theirs, bf16[512,1536]{1,0:T(8,128)(2,1)S(1)} %get-tuple-element.30.my_weight, bf16[512,1536]{1,0:T(8,128)(2,1)S(1)} %collective-permute-done.4.their_weight), custom_call_target="tpu_custom_call" | custom-call | flops 600000000 | bytes 600000 | tf_op jit(solution)/shard_map/pallas_call | solution.py:21
  26.7 5.8 %collective-permute-done.6.refs_0_ = bf16[512,128]{1,0:T(8,128)(2,1)S(1)} collective-permute-done((bf16[512,128]{1,0:T(8,128)(2,1)S(1)}, bf16[512,128]{1,0:T(8,128)(2,1)S(1)}, u32[]{:S(2)}, u32[]{:S(2)}) %collective-permute-start.6) | collective-permute-done | bytes 131104 | tf_op jit(solution)/shard_map/ppermute | solution.py:306
  32.5 0.0 collective-permute-done.7.refs_1_
  32.5 0.2 shard_map.74
  32.8 0.3 collective-permute-done.8.refs_2_
  33.1 0.8 %shard_map.76 = bf16[128,1536]{1,0:T(8,128)(2,1)} custom-call(f32[128,1536]{1,0:T(8,128)S(1)} %shard_map.70.partial, f32[128,1]{1,0:T(8,128)S(1)} %get-tuple-element.34.scale, bf16[128,512]{1,0:T(8,128)(2,1)S(1)} %get-tuple-element.35.refs_0_, bf16[128,640]{1,0:T(8,128)(2,1)S(1)} %get-tuple-element.36.refs_1_, ...), custom_call_target="tpu_custom_call" | custom-call | flops 1000000000 | bytes 1000000 | tf_op jit(solution)/shard_map/pallas_call | solution.py:21
Async XLA Ops:
  1.3 6.6 %collective-permute-start = (bf16[528,128]{1,0:T(8,128)(2,1)S(1)}, bf16[528,128]{1,0:T(8,128)(2,1)S(1)}, u32[]{:S(2)}, u32[]{:S(2)}) collective-permute-start(bf16[528,128]{1,0:T(8,128)(2,1)S(1)} %shard_map.64._.refs_0_), channel_id=1, source_target_pairs={{0,4},{4,0},{8,12},{12,8},{16,20},{20,16},{24,28},{28,24},{1,5},{5... | collective-permute-start | bytes 405512 | tf_op jit(solution)/shard_map/ppermute | solution.py:306
  8.0 5.1 %collective-permute-start.1 = (bf16[528,128]{1,0:T(8,128)(2,1)S(1)}, bf16[528,128]{1,0:T(8,128)(2,1)S(1)}, u32[]{:S(2)}, u32[]{:S(2)}) collective-permute-start(bf16[528,128]{1,0:T(8,128)(2,1)S(1)} %get-tuple-element.22.refs_0_), channel_id=1, source_target_pairs={{0,8},{4,12},{8,0},{12,4},{16,24},{20,28},{24,16},{28,20},{1,9},{5... | collective-permute-start | bytes 405512 | tf_op jit(solution)/shard_map/ppermute | solution.py:306
  9.8 16.3 %collective-permute-start.4 = (bf16[512,1536]{1,0:T(8,128)(2,1)S(1)}, bf16[512,1536]{1,0:T(8,128)(2,1)S(1)}, u32[]{:S(2)}, u32[]{:S(2)}) collective-permute-start(bf16[512,1536]{1,0:T(8,128)(2,1)S(1)} %get-tuple-element.31), channel_id=1, source_target_pairs={{0,1},{1,0},{2,3},{3,2},{4,5},{5,4},{6,7},{7,6},{8,9},{9,8},{10,11... | collective-permute-start | bytes 4718600 | tf_op jit(solution)/shard_map/ppermute | solution.py:306
  9.8 12.4 %collective-permute-start.5 = (bf16[512,1536]{1,0:T(8,128)(2,1)S(1)}, bf16[512,1536]{1,0:T(8,128)(2,1)S(1)}, u32[]{:S(2)}, u32[]{:S(2)}) collective-permute-start(bf16[512,1536]{1,0:T(8,128)(2,1)S(1)} %get-tuple-element.33), channel_id=1, source_target_pairs={{0,1},{1,0},{2,3},{3,2},{4,5},{5,4},{6,7},{7,6},{8,9},{9,8},{10,11... | collective-permute-start | bytes 4718600 | tf_op jit(solution)/shard_map/ppermute | solution.py:306
  13.2 7.3 %collective-permute-start.2 = (bf16[512,128]{1,0:T(8,128)(2,1)S(1)}, bf16[512,128]{1,0:T(8,128)(2,1)S(1)}, u32[]{:S(2)}, u32[]{:S(2)}) collective-permute-start(bf16[512,128]{1,0:T(8,128)(2,1)S(1)} %get-tuple-element.29), channel_id=1, source_target_pairs={{0,16},{4,20},{8,24},{12,28},{16,0},{20,4},{24,8},{28,12},{1,17},{... | collective-permute-start | bytes 393224 | tf_op jit(solution)/shard_map/ppermute | solution.py:306
  16.0 4.5 %copy-start = (bf16[128,512]{1,0:T(8,128)(2,1)S(1)}, bf16[128,512]{1,0:T(8,128)(2,1)}, u32[]{:S(2)}) copy-start(bf16[128,512]{1,0:T(8,128)(2,1)} %query.1) | copy-start | bytes 393220
  16.0 4.5 %copy-start.1 = (f32[512]{0:T(512)S(1)}, f32[512]{0:T(512)}, u32[]{:S(2)}) copy-start(f32[512]{0:T(512)} %param.10) | copy-start | bytes 6148
  20.8 1.5 %collective-permute-start.3 = (bf16[128,640]{1,0:T(8,128)(2,1)S(1)}, bf16[128,640]{1,0:T(8,128)(2,1)S(1)}, u32[]{:S(2)}, u32[]{:S(2)}) collective-permute-start(bf16[128,640]{1,0:T(8,128)(2,1)S(1)} %shard_map.69.mine), channel_id=1, source_target_pairs={{0,1},{1,0},{2,3},{3,2},{4,5},{5,4},{6,7},{7,6},{8,9},{9,8},{10,11... | collective-permute-start | bytes 491528 | tf_op jit(solution)/shard_map/ppermute | solution.py:306
  22.5 10.0 %collective-permute-start.7 = (bf16[656,128]{1,0:T(8,128)(2,1)S(1)}, bf16[656,128]{1,0:T(8,128)(2,1)S(1)}, u32[]{:S(2)}, u32[]{:S(2)}) collective-permute-start(bf16[656,128]{1,0:T(8,128)(2,1)S(1)} %shard_map.73), channel_id=1, source_target_pairs={{0,2},{1,3},{2,0},{3,1},{4,6},{5,7},{6,4},{7,5},{8,10},{9,11},{10,... | collective-permute-start | bytes 503816 | tf_op jit(solution)/shard_map/ppermute | solution.py:306
  24.6 8.0 %collective-permute-start.6 = (bf16[512,128]{1,0:T(8,128)(2,1)S(1)}, bf16[512,128]{1,0:T(8,128)(2,1)S(1)}, u32[]{:S(2)}, u32[]{:S(2)}) collective-permute-start(bf16[512,128]{1,0:T(8,128)(2,1)S(1)} %shard_map.72), channel_id=1, source_target_pairs={{0,2},{1,3},{2,0},{3,1},{4,6},{5,7},{6,4},{7,5},{8,10},{9,11},{10,... | collective-permute-start | bytes 393224 | tf_op jit(solution)/shard_map/ppermute | solution.py:306
  25.2 7.9 %collective-permute-start.8 = (bf16[384,128]{1,0:T(8,128)(2,1)S(1)}, bf16[384,128]{1,0:T(8,128)(2,1)S(1)}, u32[]{:S(2)}, u32[]{:S(2)}) collective-permute-start(bf16[384,128]{1,0:T(8,128)(2,1)S(1)} %shard_map.75), channel_id=1, source_target_pairs={{0,3},{1,2},{2,1},{3,0},{4,7},{5,6},{6,5},{7,4},{8,11},{9,10},{10,... | collective-permute-start | bytes 294920 | tf_op jit(solution)/shard_map/ppermute | solution.py:306

commit v6 on v5

--- a/solution.py
+++ b/solution.py
@@ -205,12 +205,7 @@
         attn = within[:, own] + factor[:, own] * carried
         squares = squares + attn * attn
         message[:, own] = (attn * gain[:, own]).astype(BF16)
-    squares = jnp.sum(squares, axis=1, keepdims=True)
-    high, mid, low = split3(squares)
-    lane = lax.broadcasted_iota(jnp.int32, (tokens, LANES), 1)
-    pieces = jnp.where(lane == 0, high.astype(F32), 0.0)
-    pieces = jnp.where(lane == 1, mid.astype(F32), pieces)
-    message[:, full:] = jnp.where(lane == 2, low.astype(F32), pieces).astype(BF16)
+    message[:, full:] = squares.astype(BF16)
 
 
 def squares_row(mine, theirs, full):

time: 34.1 us -> 34.1 us (level)
  no operation moved by 1% of the time
where the time goes in v6:
time: 34.1 us; the launch traced here: 33.8 us
  waiting for transfers between devices  13.4 us (39%)
  starting transfers between devices  11.5 us (34%)
  Pallas kernels  8.83 us (26%)
    ppermute x9, waiting for transfers between devices, swap(): return lax.ppermute(value, axis, [(i, i ^ bit) for i in range(count)])  13.4 us
    ppermute x9, starting transfers between devices, swap(): return lax.ppermute(value, axis, [(i, i ^ bit) for i in range(count)])  11.5 us
    pallas_call x13, Pallas kernels, call(): pl.pallas_call(body, out_shape=outs, in_specs=[FAR] * far + [VMEM] * (len...  8.83 us
  transfers between devices with their start and end apart: 9, of which 6 were waited for; matrix products, arithmetic and copies ran while one was open for 0% of the time, Pallas kernels for 20%

profile of v6, /device:TPU:0, one launch (start us, length us, event | category | flops | bytes accessed | tf_op | source)
XLA Modules:
  0.0 33.8 jit_solution(4121542762718716831)
XLA Ops:
  0.0 1.3 %shard_map.64._.refs_0_ = bf16[528,128]{1,0:T(8,128)(2,1)S(1)} custom-call(bf16[128,512]{1,0:T(8,128)(2,1)} %keys_far.3, bf16[128,512]{1,0:T(8,128)(2,1)} %values_far.3, f32[4,128]{1,0:T(4,128)} %bitcast.3), custom_call_target="tpu_custom_call" | custom-call | flops 1000000000 | bytes 1000000 | tf_op jit(solution)/shard_map/pallas_call | solution.py:21
  1.3 3.0 %collective-permute-start = (bf16[528,128]{1,0:T(8,128)(2,1)S(1)}, bf16[528,128]{1,0:T(8,128)(2,1)S(1)}, u32[]{:S(2)}, u32[]{:S(2)}) collective-permute-start(bf16[528,128]{1,0:T(8,128)(2,1)S(1)} %shard_map.64._.refs_0_), channel_id=1, source_target_pairs={{0,4},{4,0},{8,12},{12,8},{16,20},{20,16},{24,28},{28,24},{1,5},{5... | collective-permute-start | bytes 405512 | tf_op jit(solution)/shard_map/ppermute | solution.py:301
  4.3 2.9 %shard_map.65 = (bf16[512,1536]{1,0:T(8,128)(2,1)S(1)}, bf16[512,1536]{1,0:T(8,128)(2,1)S(1)}, bf16[512,1536]{1,0:T(8,128)(2,1)S(1)}, bf16[512,1536]{1,0:T(8,128)(2,1)S(1)}, f32[8,128]{1,0:T(8,128)S(1)}) custom-call(bf16[512,6144]{1,0:T(8,128)(2,1)} %weight_far.1, bf16[528,128]{1,0:T(8,128)(2,1)S(1)} %shard_map.64._.refs_0_), custom_call_target="tpu_custom_call" | custom-call | flops 2000000000 | bytes 2000000 | tf_op jit(solution)/shard_map/pallas_call | solution.py:21
  7.2 0.7 %collective-permute-done.refs_1_ = bf16[528,128]{1,0:T(8,128)(2,1)S(1)} collective-permute-done((bf16[528,128]{1,0:T(8,128)(2,1)S(1)}, bf16[528,128]{1,0:T(8,128)(2,1)S(1)}, u32[]{:S(2)}, u32[]{:S(2)}) %collective-permute-start) | collective-permute-done | bytes 135200 | tf_op jit(solution)/shard_map/ppermute | solution.py:301
  7.9 0.1 shard_map.66
  8.0 1.9 %collective-permute-start.1 = (bf16[528,128]{1,0:T(8,128)(2,1)S(1)}, bf16[528,128]{1,0:T(8,128)(2,1)S(1)}, u32[]{:S(2)}, u32[]{:S(2)}) collective-permute-start(bf16[528,128]{1,0:T(8,128)(2,1)S(1)} %get-tuple-element.22.refs_0_), channel_id=1, source_target_pairs={{0,8},{4,12},{8,0},{12,4},{16,24},{20,28},{24,16},{28,20},{1,9},{5... | collective-permute-start | bytes 405512 | tf_op jit(solution)/shard_map/ppermute | solution.py:301
  9.8 0.0 collective-permute-start.4
  9.8 0.5 %collective-permute-start.5 = (bf16[512,1536]{1,0:T(8,128)(2,1)S(1)}, bf16[512,1536]{1,0:T(8,128)(2,1)S(1)}, u32[]{:S(2)}, u32[]{:S(2)}) collective-permute-start(bf16[512,1536]{1,0:T(8,128)(2,1)S(1)} %get-tuple-element.33), channel_id=1, source_target_pairs={{0,1},{1,0},{2,3},{3,2},{4,5},{5,4},{6,7},{7,6},{8,9},{9,8},{10,11... | collective-permute-start | bytes 4718600 | tf_op jit(solution)/shard_map/ppermute | solution.py:301
  10.4 2.7 %collective-permute-done.1.refs_1_ = bf16[528,128]{1,0:T(8,128)(2,1)S(1)} collective-permute-done((bf16[528,128]{1,0:T(8,128)(2,1)S(1)}, bf16[528,128]{1,0:T(8,128)(2,1)S(1)}, u32[]{:S(2)}, u32[]{:S(2)}) %collective-permute-start.1) | collective-permute-done | bytes 135200 | tf_op jit(solution)/shard_map/ppermute | solution.py:301
  13.1 0.1 shard_map.67
  13.2 2.9 %collective-permute-start.2 = (bf16[512,128]{1,0:T(8,128)(2,1)S(1)}, bf16[512,128]{1,0:T(8,128)(2,1)S(1)}, u32[]{:S(2)}, u32[]{:S(2)}) collective-permute-start(bf16[512,128]{1,0:T(8,128)(2,1)S(1)} %get-tuple-element.29), channel_id=1, source_target_pairs={{0,16},{4,20},{8,24},{12,28},{16,0},{20,4},{24,8},{28,12},{1,17},{... | collective-permute-start | bytes 393224 | tf_op jit(solution)/shard_map/ppermute | solution.py:301
  16.0 0.0 copy-start
  16.0 0.0 copy-start.1
  16.0 1.6 %shard_map.68 = (f32[128,512]{1,0:T(8,128)S(1)}, f32[128,512]{1,0:T(8,128)S(1)}) custom-call(bf16[128,512]{1,0:T(8,128)(2,1)} %query.1, bf16[128,512]{1,0:T(8,128)(2,1)} %keys_far.3, bf16[128,512]{1,0:T(8,128)(2,1)} %values_far.3, f32[4,128]{1,0:T(4,128)} %bitcast.4, f32[512,128]{1,0:T(8,128)S(1)} %get-tuple-element.25.before, ...), custom_call_target="tpu_custom_call" | custom-call | flops 1000000000 | bytes 1000000 | tf_op jit(solution)/shard_map/pallas_call | solution.py:21
  17.6 2.9 %collective-permute-done.2.theirs = bf16[512,128]{1,0:T(8,128)(2,1)S(1)} collective-permute-done((bf16[512,128]{1,0:T(8,128)(2,1)S(1)}, bf16[512,128]{1,0:T(8,128)(2,1)S(1)}, u32[]{:S(2)}, u32[]{:S(2)}) %collective-permute-start.2) | collective-permute-done | bytes 131104 | tf_op jit(solution)/shard_map/ppermute | solution.py:301
  20.5 0.0 copy-done
  20.5 0.0 copy-done.1
  20.5 0.2 shard_map.69.mine
  20.7 0.1 collective-permute-start.3
  20.8 0.4 %shard_map.71.partial = f32[128,1536]{1,0:T(8,128)S(1)} custom-call(bf16[128,640]{1,0:T(8,128)(2,1)S(1)} %shard_map.69.mine, bf16[512,1536]{1,0:T(8,128)(2,1)S(1)} %get-tuple-element.32.weight), custom_call_target="tpu_custom_call" | custom-call | flops 400000000 | bytes 400000 | tf_op jit(solution)/shard_map/pallas_call | solution.py:21
  21.2 1.0 %collective-permute-done.3.theirs = bf16[128,640]{1,0:T(8,128)(2,1)S(1)} collective-permute-done((bf16[128,640]{1,0:T(8,128)(2,1)S(1)}, bf16[128,640]{1,0:T(8,128)(2,1)S(1)}, u32[]{:S(2)}, u32[]{:S(2)}) %collective-permute-start.3) | collective-permute-done | bytes 163872 | tf_op jit(solution)/shard_map/ppermute | solution.py:301
  22.2 0.0 collective-permute-done.5.their_weight
  22.2 0.3 shard_map.73
  22.4 1.8 %collective-permute-start.7 = (bf16[656,128]{1,0:T(8,128)(2,1)S(1)}, bf16[656,128]{1,0:T(8,128)(2,1)S(1)}, u32[]{:S(2)}, u32[]{:S(2)}) collective-permute-start(bf16[656,128]{1,0:T(8,128)(2,1)S(1)} %shard_map.73), channel_id=1, source_target_pairs={{0,2},{1,3},{2,0},{3,1},{4,6},{5,7},{6,4},{7,5},{8,10},{9,11},{10,... | collective-permute-start | bytes 503816 | tf_op jit(solution)/shard_map/ppermute | solution.py:301
  24.2 0.2 shard_map.72
  24.5 0.4 %collective-permute-start.6 = (bf16[512,128]{1,0:T(8,128)(2,1)S(1)}, bf16[512,128]{1,0:T(8,128)(2,1)S(1)}, u32[]{:S(2)}, u32[]{:S(2)}) collective-permute-start(bf16[512,128]{1,0:T(8,128)(2,1)S(1)} %shard_map.72), channel_id=1, source_target_pairs={{0,2},{1,3},{2,0},{3,1},{4,6},{5,7},{6,4},{7,5},{8,10},{9,11},{10,... | collective-permute-start | bytes 393224 | tf_op jit(solution)/shard_map/ppermute | solution.py:301
  24.8 0.2 shard_map.75
  25.1 1.0 %collective-permute-start.8 = (bf16[384,128]{1,0:T(8,128)(2,1)S(1)}, bf16[384,128]{1,0:T(8,128)(2,1)S(1)}, u32[]{:S(2)}, u32[]{:S(2)}) collective-permute-start(bf16[384,128]{1,0:T(8,128)(2,1)S(1)} %shard_map.75), channel_id=1, source_target_pairs={{0,3},{1,2},{2,1},{3,0},{4,7},{5,6},{6,5},{7,4},{8,11},{9,10},{10,... | collective-permute-start | bytes 294920 | tf_op jit(solution)/shard_map/ppermute | solution.py:301
  26.0 0.0 collective-permute-done.4.their_weight
  26.1 0.6 %shard_map.70.partial = f32[128,1536]{1,0:T(8,128)S(1)} custom-call(bf16[128,640]{1,0:T(8,128)(2,1)S(1)} %shard_map.69.mine, bf16[128,640]{1,0:T(8,128)(2,1)S(1)} %collective-permute-done.3.theirs, bf16[512,1536]{1,0:T(8,128)(2,1)S(1)} %get-tuple-element.30.my_weight, bf16[512,1536]{1,0:T(8,128)(2,1)S(1)} %collective-permute-done.4.their_weight), custom_call_target="tpu_custom_call" | custom-call | flops 600000000 | bytes 600000 | tf_op jit(solution)/shard_map/pallas_call | solution.py:21
  26.6 5.8 %collective-permute-done.6.refs_0_ = bf16[512,128]{1,0:T(8,128)(2,1)S(1)} collective-permute-done((bf16[512,128]{1,0:T(8,128)(2,1)S(1)}, bf16[512,128]{1,0:T(8,128)(2,1)S(1)}, u32[]{:S(2)}, u32[]{:S(2)}) %collective-permute-start.6) | collective-permute-done | bytes 131104 | tf_op jit(solution)/shard_map/ppermute | solution.py:301
  32.5 0.0 collective-permute-done.7.refs_1_
  32.5 0.2 shard_map.74
  32.7 0.3 collective-permute-done.8.refs_2_
  33.0 0.8 %shard_map.76 = bf16[128,1536]{1,0:T(8,128)(2,1)} custom-call(f32[128,1536]{1,0:T(8,128)S(1)} %shard_map.70.partial, f32[128,1]{1,0:T(8,128)S(1)} %get-tuple-element.34.scale, bf16[128,512]{1,0:T(8,128)(2,1)S(1)} %get-tuple-element.35.refs_0_, bf16[128,640]{1,0:T(8,128)(2,1)S(1)} %get-tuple-element.36.refs_1_, ...), custom_call_target="tpu_custom_call" | custom-call | flops 1000000000 | bytes 1000000 | tf_op jit(solution)/shard_map/pallas_call | solution.py:21
Async XLA Ops:
  1.3 6.6 %collective-permute-start = (bf16[528,128]{1,0:T(8,128)(2,1)S(1)}, bf16[528,128]{1,0:T(8,128)(2,1)S(1)}, u32[]{:S(2)}, u32[]{:S(2)}) collective-permute-start(bf16[528,128]{1,0:T(8,128)(2,1)S(1)} %shard_map.64._.refs_0_), channel_id=1, source_target_pairs={{0,4},{4,0},{8,12},{12,8},{16,20},{20,16},{24,28},{28,24},{1,5},{5... | collective-permute-start | bytes 405512 | tf_op jit(solution)/shard_map/ppermute | solution.py:301
  8.0 5.1 %collective-permute-start.1 = (bf16[528,128]{1,0:T(8,128)(2,1)S(1)}, bf16[528,128]{1,0:T(8,128)(2,1)S(1)}, u32[]{:S(2)}, u32[]{:S(2)}) collective-permute-start(bf16[528,128]{1,0:T(8,128)(2,1)S(1)} %get-tuple-element.22.refs_0_), channel_id=1, source_target_pairs={{0,8},{4,12},{8,0},{12,4},{16,24},{20,28},{24,16},{28,20},{1,9},{5... | collective-permute-start | bytes 405512 | tf_op jit(solution)/shard_map/ppermute | solution.py:301
  9.8 16.2 %collective-permute-start.4 = (bf16[512,1536]{1,0:T(8,128)(2,1)S(1)}, bf16[512,1536]{1,0:T(8,128)(2,1)S(1)}, u32[]{:S(2)}, u32[]{:S(2)}) collective-permute-start(bf16[512,1536]{1,0:T(8,128)(2,1)S(1)} %get-tuple-element.31), channel_id=1, source_target_pairs={{0,1},{1,0},{2,3},{3,2},{4,5},{5,4},{6,7},{7,6},{8,9},{9,8},{10,11... | collective-permute-start | bytes 4718600 | tf_op jit(solution)/shard_map/ppermute | solution.py:301
  9.8 12.3 %collective-permute-start.5 = (bf16[512,1536]{1,0:T(8,128)(2,1)S(1)}, bf16[512,1536]{1,0:T(8,128)(2,1)S(1)}, u32[]{:S(2)}, u32[]{:S(2)}) collective-permute-start(bf16[512,1536]{1,0:T(8,128)(2,1)S(1)} %get-tuple-element.33), channel_id=1, source_target_pairs={{0,1},{1,0},{2,3},{3,2},{4,5},{5,4},{6,7},{7,6},{8,9},{9,8},{10,11... | collective-permute-start | bytes 4718600 | tf_op jit(solution)/shard_map/ppermute | solution.py:301
  13.2 7.3 %collective-permute-start.2 = (bf16[512,128]{1,0:T(8,128)(2,1)S(1)}, bf16[512,128]{1,0:T(8,128)(2,1)S(1)}, u32[]{:S(2)}, u32[]{:S(2)}) collective-permute-start(bf16[512,128]{1,0:T(8,128)(2,1)S(1)} %get-tuple-element.29), channel_id=1, source_target_pairs={{0,16},{4,20},{8,24},{12,28},{16,0},{20,4},{24,8},{28,12},{1,17},{... | collective-permute-start | bytes 393224 | tf_op jit(solution)/shard_map/ppermute | solution.py:301
  16.0 4.5 %copy-start = (bf16[128,512]{1,0:T(8,128)(2,1)S(1)}, bf16[128,512]{1,0:T(8,128)(2,1)}, u32[]{:S(2)}) copy-start(bf16[128,512]{1,0:T(8,128)(2,1)} %query.1) | copy-start | bytes 393220
  16.0 4.5 %copy-start.1 = (f32[512]{0:T(512)S(1)}, f32[512]{0:T(512)}, u32[]{:S(2)}) copy-start(f32[512]{0:T(512)} %param.10) | copy-start | bytes 6148
  20.7 1.5 %collective-permute-start.3 = (bf16[128,640]{1,0:T(8,128)(2,1)S(1)}, bf16[128,640]{1,0:T(8,128)(2,1)S(1)}, u32[]{:S(2)}, u32[]{:S(2)}) collective-permute-start(bf16[128,640]{1,0:T(8,128)(2,1)S(1)} %shard_map.69.mine), channel_id=1, source_target_pairs={{0,1},{1,0},{2,3},{3,2},{4,5},{5,4},{6,7},{7,6},{8,9},{9,8},{10,11... | collective-permute-start | bytes 491528 | tf_op jit(solution)/shard_map/ppermute | solution.py:301
  22.4 10.0 %collective-permute-start.7 = (bf16[656,128]{1,0:T(8,128)(2,1)S(1)}, bf16[656,128]{1,0:T(8,128)(2,1)S(1)}, u32[]{:S(2)}, u32[]{:S(2)}) collective-permute-start(bf16[656,128]{1,0:T(8,128)(2,1)S(1)} %shard_map.73), channel_id=1, source_target_pairs={{0,2},{1,3},{2,0},{3,1},{4,6},{5,7},{6,4},{7,5},{8,10},{9,11},{10,... | collective-permute-start | bytes 503816 | tf_op jit(solution)/shard_map/ppermute | solution.py:301
  24.5 8.0 %collective-permute-start.6 = (bf16[512,128]{1,0:T(8,128)(2,1)S(1)}, bf16[512,128]{1,0:T(8,128)(2,1)S(1)}, u32[]{:S(2)}, u32[]{:S(2)}) collective-permute-start(bf16[512,128]{1,0:T(8,128)(2,1)S(1)} %shard_map.72), channel_id=1, source_target_pairs={{0,2},{1,3},{2,0},{3,1},{4,6},{5,7},{6,4},{7,5},{8,10},{9,11},{10,... | collective-permute-start | bytes 393224 | tf_op jit(solution)/shard_map/ppermute | solution.py:301
  25.1 7.9 %collective-permute-start.8 = (bf16[384,128]{1,0:T(8,128)(2,1)S(1)}, bf16[384,128]{1,0:T(8,128)(2,1)S(1)}, u32[]{:S(2)}, u32[]{:S(2)}) collective-permute-start(bf16[384,128]{1,0:T(8,128)(2,1)S(1)} %shard_map.75), channel_id=1, source_target_pairs={{0,3},{1,2},{2,1},{3,0},{4,7},{5,6},{6,5},{7,4},{8,11},{9,10},{10,... | collective-permute-start | bytes 294920 | tf_op jit(solution)/shard_map/ppermute | solution.py:301

commit v7 on v6

--- a/solution.py
+++ b/solution.py
@@ -63,10 +63,10 @@
     return row, col
 
 
-def column_sums(decay):
+def column_sums(decay, after=False):
     heads, tokens = decay.shape
     row, col = triangle(tokens)
-    lower = jnp.where(row >= col, 1.0, 0.0).astype(BF16)
+    lower = jnp.where(row < col if after else row >= col, 1.0, 0.0).astype(BF16)
     sums = [
         lax.dot_general(lower, part, (((1,), (1,)), ((), ())), preferred_element_type=F32) for part in split3(decay)
     ]
@@ -98,8 +98,7 @@
     decay_copy.wait()
     heads, tokens = decay.shape
     width = keys.shape[1] // heads
-    column = column_sums(decay[...])
-    tail = jnp.exp(column[tokens - 1 : tokens, :] - column)
+    tail = jnp.exp(column_sums(decay[...], after=True))
     for head in range(heads):
         tails[:, head * width : (head + 1) * width] = jnp.broadcast_to(tail[:, head : head + 1], (tokens, width))
     total = jnp.sum(decay[...], axis=1, keepdims=True)
@@ -252,13 +251,13 @@
         out[:, block * LANES : (block + 1) * LANES] = (summed * scale).astype(BF16)
 
 
-def middle_kernel(full, cuts, count, mine, theirs, partial, *refs):
+def middle_kernel(full, cuts, count, sent, partial, *refs):
     received, (scale, *outs) = refs[: len(cuts) * count], refs[len(cuts) * count :]
     groups = [received[part * count : (part + 1) * count] for part in range(len(cuts))]
-    total = squares_row(mine, theirs, full)
+    total = unstacked(sent[sent.shape[0] - SUBLANES :, :], 1)
     for other in groups[-1]:
         total = total + unstacked(other[other.shape[0] - SUBLANES :, :], 1)
-    row, col = triangle(mine.shape[0])
+    row, col = triangle(partial.shape[0])
     total = jnp.sum(jnp.where(row == col, total, 0.0), axis=1, keepdims=True)
     factor = lax.rsqrt(total / (full * lax.axis_size("head")) + 1e-05)
     scale[...] = factor
@@ -365,6 +364,7 @@
 
     received = [[[] for _ in range(PARTS)] for _ in range(far_count)]
     reach = far_count // 2
+    sent = None
     while reach:
         for far in range(reach, 2 * reach):
             for part, (first, end) in enumerate(zip(cuts[:-1], cuts[1:])):
@@ -374,6 +374,8 @@
                     (ahead[far], mine, mate, their_weights[far], *received[far][part]),
                     cost=0.2,
                 )
+                if part == PARTS - 2 and sent is None:
+                    sent = away
                 hop = 3 if reach == 1 and part == PARTS - 1 else reach << 1
                 received[far - reach][part].append(swap(away, "head", hop))
         reach //= 2
@@ -387,7 +389,7 @@
     scale, *done = call(
         functools.partial(middle_kernel, full, cuts[: PARTS - 1], len(received[0][0])),
         [shape((tokens, 1), F32)] + [shape((tokens, width), BF16) for width in widths[:-1]],
-        (mine, mate, partial, *(other for group in received[0][:-1] for other in group)),
+        (sent, partial, *(other for group in received[0][:-1] for other in group)),
         cost=0.3,
     )
     (mixed,) = call(

time: 34.1 us -> 34.1 us (level)
  no operation moved by 1% of the time
where the time goes in v7:
time: 34.1 us; the launch traced here: 33.8 us
  waiting for transfers between devices  13.4 us (39%)
  starting transfers between devices  11.5 us (34%)
  Pallas kernels  8.78 us (26%)
    ppermute x9, waiting for transfers between devices, swap(): return lax.ppermute(value, axis, [(i, i ^ bit) for i in range(count)])  13.4 us
    ppermute x9, starting transfers between devices, swap(): return lax.ppermute(value, axis, [(i, i ^ bit) for i in range(count)])  11.5 us
    pallas_call x13, Pallas kernels, call(): pl.pallas_call(body, out_shape=outs, in_specs=[FAR] * far + [VMEM] * (len...  8.78 us
  transfers between devices with their start and end apart: 9, of which 6 were waited for; matrix products, arithmetic and copies ran while one was open for 0% of the time, Pallas kernels for 20%

profile of v7, /device:TPU:0, one launch (start us, length us, event | category | flops | bytes accessed | tf_op | source)
XLA Modules:
  0.0 33.8 jit_solution(4804986769425779639)
XLA Ops:
  0.0 1.3 %shard_map.64._.refs_0_ = bf16[528,128]{1,0:T(8,128)(2,1)S(1)} custom-call(bf16[128,512]{1,0:T(8,128)(2,1)} %keys_far.3, bf16[128,512]{1,0:T(8,128)(2,1)} %values_far.3, f32[4,128]{1,0:T(4,128)} %bitcast.3), custom_call_target="tpu_custom_call" | custom-call | flops 1000000000 | bytes 1000000 | tf_op jit(solution)/shard_map/pallas_call | solution.py:21
  1.3 3.0 %collective-permute-start = (bf16[528,128]{1,0:T(8,128)(2,1)S(1)}, bf16[528,128]{1,0:T(8,128)(2,1)S(1)}, u32[]{:S(2)}, u32[]{:S(2)}) collective-permute-start(bf16[528,128]{1,0:T(8,128)(2,1)S(1)} %shard_map.64._.refs_0_), channel_id=1, source_target_pairs={{0,4},{4,0},{8,12},{12,8},{16,20},{20,16},{24,28},{28,24},{1,5},{5... | collective-permute-start | bytes 405512 | tf_op jit(solution)/shard_map/ppermute | solution.py:300
  4.3 2.9 %shard_map.65 = (bf16[512,1536]{1,0:T(8,128)(2,1)S(1)}, bf16[512,1536]{1,0:T(8,128)(2,1)S(1)}, bf16[512,1536]{1,0:T(8,128)(2,1)S(1)}, bf16[512,1536]{1,0:T(8,128)(2,1)S(1)}, f32[8,128]{1,0:T(8,128)S(1)}) custom-call(bf16[512,6144]{1,0:T(8,128)(2,1)} %weight_far.1, bf16[528,128]{1,0:T(8,128)(2,1)S(1)} %shard_map.64._.refs_0_), custom_call_target="tpu_custom_call" | custom-call | flops 2000000000 | bytes 2000000 | tf_op jit(solution)/shard_map/pallas_call | solution.py:21
  7.2 0.7 %collective-permute-done.refs_1_ = bf16[528,128]{1,0:T(8,128)(2,1)S(1)} collective-permute-done((bf16[528,128]{1,0:T(8,128)(2,1)S(1)}, bf16[528,128]{1,0:T(8,128)(2,1)S(1)}, u32[]{:S(2)}, u32[]{:S(2)}) %collective-permute-start) | collective-permute-done | bytes 135200 | tf_op jit(solution)/shard_map/ppermute | solution.py:300
  7.9 0.1 shard_map.66
  8.0 1.9 %collective-permute-start.1 = (bf16[528,128]{1,0:T(8,128)(2,1)S(1)}, bf16[528,128]{1,0:T(8,128)(2,1)S(1)}, u32[]{:S(2)}, u32[]{:S(2)}) collective-permute-start(bf16[528,128]{1,0:T(8,128)(2,1)S(1)} %get-tuple-element.22.refs_0_), channel_id=1, source_target_pairs={{0,8},{4,12},{8,0},{12,4},{16,24},{20,28},{24,16},{28,20},{1,9},{5... | collective-permute-start | bytes 405512 | tf_op jit(solution)/shard_map/ppermute | solution.py:300
  9.9 0.0 collective-permute-start.4
  9.9 0.5 %collective-permute-start.5 = (bf16[512,1536]{1,0:T(8,128)(2,1)S(1)}, bf16[512,1536]{1,0:T(8,128)(2,1)S(1)}, u32[]{:S(2)}, u32[]{:S(2)}) collective-permute-start(bf16[512,1536]{1,0:T(8,128)(2,1)S(1)} %get-tuple-element.33), channel_id=1, source_target_pairs={{0,1},{1,0},{2,3},{3,2},{4,5},{5,4},{6,7},{7,6},{8,9},{9,8},{10,11... | collective-permute-start | bytes 4718600 | tf_op jit(solution)/shard_map/ppermute | solution.py:300
  10.4 2.7 %collective-permute-done.1.refs_1_ = bf16[528,128]{1,0:T(8,128)(2,1)S(1)} collective-permute-done((bf16[528,128]{1,0:T(8,128)(2,1)S(1)}, bf16[528,128]{1,0:T(8,128)(2,1)S(1)}, u32[]{:S(2)}, u32[]{:S(2)}) %collective-permute-start.1) | collective-permute-done | bytes 135200 | tf_op jit(solution)/shard_map/ppermute | solution.py:300
  13.1 0.1 shard_map.67
  13.2 2.9 %collective-permute-start.2 = (bf16[512,128]{1,0:T(8,128)(2,1)S(1)}, bf16[512,128]{1,0:T(8,128)(2,1)S(1)}, u32[]{:S(2)}, u32[]{:S(2)}) collective-permute-start(bf16[512,128]{1,0:T(8,128)(2,1)S(1)} %get-tuple-element.29), channel_id=1, source_target_pairs={{0,16},{4,20},{8,24},{12,28},{16,0},{20,4},{24,8},{28,12},{1,17},{... | collective-permute-start | bytes 393224 | tf_op jit(solution)/shard_map/ppermute | solution.py:300
  16.0 0.0 copy-start
  16.0 0.0 copy-start.1
  16.1 1.6 %shard_map.68 = (f32[128,512]{1,0:T(8,128)S(1)}, f32[128,512]{1,0:T(8,128)S(1)}) custom-call(bf16[128,512]{1,0:T(8,128)(2,1)} %query.1, bf16[128,512]{1,0:T(8,128)(2,1)} %keys_far.3, bf16[128,512]{1,0:T(8,128)(2,1)} %values_far.3, f32[4,128]{1,0:T(4,128)} %bitcast.4, f32[512,128]{1,0:T(8,128)S(1)} %get-tuple-element.25.before, ...), custom_call_target="tpu_custom_call" | custom-call | flops 1000000000 | bytes 1000000 | tf_op jit(solution)/shard_map/pallas_call | solution.py:21
  17.7 2.8 %collective-permute-done.2.theirs = bf16[512,128]{1,0:T(8,128)(2,1)S(1)} collective-permute-done((bf16[512,128]{1,0:T(8,128)(2,1)S(1)}, bf16[512,128]{1,0:T(8,128)(2,1)S(1)}, u32[]{:S(2)}, u32[]{:S(2)}) %collective-permute-start.2) | collective-permute-done | bytes 131104 | tf_op jit(solution)/shard_map/ppermute | solution.py:300
  20.5 0.0 copy-done
  20.5 0.0 copy-done.1
  20.5 0.2 shard_map.69.mine
  20.7 0.1 collective-permute-start.3
  20.8 0.4 %shard_map.71.partial = f32[128,1536]{1,0:T(8,128)S(1)} custom-call(bf16[128,640]{1,0:T(8,128)(2,1)S(1)} %shard_map.69.mine, bf16[512,1536]{1,0:T(8,128)(2,1)S(1)} %get-tuple-element.32.weight), custom_call_target="tpu_custom_call" | custom-call | flops 400000000 | bytes 400000 | tf_op jit(solution)/shard_map/pallas_call | solution.py:21
  21.2 1.0 %collective-permute-done.3.theirs = bf16[128,640]{1,0:T(8,128)(2,1)S(1)} collective-permute-done((bf16[128,640]{1,0:T(8,128)(2,1)S(1)}, bf16[128,640]{1,0:T(8,128)(2,1)S(1)}, u32[]{:S(2)}, u32[]{:S(2)}) %collective-permute-start.3) | collective-permute-done | bytes 163872 | tf_op jit(solution)/shard_map/ppermute | solution.py:300
  22.2 0.0 collective-permute-done.5.their_weight
  22.2 0.3 shard_map.72.sent
  22.5 1.8 %collective-permute-start.7 = (bf16[656,128]{1,0:T(8,128)(2,1)S(1)}, bf16[656,128]{1,0:T(8,128)(2,1)S(1)}, u32[]{:S(2)}, u32[]{:S(2)}) collective-permute-start(bf16[656,128]{1,0:T(8,128)(2,1)S(1)} %shard_map.72.sent), channel_id=1, source_target_pairs={{0,2},{1,3},{2,0},{3,1},{4,6},{5,7},{6,4},{7,5},{8,10},{9,11},{10,... | collective-permute-start | bytes 503816 | tf_op jit(solution)/shard_map/ppermute | solution.py:300
  24.2 0.2 shard_map.73
  24.5 0.4 %collective-permute-start.6 = (bf16[512,128]{1,0:T(8,128)(2,1)S(1)}, bf16[512,128]{1,0:T(8,128)(2,1)S(1)}, u32[]{:S(2)}, u32[]{:S(2)}) collective-permute-start(bf16[512,128]{1,0:T(8,128)(2,1)S(1)} %shard_map.73), channel_id=1, source_target_pairs={{0,2},{1,3},{2,0},{3,1},{4,6},{5,7},{6,4},{7,5},{8,10},{9,11},{10,... | collective-permute-start | bytes 393224 | tf_op jit(solution)/shard_map/ppermute | solution.py:300
  24.9 0.2 shard_map.75
  25.1 1.0 %collective-permute-start.8 = (bf16[384,128]{1,0:T(8,128)(2,1)S(1)}, bf16[384,128]{1,0:T(8,128)(2,1)S(1)}, u32[]{:S(2)}, u32[]{:S(2)}) collective-permute-start(bf16[384,128]{1,0:T(8,128)(2,1)S(1)} %shard_map.75), channel_id=1, source_target_pairs={{0,3},{1,2},{2,1},{3,0},{4,7},{5,6},{6,5},{7,4},{8,11},{9,10},{10,... | collective-permute-start | bytes 294920 | tf_op jit(solution)/shard_map/ppermute | solution.py:300
  26.1 0.0 collective-permute-done.4.their_weight
  26.1 0.6 %shard_map.70.partial = f32[128,1536]{1,0:T(8,128)S(1)} custom-call(bf16[128,640]{1,0:T(8,128)(2,1)S(1)} %shard_map.69.mine, bf16[128,640]{1,0:T(8,128)(2,1)S(1)} %collective-permute-done.3.theirs, bf16[512,1536]{1,0:T(8,128)(2,1)S(1)} %get-tuple-element.30.my_weight, bf16[512,1536]{1,0:T(8,128)(2,1)S(1)} %collective-permute-done.4.their_weight), custom_call_target="tpu_custom_call" | custom-call | flops 600000000 | bytes 600000 | tf_op jit(solution)/shard_map/pallas_call | solution.py:21
  26.7 5.8 %collective-permute-done.6.refs_0_ = bf16[512,128]{1,0:T(8,128)(2,1)S(1)} collective-permute-done((bf16[512,128]{1,0:T(8,128)(2,1)S(1)}, bf16[512,128]{1,0:T(8,128)(2,1)S(1)}, u32[]{:S(2)}, u32[]{:S(2)}) %collective-permute-start.6) | collective-permute-done | bytes 131104 | tf_op jit(solution)/shard_map/ppermute | solution.py:300
  32.5 0.0 collective-permute-done.7.refs_1_
  32.5 0.1 shard_map.74
  32.6 0.4 %collective-permute-done.8.refs_2_ = bf16[384,128]{1,0:T(8,128)(2,1)S(1)} collective-permute-done((bf16[384,128]{1,0:T(8,128)(2,1)S(1)}, bf16[384,128]{1,0:T(8,128)(2,1)S(1)}, u32[]{:S(2)}, u32[]{:S(2)}) %collective-permute-start.8) | collective-permute-done | bytes 98336 | tf_op jit(solution)/shard_map/ppermute | solution.py:300
  33.0 0.8 %shard_map.76 = bf16[128,1536]{1,0:T(8,128)(2,1)} custom-call(f32[128,1536]{1,0:T(8,128)S(1)} %shard_map.70.partial, f32[128,1]{1,0:T(8,128)S(1)} %get-tuple-element.34.scale, bf16[128,512]{1,0:T(8,128)(2,1)S(1)} %get-tuple-element.35.refs_0_, bf16[128,640]{1,0:T(8,128)(2,1)S(1)} %get-tuple-element.36.refs_1_, ...), custom_call_target="tpu_custom_call" | custom-call | flops 1000000000 | bytes 1000000 | tf_op jit(solution)/shard_map/pallas_call | solution.py:21
Async XLA Ops:
  1.3 6.6 %collective-permute-start = (bf16[528,128]{1,0:T(8,128)(2,1)S(1)}, bf16[528,128]{1,0:T(8,128)(2,1)S(1)}, u32[]{:S(2)}, u32[]{:S(2)}) collective-permute-start(bf16[528,128]{1,0:T(8,128)(2,1)S(1)} %shard_map.64._.refs_0_), channel_id=1, source_target_pairs={{0,4},{4,0},{8,12},{12,8},{16,20},{20,16},{24,28},{28,24},{1,5},{5... | collective-permute-start | bytes 405512 | tf_op jit(solution)/shard_map/ppermute | solution.py:300
  8.0 5.1 %collective-permute-start.1 = (bf16[528,128]{1,0:T(8,128)(2,1)S(1)}, bf16[528,128]{1,0:T(8,128)(2,1)S(1)}, u32[]{:S(2)}, u32[]{:S(2)}) collective-permute-start(bf16[528,128]{1,0:T(8,128)(2,1)S(1)} %get-tuple-element.22.refs_0_), channel_id=1, source_target_pairs={{0,8},{4,12},{8,0},{12,4},{16,24},{20,28},{24,16},{28,20},{1,9},{5... | collective-permute-start | bytes 405512 | tf_op jit(solution)/shard_map/ppermute | solution.py:300
  9.9 16.2 %collective-permute-start.4 = (bf16[512,1536]{1,0:T(8,128)(2,1)S(1)}, bf16[512,1536]{1,0:T(8,128)(2,1)S(1)}, u32[]{:S(2)}, u32[]{:S(2)}) collective-permute-start(bf16[512,1536]{1,0:T(8,128)(2,1)S(1)} %get-tuple-element.31), channel_id=1, source_target_pairs={{0,1},{1,0},{2,3},{3,2},{4,5},{5,4},{6,7},{7,6},{8,9},{9,8},{10,11... | collective-permute-start | bytes 4718600 | tf_op jit(solution)/shard_map/ppermute | solution.py:300
  9.9 12.3 %collective-permute-start.5 = (bf16[512,1536]{1,0:T(8,128)(2,1)S(1)}, bf16[512,1536]{1,0:T(8,128)(2,1)S(1)}, u32[]{:S(2)}, u32[]{:S(2)}) collective-permute-start(bf16[512,1536]{1,0:T(8,128)(2,1)S(1)} %get-tuple-element.33), channel_id=1, source_target_pairs={{0,1},{1,0},{2,3},{3,2},{4,5},{5,4},{6,7},{7,6},{8,9},{9,8},{10,11... | collective-permute-start | bytes 4718600 | tf_op jit(solution)/shard_map/ppermute | solution.py:300
  13.2 7.3 %collective-permute-start.2 = (bf16[512,128]{1,0:T(8,128)(2,1)S(1)}, bf16[512,128]{1,0:T(8,128)(2,1)S(1)}, u32[]{:S(2)}, u32[]{:S(2)}) collective-permute-start(bf16[512,128]{1,0:T(8,128)(2,1)S(1)} %get-tuple-element.29), channel_id=1, source_target_pairs={{0,16},{4,20},{8,24},{12,28},{16,0},{20,4},{24,8},{28,12},{1,17},{... | collective-permute-start | bytes 393224 | tf_op jit(solution)/shard_map/ppermute | solution.py:300
  16.0 4.5 %copy-start = (bf16[128,512]{1,0:T(8,128)(2,1)S(1)}, bf16[128,512]{1,0:T(8,128)(2,1)}, u32[]{:S(2)}) copy-start(bf16[128,512]{1,0:T(8,128)(2,1)} %query.1) | copy-start | bytes 393220
  16.0 4.5 %copy-start.1 = (f32[512]{0:T(512)S(1)}, f32[512]{0:T(512)}, u32[]{:S(2)}) copy-start(f32[512]{0:T(512)} %param.10) | copy-start | bytes 6148
  20.7 1.5 %collective-permute-start.3 = (bf16[128,640]{1,0:T(8,128)(2,1)S(1)}, bf16[128,640]{1,0:T(8,128)(2,1)S(1)}, u32[]{:S(2)}, u32[]{:S(2)}) collective-permute-start(bf16[128,640]{1,0:T(8,128)(2,1)S(1)} %shard_map.69.mine), channel_id=1, source_target_pairs={{0,1},{1,0},{2,3},{3,2},{4,5},{5,4},{6,7},{7,6},{8,9},{9,8},{10,11... | collective-permute-start | bytes 491528 | tf_op jit(solution)/shard_map/ppermute | solution.py:300
  22.5 10.0 %collective-permute-start.7 = (bf16[656,128]{1,0:T(8,128)(2,1)S(1)}, bf16[656,128]{1,0:T(8,128)(2,1)S(1)}, u32[]{:S(2)}, u32[]{:S(2)}) collective-permute-start(bf16[656,128]{1,0:T(8,128)(2,1)S(1)} %shard_map.72.sent), channel_id=1, source_target_pairs={{0,2},{1,3},{2,0},{3,1},{4,6},{5,7},{6,4},{7,5},{8,10},{9,11},{10,... | collective-permute-start | bytes 503816 | tf_op jit(solution)/shard_map/ppermute | solution.py:300
  24.5 8.0 %collective-permute-start.6 = (bf16[512,128]{1,0:T(8,128)(2,1)S(1)}, bf16[512,128]{1,0:T(8,128)(2,1)S(1)}, u32[]{:S(2)}, u32[]{:S(2)}) collective-permute-start(bf16[512,128]{1,0:T(8,128)(2,1)S(1)} %shard_map.73), channel_id=1, source_target_pairs={{0,2},{1,3},{2,0},{3,1},{4,6},{5,7},{6,4},{7,5},{8,10},{9,11},{10,... | collective-permute-start | bytes 393224 | tf_op jit(solution)/shard_map/ppermute | solution.py:300
  25.1 7.9 %collective-permute-start.8 = (bf16[384,128]{1,0:T(8,128)(2,1)S(1)}, bf16[384,128]{1,0:T(8,128)(2,1)S(1)}, u32[]{:S(2)}, u32[]{:S(2)}) collective-permute-start(bf16[384,128]{1,0:T(8,128)(2,1)S(1)} %shard_map.75), channel_id=1, source_target_pairs={{0,3},{1,2},{2,1},{3,0},{4,7},{5,6},{6,5},{7,4},{8,11},{9,10},{10,... | collective-permute-start | bytes 294920 | tf_op jit(solution)/shard_map/ppermute | solution.py:300

commit v8 on v6

--- a/solution.py
+++ b/solution.py
@@ -312,7 +312,7 @@
 
     far_count = groups // 2
     blocks_out = columns // LANES
-    cuts = [0, blocks_out // 3, blocks_out - blocks_out // 4, blocks_out]
+    cuts = [0, blocks_out * 5 // 12, blocks_out - blocks_out // 4, blocks_out]
     *weights, token = call(
         functools.partial(weights_kernel, far_count, cuts[-2] * LANES),
         [shape((full, columns), BF16)] * (2 * far_count) + [shape((8, LANES), F32)],

time: 34.1 us -> 34 us (level)
  no operation moved by 1% of the time
where the time goes in v8:
time: 34 us; the launch traced here: 33.8 us
  waiting for transfers between devices  13.3 us (39%)
  starting transfers between devices  11.5 us (34%)
  Pallas kernels  8.84 us (26%)
    ppermute x9, waiting for transfers between devices, swap(): return lax.ppermute(value, axis, [(i, i ^ bit) for i in range(count)])  13.3 us
    ppermute x9, starting transfers between devices, swap(): return lax.ppermute(value, axis, [(i, i ^ bit) for i in range(count)])  11.5 us
    pallas_call x13, Pallas kernels, call(): pl.pallas_call(body, out_shape=outs, in_specs=[FAR] * far + [VMEM] * (len...  8.84 us
  transfers between devices with their start and end apart: 9, of which 6 were waited for; matrix products, arithmetic and copies ran while one was open for 0% of the time, Pallas kernels for 20%

profile of v8, /device:TPU:0, one launch (start us, length us, event | category | flops | bytes accessed | tf_op | source)
XLA Modules:
  0.0 33.8 jit_solution(9474792335615448818)
XLA Ops:
  0.0 1.3 %shard_map.64._.refs_0_ = bf16[528,128]{1,0:T(8,128)(2,1)S(1)} custom-call(bf16[128,512]{1,0:T(8,128)(2,1)} %keys_far.3, bf16[128,512]{1,0:T(8,128)(2,1)} %values_far.3, f32[4,128]{1,0:T(4,128)} %bitcast.3), custom_call_target="tpu_custom_call" | custom-call | flops 1000000000 | bytes 1000000 | tf_op jit(solution)/shard_map/pallas_call | solution.py:21
  1.3 3.0 %collective-permute-start = (bf16[528,128]{1,0:T(8,128)(2,1)S(1)}, bf16[528,128]{1,0:T(8,128)(2,1)S(1)}, u32[]{:S(2)}, u32[]{:S(2)}) collective-permute-start(bf16[528,128]{1,0:T(8,128)(2,1)S(1)} %shard_map.64._.refs_0_), channel_id=1, source_target_pairs={{0,4},{4,0},{8,12},{12,8},{16,20},{20,16},{24,28},{28,24},{1,5},{5... | collective-permute-start | bytes 405512 | tf_op jit(solution)/shard_map/ppermute | solution.py:301
  4.3 2.9 %shard_map.65 = (bf16[512,1536]{1,0:T(8,128)(2,1)S(1)}, bf16[512,1536]{1,0:T(8,128)(2,1)S(1)}, bf16[512,1536]{1,0:T(8,128)(2,1)S(1)}, bf16[512,1536]{1,0:T(8,128)(2,1)S(1)}, f32[8,128]{1,0:T(8,128)S(1)}) custom-call(bf16[512,6144]{1,0:T(8,128)(2,1)} %weight_far.1, bf16[528,128]{1,0:T(8,128)(2,1)S(1)} %shard_map.64._.refs_0_), custom_call_target="tpu_custom_call" | custom-call | flops 2000000000 | bytes 2000000 | tf_op jit(solution)/shard_map/pallas_call | solution.py:21
  7.2 0.7 %collective-permute-done.refs_1_ = bf16[528,128]{1,0:T(8,128)(2,1)S(1)} collective-permute-done((bf16[528,128]{1,0:T(8,128)(2,1)S(1)}, bf16[528,128]{1,0:T(8,128)(2,1)S(1)}, u32[]{:S(2)}, u32[]{:S(2)}) %collective-permute-start) | collective-permute-done | bytes 135200 | tf_op jit(solution)/shard_map/ppermute | solution.py:301
  7.9 0.1 shard_map.66
  8.0 1.9 %collective-permute-start.1 = (bf16[528,128]{1,0:T(8,128)(2,1)S(1)}, bf16[528,128]{1,0:T(8,128)(2,1)S(1)}, u32[]{:S(2)}, u32[]{:S(2)}) collective-permute-start(bf16[528,128]{1,0:T(8,128)(2,1)S(1)} %get-tuple-element.22.refs_0_), channel_id=1, source_target_pairs={{0,8},{4,12},{8,0},{12,4},{16,24},{20,28},{24,16},{28,20},{1,9},{5... | collective-permute-start | bytes 405512 | tf_op jit(solution)/shard_map/ppermute | solution.py:301
  9.8 0.0 collective-permute-start.4
  9.8 0.5 %collective-permute-start.5 = (bf16[512,1536]{1,0:T(8,128)(2,1)S(1)}, bf16[512,1536]{1,0:T(8,128)(2,1)S(1)}, u32[]{:S(2)}, u32[]{:S(2)}) collective-permute-start(bf16[512,1536]{1,0:T(8,128)(2,1)S(1)} %get-tuple-element.33), channel_id=1, source_target_pairs={{0,1},{1,0},{2,3},{3,2},{4,5},{5,4},{6,7},{7,6},{8,9},{9,8},{10,11... | collective-permute-start | bytes 4718600 | tf_op jit(solution)/shard_map/ppermute | solution.py:301
  10.4 2.7 %collective-permute-done.1.refs_1_ = bf16[528,128]{1,0:T(8,128)(2,1)S(1)} collective-permute-done((bf16[528,128]{1,0:T(8,128)(2,1)S(1)}, bf16[528,128]{1,0:T(8,128)(2,1)S(1)}, u32[]{:S(2)}, u32[]{:S(2)}) %collective-permute-start.1) | collective-permute-done | bytes 135200 | tf_op jit(solution)/shard_map/ppermute | solution.py:301
  13.1 0.1 shard_map.67
  13.2 2.9 %collective-permute-start.2 = (bf16[512,128]{1,0:T(8,128)(2,1)S(1)}, bf16[512,128]{1,0:T(8,128)(2,1)S(1)}, u32[]{:S(2)}, u32[]{:S(2)}) collective-permute-start(bf16[512,128]{1,0:T(8,128)(2,1)S(1)} %get-tuple-element.29), channel_id=1, source_target_pairs={{0,16},{4,20},{8,24},{12,28},{16,0},{20,4},{24,8},{28,12},{1,17},{... | collective-permute-start | bytes 393224 | tf_op jit(solution)/shard_map/ppermute | solution.py:301
  16.0 0.0 copy-start
  16.0 0.0 copy-start.1
  16.0 1.6 %shard_map.68 = (f32[128,512]{1,0:T(8,128)S(1)}, f32[128,512]{1,0:T(8,128)S(1)}) custom-call(bf16[128,512]{1,0:T(8,128)(2,1)} %query.1, bf16[128,512]{1,0:T(8,128)(2,1)} %keys_far.3, bf16[128,512]{1,0:T(8,128)(2,1)} %values_far.3, f32[4,128]{1,0:T(4,128)} %bitcast.4, f32[512,128]{1,0:T(8,128)S(1)} %get-tuple-element.25.before, ...), custom_call_target="tpu_custom_call" | custom-call | flops 1000000000 | bytes 1000000 | tf_op jit(solution)/shard_map/pallas_call | solution.py:21
  17.6 2.9 %collective-permute-done.2.theirs = bf16[512,128]{1,0:T(8,128)(2,1)S(1)} collective-permute-done((bf16[512,128]{1,0:T(8,128)(2,1)S(1)}, bf16[512,128]{1,0:T(8,128)(2,1)S(1)}, u32[]{:S(2)}, u32[]{:S(2)}) %collective-permute-start.2) | collective-permute-done | bytes 131104 | tf_op jit(solution)/shard_map/ppermute | solution.py:301
  20.5 0.0 copy-done
  20.5 0.0 copy-done.1
  20.5 0.2 shard_map.69.mine
  20.7 0.1 collective-permute-start.3
  20.8 0.4 %shard_map.71.partial = f32[128,1536]{1,0:T(8,128)S(1)} custom-call(bf16[128,640]{1,0:T(8,128)(2,1)S(1)} %shard_map.69.mine, bf16[512,1536]{1,0:T(8,128)(2,1)S(1)} %get-tuple-element.32.weight), custom_call_target="tpu_custom_call" | custom-call | flops 400000000 | bytes 400000 | tf_op jit(solution)/shard_map/pallas_call | solution.py:21
  21.2 1.0 %collective-permute-done.3.theirs = bf16[128,640]{1,0:T(8,128)(2,1)S(1)} collective-permute-done((bf16[128,640]{1,0:T(8,128)(2,1)S(1)}, bf16[128,640]{1,0:T(8,128)(2,1)S(1)}, u32[]{:S(2)}, u32[]{:S(2)}) %collective-permute-start.3) | collective-permute-done | bytes 163872 | tf_op jit(solution)/shard_map/ppermute | solution.py:301
  22.2 0.0 collective-permute-done.5.their_weight
  22.2 0.3 shard_map.72
  22.4 1.8 %collective-permute-start.6 = (bf16[640,128]{1,0:T(8,128)(2,1)S(1)}, bf16[640,128]{1,0:T(8,128)(2,1)S(1)}, u32[]{:S(2)}, u32[]{:S(2)}) collective-permute-start(bf16[640,128]{1,0:T(8,128)(2,1)S(1)} %shard_map.72), channel_id=1, source_target_pairs={{0,2},{1,3},{2,0},{3,1},{4,6},{5,7},{6,4},{7,5},{8,10},{9,11},{10,... | collective-permute-start | bytes 491528 | tf_op jit(solution)/shard_map/ppermute | solution.py:301
  24.2 0.2 shard_map.73
  24.5 0.4 %collective-permute-start.7 = (bf16[528,128]{1,0:T(8,128)(2,1)S(1)}, bf16[528,128]{1,0:T(8,128)(2,1)S(1)}, u32[]{:S(2)}, u32[]{:S(2)}) collective-permute-start(bf16[528,128]{1,0:T(8,128)(2,1)S(1)} %shard_map.73), channel_id=1, source_target_pairs={{0,2},{1,3},{2,0},{3,1},{4,6},{5,7},{6,4},{7,5},{8,10},{9,11},{10,... | collective-permute-start | bytes 405512 | tf_op jit(solution)/shard_map/ppermute | solution.py:301
  24.8 0.2 shard_map.75
  25.1 1.0 %collective-permute-start.8 = (bf16[384,128]{1,0:T(8,128)(2,1)S(1)}, bf16[384,128]{1,0:T(8,128)(2,1)S(1)}, u32[]{:S(2)}, u32[]{:S(2)}) collective-permute-start(bf16[384,128]{1,0:T(8,128)(2,1)S(1)} %shard_map.75), channel_id=1, source_target_pairs={{0,3},{1,2},{2,1},{3,0},{4,7},{5,6},{6,5},{7,4},{8,11},{9,10},{10,... | collective-permute-start | bytes 294920 | tf_op jit(solution)/shard_map/ppermute | solution.py:301
  26.0 0.0 collective-permute-done.4.their_weight
  26.0 0.6 %shard_map.70.partial = f32[128,1536]{1,0:T(8,128)S(1)} custom-call(bf16[128,640]{1,0:T(8,128)(2,1)S(1)} %shard_map.69.mine, bf16[128,640]{1,0:T(8,128)(2,1)S(1)} %collective-permute-done.3.theirs, bf16[512,1536]{1,0:T(8,128)(2,1)S(1)} %get-tuple-element.30.my_weight, bf16[512,1536]{1,0:T(8,128)(2,1)S(1)} %collective-permute-done.4.their_weight), custom_call_target="tpu_custom_call" | custom-call | flops 600000000 | bytes 600000 | tf_op jit(solution)/shard_map/pallas_call | solution.py:21
  26.6 5.8 %collective-permute-done.7.refs_1_ = bf16[528,128]{1,0:T(8,128)(2,1)S(1)} collective-permute-done((bf16[528,128]{1,0:T(8,128)(2,1)S(1)}, bf16[528,128]{1,0:T(8,128)(2,1)S(1)}, u32[]{:S(2)}, u32[]{:S(2)}) %collective-permute-start.7) | collective-permute-done | bytes 135200 | tf_op jit(solution)/shard_map/ppermute | solution.py:301
  32.4 0.0 collective-permute-done.6.refs_0_
  32.5 0.2 shard_map.74
  32.7 0.3 collective-permute-done.8.refs_2_
  33.0 0.8 %shard_map.76 = bf16[128,1536]{1,0:T(8,128)(2,1)} custom-call(f32[128,1536]{1,0:T(8,128)S(1)} %shard_map.70.partial, f32[128,1]{1,0:T(8,128)S(1)} %get-tuple-element.34.scale, bf16[128,640]{1,0:T(8,128)(2,1)S(1)} %get-tuple-element.35.refs_0_, bf16[128,512]{1,0:T(8,128)(2,1)S(1)} %get-tuple-element.36.refs_1_, ...), custom_call_target="tpu_custom_call" | custom-call | flops 1000000000 | bytes 1000000 | tf_op jit(solution)/shard_map/pallas_call | solution.py:21
Async XLA Ops:
  1.3 6.6 %collective-permute-start = (bf16[528,128]{1,0:T(8,128)(2,1)S(1)}, bf16[528,128]{1,0:T(8,128)(2,1)S(1)}, u32[]{:S(2)}, u32[]{:S(2)}) collective-permute-start(bf16[528,128]{1,0:T(8,128)(2,1)S(1)} %shard_map.64._.refs_0_), channel_id=1, source_target_pairs={{0,4},{4,0},{8,12},{12,8},{16,20},{20,16},{24,28},{28,24},{1,5},{5... | collective-permute-start | bytes 405512 | tf_op jit(solution)/shard_map/ppermute | solution.py:301
  8.0 5.1 %collective-permute-start.1 = (bf16[528,128]{1,0:T(8,128)(2,1)S(1)}, bf16[528,128]{1,0:T(8,128)(2,1)S(1)}, u32[]{:S(2)}, u32[]{:S(2)}) collective-permute-start(bf16[528,128]{1,0:T(8,128)(2,1)S(1)} %get-tuple-element.22.refs_0_), channel_id=1, source_target_pairs={{0,8},{4,12},{8,0},{12,4},{16,24},{20,28},{24,16},{28,20},{1,9},{5... | collective-permute-start | bytes 405512 | tf_op jit(solution)/shard_map/ppermute | solution.py:301
  9.8 16.2 %collective-permute-start.4 = (bf16[512,1536]{1,0:T(8,128)(2,1)S(1)}, bf16[512,1536]{1,0:T(8,128)(2,1)S(1)}, u32[]{:S(2)}, u32[]{:S(2)}) collective-permute-start(bf16[512,1536]{1,0:T(8,128)(2,1)S(1)} %get-tuple-element.31), channel_id=1, source_target_pairs={{0,1},{1,0},{2,3},{3,2},{4,5},{5,4},{6,7},{7,6},{8,9},{9,8},{10,11... | collective-permute-start | bytes 4718600 | tf_op jit(solution)/shard_map/ppermute | solution.py:301
  9.8 12.3 %collective-permute-start.5 = (bf16[512,1536]{1,0:T(8,128)(2,1)S(1)}, bf16[512,1536]{1,0:T(8,128)(2,1)S(1)}, u32[]{:S(2)}, u32[]{:S(2)}) collective-permute-start(bf16[512,1536]{1,0:T(8,128)(2,1)S(1)} %get-tuple-element.33), channel_id=1, source_target_pairs={{0,1},{1,0},{2,3},{3,2},{4,5},{5,4},{6,7},{7,6},{8,9},{9,8},{10,11... | collective-permute-start | bytes 4718600 | tf_op jit(solution)/shard_map/ppermute | solution.py:301
  13.2 7.3 %collective-permute-start.2 = (bf16[512,128]{1,0:T(8,128)(2,1)S(1)}, bf16[512,128]{1,0:T(8,128)(2,1)S(1)}, u32[]{:S(2)}, u32[]{:S(2)}) collective-permute-start(bf16[512,128]{1,0:T(8,128)(2,1)S(1)} %get-tuple-element.29), channel_id=1, source_target_pairs={{0,16},{4,20},{8,24},{12,28},{16,0},{20,4},{24,8},{28,12},{1,17},{... | collective-permute-start | bytes 393224 | tf_op jit(solution)/shard_map/ppermute | solution.py:301
  16.0 4.5 %copy-start = (bf16[128,512]{1,0:T(8,128)(2,1)S(1)}, bf16[128,512]{1,0:T(8,128)(2,1)}, u32[]{:S(2)}) copy-start(bf16[128,512]{1,0:T(8,128)(2,1)} %query.1) | copy-start | bytes 393220
  16.0 4.5 %copy-start.1 = (f32[512]{0:T(512)S(1)}, f32[512]{0:T(512)}, u32[]{:S(2)}) copy-start(f32[512]{0:T(512)} %param.10) | copy-start | bytes 6148
  20.7 1.5 %collective-permute-start.3 = (bf16[128,640]{1,0:T(8,128)(2,1)S(1)}, bf16[128,640]{1,0:T(8,128)(2,1)S(1)}, u32[]{:S(2)}, u32[]{:S(2)}) collective-permute-start(bf16[128,640]{1,0:T(8,128)(2,1)S(1)} %shard_map.69.mine), channel_id=1, source_target_pairs={{0,1},{1,0},{2,3},{3,2},{4,5},{5,4},{6,7},{7,6},{8,9},{9,8},{10,11... | collective-permute-start | bytes 491528 | tf_op jit(solution)/shard_map/ppermute | solution.py:301
  22.4 10.0 %collective-permute-start.6 = (bf16[640,128]{1,0:T(8,128)(2,1)S(1)}, bf16[640,128]{1,0:T(8,128)(2,1)S(1)}, u32[]{:S(2)}, u32[]{:S(2)}) collective-permute-start(bf16[640,128]{1,0:T(8,128)(2,1)S(1)} %shard_map.72), channel_id=1, source_target_pairs={{0,2},{1,3},{2,0},{3,1},{4,6},{5,7},{6,4},{7,5},{8,10},{9,11},{10,... | collective-permute-start | bytes 491528 | tf_op jit(solution)/shard_map/ppermute | solution.py:301
  24.5 8.0 %collective-permute-start.7 = (bf16[528,128]{1,0:T(8,128)(2,1)S(1)}, bf16[528,128]{1,0:T(8,128)(2,1)S(1)}, u32[]{:S(2)}, u32[]{:S(2)}) collective-permute-start(bf16[528,128]{1,0:T(8,128)(2,1)S(1)} %shard_map.73), channel_id=1, source_target_pairs={{0,2},{1,3},{2,0},{3,1},{4,6},{5,7},{6,4},{7,5},{8,10},{9,11},{10,... | collective-permute-start | bytes 405512 | tf_op jit(solution)/shard_map/ppermute | solution.py:301
  25.1 7.9 %collective-permute-start.8 = (bf16[384,128]{1,0:T(8,128)(2,1)S(1)}, bf16[384,128]{1,0:T(8,128)(2,1)S(1)}, u32[]{:S(2)}, u32[]{:S(2)}) collective-permute-start(bf16[384,128]{1,0:T(8,128)(2,1)S(1)} %shard_map.75), channel_id=1, source_target_pairs={{0,3},{1,2},{2,1},{3,0},{4,7},{5,6},{6,5},{7,4},{8,11},{9,10},{10,... | collective-permute-start | bytes 294920 | tf_op jit(solution)/shard_map/ppermute | solution.py:301

commit v9 on v8

--- a/solution.py
+++ b/solution.py
@@ -312,7 +312,7 @@
 
     far_count = groups // 2
     blocks_out = columns // LANES
-    cuts = [0, blocks_out * 5 // 12, blocks_out - blocks_out // 4, blocks_out]
+    cuts = [0, blocks_out // 2, blocks_out - blocks_out // 4, blocks_out]
     *weights, token = call(
         functools.partial(weights_kernel, far_count, cuts[-2] * LANES),
         [shape((full, columns), BF16)] * (2 * far_count) + [shape((8, LANES), F32)],

time: 34 us -> 34.1 us (level)
  no operation moved by 1% of the time
where the time goes in v9:
time: 34.1 us; the launch traced here: 33.8 us
  waiting for transfers between devices  13.3 us (39%)
  starting transfers between devices  11.5 us (34%)
  Pallas kernels  8.84 us (26%)
    ppermute x9, waiting for transfers between devices, swap(): return lax.ppermute(value, axis, [(i, i ^ bit) for i in range(count)])  13.3 us
    ppermute x9, starting transfers between devices, swap(): return lax.ppermute(value, axis, [(i, i ^ bit) for i in range(count)])  11.5 us
    pallas_call x13, Pallas kernels, call(): pl.pallas_call(body, out_shape=outs, in_specs=[FAR] * far + [VMEM] * (len...  8.84 us
  transfers between devices with their start and end apart: 9, of which 6 were waited for; matrix products, arithmetic and copies ran while one was open for 0% of the time, Pallas kernels for 20%

profile of v9, /device:TPU:0, one launch (start us, length us, event | category | flops | bytes accessed | tf_op | source)
XLA Modules:
  0.0 33.8 jit_solution(4895436935239588485)
XLA Ops:
  0.0 1.3 %shard_map.64._.refs_0_ = bf16[528,128]{1,0:T(8,128)(2,1)S(1)} custom-call(bf16[128,512]{1,0:T(8,128)(2,1)} %keys_far.3, bf16[128,512]{1,0:T(8,128)(2,1)} %values_far.3, f32[4,128]{1,0:T(4,128)} %bitcast.3), custom_call_target="tpu_custom_call" | custom-call | flops 1000000000 | bytes 1000000 | tf_op jit(solution)/shard_map/pallas_call | solution.py:21
  1.3 3.0 %collective-permute-start = (bf16[528,128]{1,0:T(8,128)(2,1)S(1)}, bf16[528,128]{1,0:T(8,128)(2,1)S(1)}, u32[]{:S(2)}, u32[]{:S(2)}) collective-permute-start(bf16[528,128]{1,0:T(8,128)(2,1)S(1)} %shard_map.64._.refs_0_), channel_id=1, source_target_pairs={{0,4},{4,0},{8,12},{12,8},{16,20},{20,16},{24,28},{28,24},{1,5},{5... | collective-permute-start | bytes 405512 | tf_op jit(solution)/shard_map/ppermute | solution.py:301
  4.3 2.9 %shard_map.65 = (bf16[512,1536]{1,0:T(8,128)(2,1)S(1)}, bf16[512,1536]{1,0:T(8,128)(2,1)S(1)}, bf16[512,1536]{1,0:T(8,128)(2,1)S(1)}, bf16[512,1536]{1,0:T(8,128)(2,1)S(1)}, f32[8,128]{1,0:T(8,128)S(1)}) custom-call(bf16[512,6144]{1,0:T(8,128)(2,1)} %weight_far.1, bf16[528,128]{1,0:T(8,128)(2,1)S(1)} %shard_map.64._.refs_0_), custom_call_target="tpu_custom_call" | custom-call | flops 2000000000 | bytes 2000000 | tf_op jit(solution)/shard_map/pallas_call | solution.py:21
  7.2 0.7 %collective-permute-done.refs_1_ = bf16[528,128]{1,0:T(8,128)(2,1)S(1)} collective-permute-done((bf16[528,128]{1,0:T(8,128)(2,1)S(1)}, bf16[528,128]{1,0:T(8,128)(2,1)S(1)}, u32[]{:S(2)}, u32[]{:S(2)}) %collective-permute-start) | collective-permute-done | bytes 135200 | tf_op jit(solution)/shard_map/ppermute | solution.py:301
  7.9 0.1 shard_map.66
  8.0 1.9 %collective-permute-start.1 = (bf16[528,128]{1,0:T(8,128)(2,1)S(1)}, bf16[528,128]{1,0:T(8,128)(2,1)S(1)}, u32[]{:S(2)}, u32[]{:S(2)}) collective-permute-start(bf16[528,128]{1,0:T(8,128)(2,1)S(1)} %get-tuple-element.22.refs_0_), channel_id=1, source_target_pairs={{0,8},{4,12},{8,0},{12,4},{16,24},{20,28},{24,16},{28,20},{1,9},{5... | collective-permute-start | bytes 405512 | tf_op jit(solution)/shard_map/ppermute | solution.py:301
  9.8 0.0 collective-permute-start.4
  9.8 0.5 %collective-permute-start.5 = (bf16[512,1536]{1,0:T(8,128)(2,1)S(1)}, bf16[512,1536]{1,0:T(8,128)(2,1)S(1)}, u32[]{:S(2)}, u32[]{:S(2)}) collective-permute-start(bf16[512,1536]{1,0:T(8,128)(2,1)S(1)} %get-tuple-element.33), channel_id=1, source_target_pairs={{0,1},{1,0},{2,3},{3,2},{4,5},{5,4},{6,7},{7,6},{8,9},{9,8},{10,11... | collective-permute-start | bytes 4718600 | tf_op jit(solution)/shard_map/ppermute | solution.py:301
  10.4 2.7 %collective-permute-done.1.refs_1_ = bf16[528,128]{1,0:T(8,128)(2,1)S(1)} collective-permute-done((bf16[528,128]{1,0:T(8,128)(2,1)S(1)}, bf16[528,128]{1,0:T(8,128)(2,1)S(1)}, u32[]{:S(2)}, u32[]{:S(2)}) %collective-permute-start.1) | collective-permute-done | bytes 135200 | tf_op jit(solution)/shard_map/ppermute | solution.py:301
  13.1 0.1 shard_map.67
  13.2 2.9 %collective-permute-start.2 = (bf16[512,128]{1,0:T(8,128)(2,1)S(1)}, bf16[512,128]{1,0:T(8,128)(2,1)S(1)}, u32[]{:S(2)}, u32[]{:S(2)}) collective-permute-start(bf16[512,128]{1,0:T(8,128)(2,1)S(1)} %get-tuple-element.29), channel_id=1, source_target_pairs={{0,16},{4,20},{8,24},{12,28},{16,0},{20,4},{24,8},{28,12},{1,17},{... | collective-permute-start | bytes 393224 | tf_op jit(solution)/shard_map/ppermute | solution.py:301
  16.0 0.0 copy-start
  16.0 0.0 copy-start.1
  16.0 1.6 %shard_map.68 = (f32[128,512]{1,0:T(8,128)S(1)}, f32[128,512]{1,0:T(8,128)S(1)}) custom-call(bf16[128,512]{1,0:T(8,128)(2,1)} %query.1, bf16[128,512]{1,0:T(8,128)(2,1)} %keys_far.3, bf16[128,512]{1,0:T(8,128)(2,1)} %values_far.3, f32[4,128]{1,0:T(4,128)} %bitcast.4, f32[512,128]{1,0:T(8,128)S(1)} %get-tuple-element.25.before, ...), custom_call_target="tpu_custom_call" | custom-call | flops 1000000000 | bytes 1000000 | tf_op jit(solution)/shard_map/pallas_call | solution.py:21
  17.6 2.9 %collective-permute-done.2.theirs = bf16[512,128]{1,0:T(8,128)(2,1)S(1)} collective-permute-done((bf16[512,128]{1,0:T(8,128)(2,1)S(1)}, bf16[512,128]{1,0:T(8,128)(2,1)S(1)}, u32[]{:S(2)}, u32[]{:S(2)}) %collective-permute-start.2) | collective-permute-done | bytes 131104 | tf_op jit(solution)/shard_map/ppermute | solution.py:301
  20.5 0.0 copy-done
  20.5 0.0 copy-done.1
  20.5 0.2 shard_map.69.mine
  20.7 0.1 collective-permute-start.3
  20.8 0.4 %shard_map.71.partial = f32[128,1536]{1,0:T(8,128)S(1)} custom-call(bf16[128,640]{1,0:T(8,128)(2,1)S(1)} %shard_map.69.mine, bf16[512,1536]{1,0:T(8,128)(2,1)S(1)} %get-tuple-element.32.weight), custom_call_target="tpu_custom_call" | custom-call | flops 400000000 | bytes 400000 | tf_op jit(solution)/shard_map/pallas_call | solution.py:21
  21.2 1.0 %collective-permute-done.3.theirs = bf16[128,640]{1,0:T(8,128)(2,1)S(1)} collective-permute-done((bf16[128,640]{1,0:T(8,128)(2,1)S(1)}, bf16[128,640]{1,0:T(8,128)(2,1)S(1)}, u32[]{:S(2)}, u32[]{:S(2)}) %collective-permute-start.3) | collective-permute-done | bytes 163872 | tf_op jit(solution)/shard_map/ppermute | solution.py:301
  22.2 0.0 collective-permute-done.5.their_weight
  22.2 0.3 shard_map.72
  22.5 1.8 %collective-permute-start.6 = (bf16[768,128]{1,0:T(8,128)(2,1)S(1)}, bf16[768,128]{1,0:T(8,128)(2,1)S(1)}, u32[]{:S(2)}, u32[]{:S(2)}) collective-permute-start(bf16[768,128]{1,0:T(8,128)(2,1)S(1)} %shard_map.72), channel_id=1, source_target_pairs={{0,2},{1,3},{2,0},{3,1},{4,6},{5,7},{6,4},{7,5},{8,10},{9,11},{10,... | collective-permute-start | bytes 589832 | tf_op jit(solution)/shard_map/ppermute | solution.py:301
  24.2 0.2 shard_map.73
  24.5 0.4 %collective-permute-start.7 = (bf16[400,128]{1,0:T(8,128)(2,1)S(1)}, bf16[400,128]{1,0:T(8,128)(2,1)S(1)}, u32[]{:S(2)}, u32[]{:S(2)}) collective-permute-start(bf16[400,128]{1,0:T(8,128)(2,1)S(1)} %shard_map.73), channel_id=1, source_target_pairs={{0,2},{1,3},{2,0},{3,1},{4,6},{5,7},{6,4},{7,5},{8,10},{9,11},{10,... | collective-permute-start | bytes 307208 | tf_op jit(solution)/shard_map/ppermute | solution.py:301
  24.8 0.2 shard_map.75
  25.1 1.0 %collective-permute-start.8 = (bf16[384,128]{1,0:T(8,128)(2,1)S(1)}, bf16[384,128]{1,0:T(8,128)(2,1)S(1)}, u32[]{:S(2)}, u32[]{:S(2)}) collective-permute-start(bf16[384,128]{1,0:T(8,128)(2,1)S(1)} %shard_map.75), channel_id=1, source_target_pairs={{0,3},{1,2},{2,1},{3,0},{4,7},{5,6},{6,5},{7,4},{8,11},{9,10},{10,... | collective-permute-start | bytes 294920 | tf_op jit(solution)/shard_map/ppermute | solution.py:301
  26.0 0.0 collective-permute-done.4.their_weight
  26.0 0.6 %shard_map.70.partial = f32[128,1536]{1,0:T(8,128)S(1)} custom-call(bf16[128,640]{1,0:T(8,128)(2,1)S(1)} %shard_map.69.mine, bf16[128,640]{1,0:T(8,128)(2,1)S(1)} %collective-permute-done.3.theirs, bf16[512,1536]{1,0:T(8,128)(2,1)S(1)} %get-tuple-element.30.my_weight, bf16[512,1536]{1,0:T(8,128)(2,1)S(1)} %collective-permute-done.4.their_weight), custom_call_target="tpu_custom_call" | custom-call | flops 600000000 | bytes 600000 | tf_op jit(solution)/shard_map/pallas_call | solution.py:21
  26.6 5.8 %collective-permute-done.7.refs_1_ = bf16[400,128]{1,0:T(8,128)(2,1)S(1)} collective-permute-done((bf16[400,128]{1,0:T(8,128)(2,1)S(1)}, bf16[400,128]{1,0:T(8,128)(2,1)S(1)}, u32[]{:S(2)}, u32[]{:S(2)}) %collective-permute-start.7) | collective-permute-done | bytes 102432 | tf_op jit(solution)/shard_map/ppermute | solution.py:301
  32.5 0.0 collective-permute-done.6.refs_0_
  32.5 0.2 shard_map.74
  32.7 0.3 collective-permute-done.8.refs_2_
  33.0 0.8 %shard_map.76 = bf16[128,1536]{1,0:T(8,128)(2,1)} custom-call(f32[128,1536]{1,0:T(8,128)S(1)} %shard_map.70.partial, f32[128,1]{1,0:T(8,128)S(1)} %get-tuple-element.34.scale, bf16[128,768]{1,0:T(8,128)(2,1)S(1)} %get-tuple-element.35.refs_0_, bf16[128,384]{1,0:T(8,128)(2,1)S(1)} %get-tuple-element.36.refs_1_, ...), custom_call_target="tpu_custom_call" | custom-call | flops 1000000000 | bytes 1000000 | tf_op jit(solution)/shard_map/pallas_call | solution.py:21
Async XLA Ops:
  1.3 6.6 %collective-permute-start = (bf16[528,128]{1,0:T(8,128)(2,1)S(1)}, bf16[528,128]{1,0:T(8,128)(2,1)S(1)}, u32[]{:S(2)}, u32[]{:S(2)}) collective-permute-start(bf16[528,128]{1,0:T(8,128)(2,1)S(1)} %shard_map.64._.refs_0_), channel_id=1, source_target_pairs={{0,4},{4,0},{8,12},{12,8},{16,20},{20,16},{24,28},{28,24},{1,5},{5... | collective-permute-start | bytes 405512 | tf_op jit(solution)/shard_map/ppermute | solution.py:301
  8.0 5.1 %collective-permute-start.1 = (bf16[528,128]{1,0:T(8,128)(2,1)S(1)}, bf16[528,128]{1,0:T(8,128)(2,1)S(1)}, u32[]{:S(2)}, u32[]{:S(2)}) collective-permute-start(bf16[528,128]{1,0:T(8,128)(2,1)S(1)} %get-tuple-element.22.refs_0_), channel_id=1, source_target_pairs={{0,8},{4,12},{8,0},{12,4},{16,24},{20,28},{24,16},{28,20},{1,9},{5... | collective-permute-start | bytes 405512 | tf_op jit(solution)/shard_map/ppermute | solution.py:301
  9.8 16.2 %collective-permute-start.4 = (bf16[512,1536]{1,0:T(8,128)(2,1)S(1)}, bf16[512,1536]{1,0:T(8,128)(2,1)S(1)}, u32[]{:S(2)}, u32[]{:S(2)}) collective-permute-start(bf16[512,1536]{1,0:T(8,128)(2,1)S(1)} %get-tuple-element.31), channel_id=1, source_target_pairs={{0,1},{1,0},{2,3},{3,2},{4,5},{5,4},{6,7},{7,6},{8,9},{9,8},{10,11... | collective-permute-start | bytes 4718600 | tf_op jit(solution)/shard_map/ppermute | solution.py:301
  9.8 12.3 %collective-permute-start.5 = (bf16[512,1536]{1,0:T(8,128)(2,1)S(1)}, bf16[512,1536]{1,0:T(8,128)(2,1)S(1)}, u32[]{:S(2)}, u32[]{:S(2)}) collective-permute-start(bf16[512,1536]{1,0:T(8,128)(2,1)S(1)} %get-tuple-element.33), channel_id=1, source_target_pairs={{0,1},{1,0},{2,3},{3,2},{4,5},{5,4},{6,7},{7,6},{8,9},{9,8},{10,11... | collective-permute-start | bytes 4718600 | tf_op jit(solution)/shard_map/ppermute | solution.py:301
  13.2 7.3 %collective-permute-start.2 = (bf16[512,128]{1,0:T(8,128)(2,1)S(1)}, bf16[512,128]{1,0:T(8,128)(2,1)S(1)}, u32[]{:S(2)}, u32[]{:S(2)}) collective-permute-start(bf16[512,128]{1,0:T(8,128)(2,1)S(1)} %get-tuple-element.29), channel_id=1, source_target_pairs={{0,16},{4,20},{8,24},{12,28},{16,0},{20,4},{24,8},{28,12},{1,17},{... | collective-permute-start | bytes 393224 | tf_op jit(solution)/shard_map/ppermute | solution.py:301
  16.0 4.5 %copy-start = (bf16[128,512]{1,0:T(8,128)(2,1)S(1)}, bf16[128,512]{1,0:T(8,128)(2,1)}, u32[]{:S(2)}) copy-start(bf16[128,512]{1,0:T(8,128)(2,1)} %query.1) | copy-start | bytes 393220
  16.0 4.5 %copy-start.1 = (f32[512]{0:T(512)S(1)}, f32[512]{0:T(512)}, u32[]{:S(2)}) copy-start(f32[512]{0:T(512)} %param.10) | copy-start | bytes 6148
  20.7 1.5 %collective-permute-start.3 = (bf16[128,640]{1,0:T(8,128)(2,1)S(1)}, bf16[128,640]{1,0:T(8,128)(2,1)S(1)}, u32[]{:S(2)}, u32[]{:S(2)}) collective-permute-start(bf16[128,640]{1,0:T(8,128)(2,1)S(1)} %shard_map.69.mine), channel_id=1, source_target_pairs={{0,1},{1,0},{2,3},{3,2},{4,5},{5,4},{6,7},{7,6},{8,9},{9,8},{10,11... | collective-permute-start | bytes 491528 | tf_op jit(solution)/shard_map/ppermute | solution.py:301
  22.5 10.0 %collective-permute-start.6 = (bf16[768,128]{1,0:T(8,128)(2,1)S(1)}, bf16[768,128]{1,0:T(8,128)(2,1)S(1)}, u32[]{:S(2)}, u32[]{:S(2)}) collective-permute-start(bf16[768,128]{1,0:T(8,128)(2,1)S(1)} %shard_map.72), channel_id=1, source_target_pairs={{0,2},{1,3},{2,0},{3,1},{4,6},{5,7},{6,4},{7,5},{8,10},{9,11},{10,... | collective-permute-start | bytes 589832 | tf_op jit(solution)/shard_map/ppermute | solution.py:301
  24.5 8.0 %collective-permute-start.7 = (bf16[400,128]{1,0:T(8,128)(2,1)S(1)}, bf16[400,128]{1,0:T(8,128)(2,1)S(1)}, u32[]{:S(2)}, u32[]{:S(2)}) collective-permute-start(bf16[400,128]{1,0:T(8,128)(2,1)S(1)} %shard_map.73), channel_id=1, source_target_pairs={{0,2},{1,3},{2,0},{3,1},{4,6},{5,7},{6,4},{7,5},{8,10},{9,11},{10,... | collective-permute-start | bytes 307208 | tf_op jit(solution)/shard_map/ppermute | solution.py:301
  25.1 7.9 %collective-permute-start.8 = (bf16[384,128]{1,0:T(8,128)(2,1)S(1)}, bf16[384,128]{1,0:T(8,128)(2,1)S(1)}, u32[]{:S(2)}, u32[]{:S(2)}) collective-permute-start(bf16[384,128]{1,0:T(8,128)(2,1)S(1)} %shard_map.75), channel_id=1, source_target_pairs={{0,3},{1,2},{2,1},{3,0},{4,7},{5,6},{6,5},{7,4},{8,11},{9,10},{10,... | collective-permute-start | bytes 294920 | tf_op jit(solution)/shard_map/ppermute | solution.py:301

commit v10 on v7

--- a/solution.py
+++ b/solution.py
@@ -63,10 +63,10 @@
     return row, col
 
 
-def column_sums(decay, after=False):
+def column_sums(decay):
     heads, tokens = decay.shape
     row, col = triangle(tokens)
-    lower = jnp.where(row < col if after else row >= col, 1.0, 0.0).astype(BF16)
+    lower = jnp.where(row >= col, 1.0, 0.0).astype(BF16)
     sums = [
         lax.dot_general(lower, part, (((1,), (1,)), ((), ())), preferred_element_type=F32) for part in split3(decay)
     ]
@@ -98,7 +98,8 @@
     decay_copy.wait()
     heads, tokens = decay.shape
     width = keys.shape[1] // heads
-    tail = jnp.exp(column_sums(decay[...], after=True))
+    column = column_sums(decay[...])
+    tail = jnp.exp(column[tokens - 1 : tokens, :] - column)
     for head in range(heads):
         tails[:, head * width : (head + 1) * width] = jnp.broadcast_to(tail[:, head : head + 1], (tokens, width))
     total = jnp.sum(decay[...], axis=1, keepdims=True)
@@ -311,7 +312,7 @@
 
     far_count = groups // 2
     blocks_out = columns // LANES
-    cuts = [0, blocks_out // 3, blocks_out - blocks_out // 4, blocks_out]
+    cuts = [0, blocks_out * 5 // 12, blocks_out - blocks_out // 4, blocks_out]
     *weights, token = call(
         functools.partial(weights_kernel, far_count, cuts[-2] * LANES),
         [shape((full, columns), BF16)] * (2 * far_count) + [shape((8, LANES), F32)],

time: 34.1 us -> 34 us (level)
  no operation moved by 1% of the time
where the time goes in v10:
time: 34 us; the launch traced here: 33.8 us
  waiting for transfers between devices  13.4 us (39%)
  starting transfers between devices  11.5 us (34%)
  Pallas kernels  8.75 us (26%)
    ppermute x9, waiting for transfers between devices, swap(): return lax.ppermute(value, axis, [(i, i ^ bit) for i in range(count)])  13.4 us
    ppermute x9, starting transfers between devices, swap(): return lax.ppermute(value, axis, [(i, i ^ bit) for i in range(count)])  11.5 us
    pallas_call x13, Pallas kernels, call(): pl.pallas_call(body, out_shape=outs, in_specs=[FAR] * far + [VMEM] * (len...  8.75 us
  transfers between devices with their start and end apart: 9, of which 6 were waited for; matrix products, arithmetic and copies ran while one was open for 0% of the time, Pallas kernels for 20%

profile of v10, /device:TPU:0, one launch (start us, length us, event | category | flops | bytes accessed | tf_op | source)
XLA Modules:
  0.0 33.8 jit_solution(11078037287391003230)
XLA Ops:
  0.0 1.3 %shard_map.64._.refs_0_ = bf16[528,128]{1,0:T(8,128)(2,1)S(1)} custom-call(bf16[128,512]{1,0:T(8,128)(2,1)} %keys_far.3, bf16[128,512]{1,0:T(8,128)(2,1)} %values_far.3, f32[4,128]{1,0:T(4,128)} %bitcast.3), custom_call_target="tpu_custom_call" | custom-call | flops 1000000000 | bytes 1000000 | tf_op jit(solution)/shard_map/pallas_call | solution.py:21
  1.3 3.0 %collective-permute-start = (bf16[528,128]{1,0:T(8,128)(2,1)S(1)}, bf16[528,128]{1,0:T(8,128)(2,1)S(1)}, u32[]{:S(2)}, u32[]{:S(2)}) collective-permute-start(bf16[528,128]{1,0:T(8,128)(2,1)S(1)} %shard_map.64._.refs_0_), channel_id=1, source_target_pairs={{0,4},{4,0},{8,12},{12,8},{16,20},{20,16},{24,28},{28,24},{1,5},{5... | collective-permute-start | bytes 405512 | tf_op jit(solution)/shard_map/ppermute | solution.py:301
  4.3 2.9 %shard_map.65 = (bf16[512,1536]{1,0:T(8,128)(2,1)S(1)}, bf16[512,1536]{1,0:T(8,128)(2,1)S(1)}, bf16[512,1536]{1,0:T(8,128)(2,1)S(1)}, bf16[512,1536]{1,0:T(8,128)(2,1)S(1)}, f32[8,128]{1,0:T(8,128)S(1)}) custom-call(bf16[512,6144]{1,0:T(8,128)(2,1)} %weight_far.1, bf16[528,128]{1,0:T(8,128)(2,1)S(1)} %shard_map.64._.refs_0_), custom_call_target="tpu_custom_call" | custom-call | flops 2000000000 | bytes 2000000 | tf_op jit(solution)/shard_map/pallas_call | solution.py:21
  7.2 0.7 %collective-permute-done.refs_1_ = bf16[528,128]{1,0:T(8,128)(2,1)S(1)} collective-permute-done((bf16[528,128]{1,0:T(8,128)(2,1)S(1)}, bf16[528,128]{1,0:T(8,128)(2,1)S(1)}, u32[]{:S(2)}, u32[]{:S(2)}) %collective-permute-start) | collective-permute-done | bytes 135200 | tf_op jit(solution)/shard_map/ppermute | solution.py:301
  7.9 0.1 shard_map.66
  8.0 1.9 %collective-permute-start.1 = (bf16[528,128]{1,0:T(8,128)(2,1)S(1)}, bf16[528,128]{1,0:T(8,128)(2,1)S(1)}, u32[]{:S(2)}, u32[]{:S(2)}) collective-permute-start(bf16[528,128]{1,0:T(8,128)(2,1)S(1)} %get-tuple-element.22.refs_0_), channel_id=1, source_target_pairs={{0,8},{4,12},{8,0},{12,4},{16,24},{20,28},{24,16},{28,20},{1,9},{5... | collective-permute-start | bytes 405512 | tf_op jit(solution)/shard_map/ppermute | solution.py:301
  9.8 0.0 collective-permute-start.4
  9.8 0.5 %collective-permute-start.5 = (bf16[512,1536]{1,0:T(8,128)(2,1)S(1)}, bf16[512,1536]{1,0:T(8,128)(2,1)S(1)}, u32[]{:S(2)}, u32[]{:S(2)}) collective-permute-start(bf16[512,1536]{1,0:T(8,128)(2,1)S(1)} %get-tuple-element.33), channel_id=1, source_target_pairs={{0,1},{1,0},{2,3},{3,2},{4,5},{5,4},{6,7},{7,6},{8,9},{9,8},{10,11... | collective-permute-start | bytes 4718600 | tf_op jit(solution)/shard_map/ppermute | solution.py:301
  10.4 2.7 %collective-permute-done.1.refs_1_ = bf16[528,128]{1,0:T(8,128)(2,1)S(1)} collective-permute-done((bf16[528,128]{1,0:T(8,128)(2,1)S(1)}, bf16[528,128]{1,0:T(8,128)(2,1)S(1)}, u32[]{:S(2)}, u32[]{:S(2)}) %collective-permute-start.1) | collective-permute-done | bytes 135200 | tf_op jit(solution)/shard_map/ppermute | solution.py:301
  13.1 0.1 shard_map.67
  13.2 2.9 %collective-permute-start.2 = (bf16[512,128]{1,0:T(8,128)(2,1)S(1)}, bf16[512,128]{1,0:T(8,128)(2,1)S(1)}, u32[]{:S(2)}, u32[]{:S(2)}) collective-permute-start(bf16[512,128]{1,0:T(8,128)(2,1)S(1)} %get-tuple-element.29), channel_id=1, source_target_pairs={{0,16},{4,20},{8,24},{12,28},{16,0},{20,4},{24,8},{28,12},{1,17},{... | collective-permute-start | bytes 393224 | tf_op jit(solution)/shard_map/ppermute | solution.py:301
  16.0 0.0 copy-start
  16.0 0.0 copy-start.1
  16.0 1.6 %shard_map.68 = (f32[128,512]{1,0:T(8,128)S(1)}, f32[128,512]{1,0:T(8,128)S(1)}) custom-call(bf16[128,512]{1,0:T(8,128)(2,1)} %query.1, bf16[128,512]{1,0:T(8,128)(2,1)} %keys_far.3, bf16[128,512]{1,0:T(8,128)(2,1)} %values_far.3, f32[4,128]{1,0:T(4,128)} %bitcast.4, f32[512,128]{1,0:T(8,128)S(1)} %get-tuple-element.25.before, ...), custom_call_target="tpu_custom_call" | custom-call | flops 1000000000 | bytes 1000000 | tf_op jit(solution)/shard_map/pallas_call | solution.py:21
  17.6 2.9 %collective-permute-done.2.theirs = bf16[512,128]{1,0:T(8,128)(2,1)S(1)} collective-permute-done((bf16[512,128]{1,0:T(8,128)(2,1)S(1)}, bf16[512,128]{1,0:T(8,128)(2,1)S(1)}, u32[]{:S(2)}, u32[]{:S(2)}) %collective-permute-start.2) | collective-permute-done | bytes 131104 | tf_op jit(solution)/shard_map/ppermute | solution.py:301
  20.5 0.0 copy-done
  20.5 0.0 copy-done.1
  20.5 0.2 shard_map.69.mine
  20.7 0.1 collective-permute-start.3
  20.8 0.4 %shard_map.71.partial = f32[128,1536]{1,0:T(8,128)S(1)} custom-call(bf16[128,640]{1,0:T(8,128)(2,1)S(1)} %shard_map.69.mine, bf16[512,1536]{1,0:T(8,128)(2,1)S(1)} %get-tuple-element.32.weight), custom_call_target="tpu_custom_call" | custom-call | flops 400000000 | bytes 400000 | tf_op jit(solution)/shard_map/pallas_call | solution.py:21
  21.2 1.0 %collective-permute-done.3.theirs = bf16[128,640]{1,0:T(8,128)(2,1)S(1)} collective-permute-done((bf16[128,640]{1,0:T(8,128)(2,1)S(1)}, bf16[128,640]{1,0:T(8,128)(2,1)S(1)}, u32[]{:S(2)}, u32[]{:S(2)}) %collective-permute-start.3) | collective-permute-done | bytes 163872 | tf_op jit(solution)/shard_map/ppermute | solution.py:301
  22.2 0.0 collective-permute-done.5.their_weight
  22.2 0.3 shard_map.73
  22.4 1.8 %collective-permute-start.6 = (bf16[640,128]{1,0:T(8,128)(2,1)S(1)}, bf16[640,128]{1,0:T(8,128)(2,1)S(1)}, u32[]{:S(2)}, u32[]{:S(2)}) collective-permute-start(bf16[640,128]{1,0:T(8,128)(2,1)S(1)} %shard_map.73), channel_id=1, source_target_pairs={{0,2},{1,3},{2,0},{3,1},{4,6},{5,7},{6,4},{7,5},{8,10},{9,11},{10,... | collective-permute-start | bytes 491528 | tf_op jit(solution)/shard_map/ppermute | solution.py:301
  24.2 0.2 shard_map.72.sent
  24.5 0.4 %collective-permute-start.7 = (bf16[528,128]{1,0:T(8,128)(2,1)S(1)}, bf16[528,128]{1,0:T(8,128)(2,1)S(1)}, u32[]{:S(2)}, u32[]{:S(2)}) collective-permute-start(bf16[528,128]{1,0:T(8,128)(2,1)S(1)} %shard_map.72.sent), channel_id=1, source_target_pairs={{0,2},{1,3},{2,0},{3,1},{4,6},{5,7},{6,4},{7,5},{8,10},{9,11},{10,... | collective-permute-start | bytes 405512 | tf_op jit(solution)/shard_map/ppermute | solution.py:301
  24.8 0.2 shard_map.75
  25.1 1.0 %collective-permute-start.8 = (bf16[384,128]{1,0:T(8,128)(2,1)S(1)}, bf16[384,128]{1,0:T(8,128)(2,1)S(1)}, u32[]{:S(2)}, u32[]{:S(2)}) collective-permute-start(bf16[384,128]{1,0:T(8,128)(2,1)S(1)} %shard_map.75), channel_id=1, source_target_pairs={{0,3},{1,2},{2,1},{3,0},{4,7},{5,6},{6,5},{7,4},{8,11},{9,10},{10,... | collective-permute-start | bytes 294920 | tf_op jit(solution)/shard_map/ppermute | solution.py:301
  26.0 0.0 collective-permute-done.4.their_weight
  26.0 0.6 %shard_map.70.partial = f32[128,1536]{1,0:T(8,128)S(1)} custom-call(bf16[128,640]{1,0:T(8,128)(2,1)S(1)} %shard_map.69.mine, bf16[128,640]{1,0:T(8,128)(2,1)S(1)} %collective-permute-done.3.theirs, bf16[512,1536]{1,0:T(8,128)(2,1)S(1)} %get-tuple-element.30.my_weight, bf16[512,1536]{1,0:T(8,128)(2,1)S(1)} %collective-permute-done.4.their_weight), custom_call_target="tpu_custom_call" | custom-call | flops 600000000 | bytes 600000 | tf_op jit(solution)/shard_map/pallas_call | solution.py:21
  26.6 5.8 %collective-permute-done.7.refs_1_ = bf16[528,128]{1,0:T(8,128)(2,1)S(1)} collective-permute-done((bf16[528,128]{1,0:T(8,128)(2,1)S(1)}, bf16[528,128]{1,0:T(8,128)(2,1)S(1)}, u32[]{:S(2)}, u32[]{:S(2)}) %collective-permute-start.7) | collective-permute-done | bytes 135200 | tf_op jit(solution)/shard_map/ppermute | solution.py:301
  32.4 0.0 collective-permute-done.6.refs_0_
  32.5 0.1 shard_map.74
  32.6 0.4 %collective-permute-done.8.refs_2_ = bf16[384,128]{1,0:T(8,128)(2,1)S(1)} collective-permute-done((bf16[384,128]{1,0:T(8,128)(2,1)S(1)}, bf16[384,128]{1,0:T(8,128)(2,1)S(1)}, u32[]{:S(2)}, u32[]{:S(2)}) %collective-permute-start.8) | collective-permute-done | bytes 98336 | tf_op jit(solution)/shard_map/ppermute | solution.py:301
  33.0 0.8 %shard_map.76 = bf16[128,1536]{1,0:T(8,128)(2,1)} custom-call(f32[128,1536]{1,0:T(8,128)S(1)} %shard_map.70.partial, f32[128,1]{1,0:T(8,128)S(1)} %get-tuple-element.34.scale, bf16[128,640]{1,0:T(8,128)(2,1)S(1)} %get-tuple-element.35.refs_0_, bf16[128,512]{1,0:T(8,128)(2,1)S(1)} %get-tuple-element.36.refs_1_, ...), custom_call_target="tpu_custom_call" | custom-call | flops 1000000000 | bytes 1000000 | tf_op jit(solution)/shard_map/pallas_call | solution.py:21
Async XLA Ops:
  1.3 6.6 %collective-permute-start = (bf16[528,128]{1,0:T(8,128)(2,1)S(1)}, bf16[528,128]{1,0:T(8,128)(2,1)S(1)}, u32[]{:S(2)}, u32[]{:S(2)}) collective-permute-start(bf16[528,128]{1,0:T(8,128)(2,1)S(1)} %shard_map.64._.refs_0_), channel_id=1, source_target_pairs={{0,4},{4,0},{8,12},{12,8},{16,20},{20,16},{24,28},{28,24},{1,5},{5... | collective-permute-start | bytes 405512 | tf_op jit(solution)/shard_map/ppermute | solution.py:301
  8.0 5.1 %collective-permute-start.1 = (bf16[528,128]{1,0:T(8,128)(2,1)S(1)}, bf16[528,128]{1,0:T(8,128)(2,1)S(1)}, u32[]{:S(2)}, u32[]{:S(2)}) collective-permute-start(bf16[528,128]{1,0:T(8,128)(2,1)S(1)} %get-tuple-element.22.refs_0_), channel_id=1, source_target_pairs={{0,8},{4,12},{8,0},{12,4},{16,24},{20,28},{24,16},{28,20},{1,9},{5... | collective-permute-start | bytes 405512 | tf_op jit(solution)/shard_map/ppermute | solution.py:301
  9.8 16.2 %collective-permute-start.4 = (bf16[512,1536]{1,0:T(8,128)(2,1)S(1)}, bf16[512,1536]{1,0:T(8,128)(2,1)S(1)}, u32[]{:S(2)}, u32[]{:S(2)}) collective-permute-start(bf16[512,1536]{1,0:T(8,128)(2,1)S(1)} %get-tuple-element.31), channel_id=1, source_target_pairs={{0,1},{1,0},{2,3},{3,2},{4,5},{5,4},{6,7},{7,6},{8,9},{9,8},{10,11... | collective-permute-start | bytes 4718600 | tf_op jit(solution)/shard_map/ppermute | solution.py:301
  9.8 12.3 %collective-permute-start.5 = (bf16[512,1536]{1,0:T(8,128)(2,1)S(1)}, bf16[512,1536]{1,0:T(8,128)(2,1)S(1)}, u32[]{:S(2)}, u32[]{:S(2)}) collective-permute-start(bf16[512,1536]{1,0:T(8,128)(2,1)S(1)} %get-tuple-element.33), channel_id=1, source_target_pairs={{0,1},{1,0},{2,3},{3,2},{4,5},{5,4},{6,7},{7,6},{8,9},{9,8},{10,11... | collective-permute-start | bytes 4718600 | tf_op jit(solution)/shard_map/ppermute | solution.py:301
  13.2 7.3 %collective-permute-start.2 = (bf16[512,128]{1,0:T(8,128)(2,1)S(1)}, bf16[512,128]{1,0:T(8,128)(2,1)S(1)}, u32[]{:S(2)}, u32[]{:S(2)}) collective-permute-start(bf16[512,128]{1,0:T(8,128)(2,1)S(1)} %get-tuple-element.29), channel_id=1, source_target_pairs={{0,16},{4,20},{8,24},{12,28},{16,0},{20,4},{24,8},{28,12},{1,17},{... | collective-permute-start | bytes 393224 | tf_op jit(solution)/shard_map/ppermute | solution.py:301
  16.0 4.5 %copy-start = (bf16[128,512]{1,0:T(8,128)(2,1)S(1)}, bf16[128,512]{1,0:T(8,128)(2,1)}, u32[]{:S(2)}) copy-start(bf16[128,512]{1,0:T(8,128)(2,1)} %query.1) | copy-start | bytes 393220
  16.0 4.5 %copy-start.1 = (f32[512]{0:T(512)S(1)}, f32[512]{0:T(512)}, u32[]{:S(2)}) copy-start(f32[512]{0:T(512)} %param.10) | copy-start | bytes 6148
  20.7 1.5 %collective-permute-start.3 = (bf16[128,640]{1,0:T(8,128)(2,1)S(1)}, bf16[128,640]{1,0:T(8,128)(2,1)S(1)}, u32[]{:S(2)}, u32[]{:S(2)}) collective-permute-start(bf16[128,640]{1,0:T(8,128)(2,1)S(1)} %shard_map.69.mine), channel_id=1, source_target_pairs={{0,1},{1,0},{2,3},{3,2},{4,5},{5,4},{6,7},{7,6},{8,9},{9,8},{10,11... | collective-permute-start | bytes 491528 | tf_op jit(solution)/shard_map/ppermute | solution.py:301
  22.4 10.0 %collective-permute-start.6 = (bf16[640,128]{1,0:T(8,128)(2,1)S(1)}, bf16[640,128]{1,0:T(8,128)(2,1)S(1)}, u32[]{:S(2)}, u32[]{:S(2)}) collective-permute-start(bf16[640,128]{1,0:T(8,128)(2,1)S(1)} %shard_map.73), channel_id=1, source_target_pairs={{0,2},{1,3},{2,0},{3,1},{4,6},{5,7},{6,4},{7,5},{8,10},{9,11},{10,... | collective-permute-start | bytes 491528 | tf_op jit(solution)/shard_map/ppermute | solution.py:301
  24.5 8.0 %collective-permute-start.7 = (bf16[528,128]{1,0:T(8,128)(2,1)S(1)}, bf16[528,128]{1,0:T(8,128)(2,1)S(1)}, u32[]{:S(2)}, u32[]{:S(2)}) collective-permute-start(bf16[528,128]{1,0:T(8,128)(2,1)S(1)} %shard_map.72.sent), channel_id=1, source_target_pairs={{0,2},{1,3},{2,0},{3,1},{4,6},{5,7},{6,4},{7,5},{8,10},{9,11},{10,... | collective-permute-start | bytes 405512 | tf_op jit(solution)/shard_map/ppermute | solution.py:301
  25.1 7.9 %collective-permute-start.8 = (bf16[384,128]{1,0:T(8,128)(2,1)S(1)}, bf16[384,128]{1,0:T(8,128)(2,1)S(1)}, u32[]{:S(2)}, u32[]{:S(2)}) collective-permute-start(bf16[384,128]{1,0:T(8,128)(2,1)S(1)} %shard_map.75), channel_id=1, source_target_pairs={{0,3},{1,2},{2,1},{3,0},{4,7},{5,6},{6,5},{7,4},{8,11},{9,10},{10,... | collective-permute-start | bytes 294920 | tf_op jit(solution)/shard_map/ppermute | solution.py:301
